TPU v7x, 1024 devices: a whole 8x8x8 slice. The times are simulated.
1024 devices in a mesh: phase: 4 (over x_lo), dp: 16 (over x_hi, z), expert: 16 (over y, core).
Axes of the slice: x: 8 (x_hi: 2, x_lo: 4; x = x_hi * 4 + x_lo), y: 8, z: 8, core: 2. Of those that a mesh axis runs over, the one named last changes fastest.
Arguments:
- grad_out: bfloat16 [4, 32768, 5120], P('phase', ('dp', 'expert')), may hold values from -6 to 6
- routes: int32 [4, 32768, 2], P('phase', ('dp', 'expert')), may hold values from 0 to 63, as said below
- gates: float32 [4, 32768, 2], P('phase', ('dp', 'expert')), may hold values from 0.2 to 1
- saved_in: bfloat16 [4, 16, 256, 10240], P('phase', 'dp', None, 'expert'), may hold values from -6 to 6
- saved_pre: bfloat16 [4, 16, 16, 256, 768], P('phase', 'dp', 'expert'), may hold values from -4 to 4, as said below
- w_up: bfloat16 [4, 10240, 768], P('phase', 'expert'), may hold values from -0.078125 to 0.078125
- w_down: bfloat16 [4, 768, 10240], P('phase', None, 'expert'), may hold values from -0.21875 to 0.21875
Outputs:
- grad_in: bfloat16 [4, 32768, 5120], P('phase', ('dp', 'expert'))
- grad_up: bfloat16 [4, 768, 10240], P('phase', 'dp', 'expert')
- grad_down: bfloat16 [4, 768, 10240], P('phase', 'dp', 'expert')
Inputs may be any that keep to these rules, and one draw needn't show every extreme that they name: `routes`: the two experts of a token differ. In each aligned block of 128 rows (the tokens of one device) every expert below 2 is named by at least one row and at most 16 rows; within each token group (2048 rows) one expert below 2 is named by exactly 16 rows of every block, and the other experts below 2 by at most one eighth of 16 rows (at least one) of each block. saved_pre[s, g, j] is the same for all j with the same j // 8.
All inputs are finite; a program needn't handle non-finite values.
Results may differ from a plain program's by a relative error of at most 0.024.
Values may be sent and summed in bfloat16 or wider, within the bound.
No kernel may reach another device: no remote copies, remote signals or barrier semaphores. Data moves between devices by JAX's collectives and lax.ppermute only.
A program may use at most 32 MiB of HBM per device.

v0:
```python
import jax
import jax.numpy as jnp
from jax import lax
from jax.sharding import PartitionSpec as P


def partner(block, axis, bit):
    count = lax.axis_size(axis)
    route = []
    for low in range(count):
        high = low | 1 << bit
        if high != low and high < count:
            route += [(low, high), (high, low)]
    return lax.ppermute(block, axis, route)


def from_behind(x, axis, by):
    peers = lax.axis_size(axis)
    pairs = [(i, i + by) for i in range(peers) if 0 <= i + by < peers]
    return lax.ppermute(x, axis, pairs)


def gelu_parts(pre):
    value = pre.astype(jnp.float32)
    cdf = 0.5 * (1.0 + lax.erf(value * 0.7071067811865476))
    dens = jnp.exp(-0.5 * value * value) * 0.3989422804014327
    return (value * cdf, cdf + value * dens)


def route(buffer):
    count = lax.axis_size("expert")
    position = lax.axis_index("expert")
    slots_per = buffer.shape[1]
    columns = buffer.shape[2]
    for level in range(count.bit_length() - 1):
        mine = position >> level & 1
        shaped = buffer.reshape(count >> level + 1, 2, 1 << level, slots_per, columns)
        lower_half = shaped[:, 0]
        upper_half = shaped[:, 1]
        keep = jnp.where(mine == 1, upper_half, lower_half)
        away = jnp.where(mine == 1, lower_half, upper_half)
        got = partner(away, "expert", level)
        first = jnp.where(mine == 1, got, keep)
        second = jnp.where(mine == 1, keep, got)
        buffer = jnp.stack([first, second], axis=1).reshape(count, slots_per, columns)
    return buffer


def body(grad_out, routes, gates, saved_in, saved_pre, w_up, w_down):
    count = lax.axis_size("expert")
    width = grad_out.shape[2]
    quarter = w_up.shape[1]
    split = width // quarter
    experts = count // split
    slots_per = saved_in.shape[2] // count
    levels = split.bit_length() - 1
    grads = grad_out[0]
    tokens = grads.shape[0]
    chosen = routes[0]
    weights = gates[0]
    flat = chosen.reshape(-1)
    onehot = (flat[:, None] == jnp.arange(experts, dtype=jnp.int32)[None, :]).astype(jnp.int32)
    before = jnp.cumsum(onehot, axis=0) - onehot
    slot = jnp.sum(before * onehot, axis=1)
    target = (flat * slots_per + slot).reshape(tokens, 2)
    slot_ids = jnp.arange(experts * slots_per, dtype=jnp.int32)
    place_first = (target[:, 0][None, :] == slot_ids[:, None]).astype(jnp.bfloat16)
    place_second = (target[:, 1][None, :] == slot_ids[:, None]).astype(jnp.bfloat16)
    scaled_first = (weights[:, 0:1] * grads.astype(jnp.float32)).astype(jnp.bfloat16)
    scaled_second = (weights[:, 1:2] * grads.astype(jnp.float32)).astype(jnp.bfloat16)
    packed = (
        jnp.dot(place_first, scaled_first, preferred_element_type=jnp.float32)
        + jnp.dot(place_second, scaled_second, preferred_element_type=jnp.float32)
    ).astype(jnp.bfloat16)
    outgoing = (
        packed.reshape(experts, slots_per, split, quarter)
        .transpose(0, 2, 1, 3)
        .reshape(count, slots_per, quarter)
    )
    incoming = route(outgoing)
    rows = incoming.reshape(count * slots_per, quarter)
    act, slope = gelu_parts(saved_pre[0, 0, 0])
    act = act.astype(jnp.bfloat16)
    term_down = lax.dot_general(
        act, rows, (((0,), (0,)), ((), ())), preferred_element_type=jnp.float32
    )
    partial_value = lax.dot_general(
        rows, w_down[0], (((1,), (1,)), ((), ())), preferred_element_type=jnp.float32
    )
    for level in range(levels):
        partial_value = partial_value + partner(
            partial_value.astype(jnp.bfloat16), "expert", level
        ).astype(partial_value.dtype)
    hidden_grad = (partial_value * slope).astype(jnp.bfloat16)
    term_up = lax.dot_general(
        hidden_grad, saved_in[0, 0], (((0,), (0,)), ((), ())), preferred_element_type=jnp.float32
    )
    back = lax.dot_general(
        hidden_grad, w_up[0], (((1,), (1,)), ((), ())), preferred_element_type=jnp.float32
    ).astype(jnp.bfloat16)
    returned = route(back.reshape(count, slots_per, quarter))
    unpacked = (
        returned.reshape(experts, split, slots_per, quarter)
        .transpose(0, 2, 1, 3)
        .reshape(experts * slots_per, width)
    )
    picked_first = lax.dot_general(
        place_first, unpacked, (((0,), (0,)), ((), ())), preferred_element_type=jnp.float32
    )
    picked_second = lax.dot_general(
        place_second, unpacked, (((0,), (0,)), ((), ())), preferred_element_type=jnp.float32
    )
    total = (grads.astype(jnp.float32) + picked_first + picked_second).astype(jnp.bfloat16)
    down_sum, up_sum = (
        lax.psum_scatter(
            term_down.astype(jnp.bfloat16), "dp", scatter_dimension=0, tiled=True
        ).astype(jnp.float32),
        lax.psum_scatter(
            term_up.astype(jnp.bfloat16), "dp", scatter_dimension=0, tiled=True
        ).astype(jnp.float32),
    )
    passed = from_behind(total, "phase", -1)
    return (passed[None], up_sum.astype(jnp.bfloat16)[None], down_sum.astype(jnp.bfloat16)[None])


def solution(mesh):
    in_specs = (
        P("phase", ("dp", "expert"), None),
        P("phase", ("dp", "expert"), None),
        P("phase", ("dp", "expert"), None),
        P("phase", "dp", None, "expert"),
        P("phase", "dp", "expert", None, None),
        P("phase", "expert", None),
        P("phase", None, "expert"),
    )
    out_specs = (
        P("phase", ("dp", "expert"), None),
        P("phase", "dp", "expert"),
        P("phase", "dp", "expert"),
    )
    return jax.shard_map(body, mesh=mesh, in_specs=in_specs, out_specs=out_specs, check_vma=False)
```

profile of v0, /device:TPU:1, one launch (start us, length us, event | category | flops | bytes accessed | tf_op | source)
XLA Modules:
  0.0 529.7 jit_solution(14177907879940060172)
XLA Ops:
  7.2 0.9 copy.54
  8.2 0.1 eq.46
  8.3 0.1 eq.42
  8.5 0.8 slice_bitcast_fusion.2
  9.2 0.6 reduce-window.6
  9.8 0.2 slice_reduce_fusion.2
  10.0 0.2 reduce-window.9
  10.2 0.1 add_bitcast_fusion
  10.3 0.1 reduce_sum.12
  10.5 0.2 slice_reduce_fusion
  10.7 1.7 fusion.5
  12.4 0.4 fusion.1
  13.0 16.1 %collective-permute-start = (bf16[8,1,16,640]{3,2,0,1:T(8,128)(2,1)S(1)}, bf16[8,1,16,640]{3,2,0,1:T(8,128)(2,1)S(1)}, u32[]{:S(2)}, u32[]{:S(2)}) collective-permute-start(bf16[8,1,16,640]{3,2,0,1:T(8,128)(2,1)S(1)} %fusion.45), channel_id=1, source_target_pairs={{0,1},{1,0},{2,3},{3,2},{4,5},{5,4},{6,7},{7,6},{8,9},{9,8},{10,11... | collective-permute-start | bytes 491528 | tf_op jit(solution)/shard_map/ppermute | solution.py:14
  29.1 1.0 collective-permute-done
  30.1 1.9 collective-permute-start.1
  32.1 5.4 %collective-permute-done.1 = bf16[4,2,16,640]{3,2,0,1:T(8,128)(2,1)S(1)} collective-permute-done((bf16[4,2,16,640]{3,2,0,1:T(8,128)(2,1)S(1)}, bf16[4,2,16,640]{3,2,0,1:T(8,128)(2,1)S(1)}, u32[]{:S(2)}, u32[]{:S(2)}) %collective-permute-start.1) | collective-permute-done | bytes 163872 | tf_op jit(solution)/shard_map/ppermute | solution.py:14
  37.6 1.9 collective-permute-start.2
  39.6 10.4 %collective-permute-done.2 = bf16[2,4,16,640]{3,2,1,0:T(8,128)(2,1)S(1)} collective-permute-done((bf16[2,4,16,640]{3,2,1,0:T(8,128)(2,1)S(1)}, bf16[2,4,16,640]{3,2,1,0:T(8,128)(2,1)S(1)}, u32[]{:S(2)}, u32[]{:S(2)}) %collective-permute-start.2) | collective-permute-done | bytes 163872 | tf_op jit(solution)/shard_map/ppermute | solution.py:14
  50.1 1.9 collective-permute-start.3
  52.1 9.6 %collective-permute-done.3 = bf16[1,8,16,640]{3,2,1,0:T(8,128)(2,1)S(1)} collective-permute-done((bf16[1,8,16,640]{3,2,1,0:T(8,128)(2,1)S(1)}, bf16[1,8,16,640]{3,2,1,0:T(8,128)(2,1)S(1)}, u32[]{:S(2)}, u32[]{:S(2)}) %collective-permute-start.3) | collective-permute-done | bytes 163872 | tf_op jit(solution)/shard_map/ppermute | solution.py:14
  61.8 0.5 fusion.68
  62.3 3.6 collective-permute-start.4
  66.0 1.3 collective-permute-done.4
  67.3 0.1 fusion.30
  67.4 2.1 collective-permute-start.5
  69.4 10.3 %collective-permute-done.5 = bf16[256,768]{1,0:T(8,128)(2,1)S(1)} collective-permute-done((bf16[256,768]{1,0:T(8,128)(2,1)S(1)}, bf16[256,768]{1,0:T(8,128)(2,1)S(1)}, u32[]{:S(2)}, u32[]{:S(2)}) %collective-permute-start.5) | collective-permute-done | bytes 393248 | tf_op jit(solution)/shard_map/ppermute | solution.py:14
  79.7 0.1 fusion.37
  79.9 2.8 collective-permute-start.6
  82.7 19.4 %collective-permute-done.6 = bf16[256,768]{1,0:T(8,128)(2,1)S(1)} collective-permute-done((bf16[256,768]{1,0:T(8,128)(2,1)S(1)}, bf16[256,768]{1,0:T(8,128)(2,1)S(1)}, u32[]{:S(2)}, u32[]{:S(2)}) %collective-permute-start.6) | collective-permute-done | bytes 393248 | tf_op jit(solution)/shard_map/ppermute | solution.py:14
  102.1 0.5 fusion.29
  102.6 0.5 convolution_convert_fusion.2
  103.1 2.5 collective-permute-start.7
  105.6 1.0 collective-permute-done.7
  106.7 1.9 collective-permute-start.8
  108.6 1.5 convolution_convert_fusion
  110.2 3.8 collective-permute-done.8
  114.2 2.1 collective-permute-start.9
  116.3 10.4 %collective-permute-done.9 = bf16[2,4,16,640]{3,2,1,0:T(8,128)(2,1)S(1)} collective-permute-done((bf16[2,4,16,640]{3,2,1,0:T(8,128)(2,1)S(1)}, bf16[2,4,16,640]{3,2,1,0:T(8,128)(2,1)S(1)}, u32[]{:S(2)}, u32[]{:S(2)}) %collective-permute-start.9) | collective-permute-done | bytes 163872 | tf_op jit(solution)/shard_map/ppermute | solution.py:14
  126.8 4.1 collective-permute-start.10
  131.0 1.5 convolution_convert_fusion.1
  132.5 8.9 %collective-permute-done.10 = bf16[1,8,16,640]{3,2,1,0:T(8,128)(2,1)S(1)} collective-permute-done((bf16[1,8,16,640]{3,2,1,0:T(8,128)(2,1)S(1)}, bf16[1,8,16,640]{3,2,1,0:T(8,128)(2,1)S(1)}, u32[]{:S(2)}, u32[]{:S(2)}) %collective-permute-start.10) | collective-permute-done | bytes 163872 | tf_op jit(solution)/shard_map/ppermute | solution.py:14
  141.6 0.6 convolution_add_fusion.1
  142.2 0.6 fusion
  142.7 1.3 collective-permute-start.11
  144.0 32.3 %collective-permute-done.11 = bf16[128,5120]{1,0:T(8,128)(2,1)S(1)} collective-permute-done((bf16[128,5120]{1,0:T(8,128)(2,1)S(1)}, bf16[128,5120]{1,0:T(8,128)(2,1)S(1)}, u32[]{:S(2)}, u32[]{:S(2)}) %collective-permute-start.11) | collective-permute-done | bytes 1310752 | tf_op jit(solution)/shard_map/ppermute | solution.py:20
  176.4 136.2 %reduce-scatter.5.cloned.1.call-done = bf16[48,640]{1,0:T(8,128)(2,1)} async-done(((bf16[768,640]{1,0:T(8,128)(2,1)}), bf16[48,640]{1,0:T(8,128)(2,1)}) %reduce-scatter.5.cloned.1.call-update) | async-done | bytes 61456 | tf_op jit(solution)/shard_map/reduce_scatter | solution.py:115
  312.6 209.3 %reduce-scatter.3.cloned.1.call-done = bf16[48,640]{1,0:T(8,128)(2,1)} async-done(((bf16[768,640]{1,0:T(8,128)(2,1)}), bf16[48,640]{1,0:T(8,128)(2,1)}) %reduce-scatter.3.cloned.1.call-update) | async-done | bytes 61456 | tf_op jit(solution)/shard_map/reduce_scatter | solution.py:118
  521.8 1.1 copy.117
  (46 shorter events, 1.3 us)
Async XLA Ops:
  7.2 54.6 %copy-start = (bf16[1,768,640]{2,1,0:T(8,128)(2,1)S(1)}, bf16[1,768,640]{2,1,0:T(8,128)(2,1)}, u32[]{:S(2)}) copy-start(bf16[1,768,640]{2,1,0:T(8,128)(2,1)} %param.13) | copy-start | bytes 2949124
  7.2 5.2 copy-start.1
  7.2 305.4 %reduce-scatter.5.cloned.1.call-start = ((), (), s32[]{:S(2)}) async-start(), calls=%async_computation.3 | async-start | bytes 1044480 | tf_op jit(solution)/shard_map/reduce_scatter | solution.py:115
  13.0 17.1 %collective-permute-start = (bf16[8,1,16,640]{3,2,0,1:T(8,128)(2,1)S(1)}, bf16[8,1,16,640]{3,2,0,1:T(8,128)(2,1)S(1)}, u32[]{:S(2)}, u32[]{:S(2)}) collective-permute-start(bf16[8,1,16,640]{3,2,0,1:T(8,128)(2,1)S(1)} %fusion.45), channel_id=1, source_target_pairs={{0,1},{1,0},{2,3},{3,2},{4,5},{5,4},{6,7},{7,6},{8,9},{9,8},{10,11... | collective-permute-start | bytes 491528 | tf_op jit(solution)/shard_map/ppermute | solution.py:14
  30.1 7.3 %collective-permute-start.1 = (bf16[4,2,16,640]{3,2,0,1:T(8,128)(2,1)S(1)}, bf16[4,2,16,640]{3,2,0,1:T(8,128)(2,1)S(1)}, u32[]{:S(2)}, u32[]{:S(2)}) collective-permute-start(bf16[4,2,16,640]{3,2,0,1:T(8,128)(2,1)S(1)} %fusion.44), channel_id=1, source_target_pairs={{0,2},{2,0},{1,3},{3,1},{4,6},{6,4},{5,7},{7,5},{8,10},{10,8},{9,1... | collective-permute-start | bytes 491528 | tf_op jit(solution)/shard_map/ppermute | solution.py:14
  37.6 12.4 %collective-permute-start.2 = (bf16[2,4,16,640]{3,2,1,0:T(8,128)(2,1)S(1)}, bf16[2,4,16,640]{3,2,1,0:T(8,128)(2,1)S(1)}, u32[]{:S(2)}, u32[]{:S(2)}) collective-permute-start(bf16[2,4,16,640]{3,2,1,0:T(8,128)(2,1)S(1)} %select_bitcast_fusion.5), channel_id=1, source_target_pairs={{0,4},{4,0},{1,5},{5,1},{2,6},{6,2},{3,7},{7,3},{8,12},{12,8},{9,1... | collective-permute-start | bytes 491528 | tf_op jit(solution)/shard_map/ppermute | solution.py:14
  50.1 11.6 %collective-permute-start.3 = (bf16[1,8,16,640]{3,2,1,0:T(8,128)(2,1)S(1)}, bf16[1,8,16,640]{3,2,1,0:T(8,128)(2,1)S(1)}, u32[]{:S(2)}, u32[]{:S(2)}) collective-permute-start(bf16[1,8,16,640]{3,2,1,0:T(8,128)(2,1)S(1)} %select_bitcast_fusion.4), channel_id=1, source_target_pairs={{0,8},{8,0},{1,9},{9,1},{2,10},{10,2},{3,11},{11,3},{4,12},{12,4},... | collective-permute-start | bytes 491528 | tf_op jit(solution)/shard_map/ppermute | solution.py:14
  62.3 39.8 %copy-start.3 = (bf16[1,1,1,256,768]{4,3,2,1,0:T(8,128)(2,1)S(1)}, bf16[1,1,1,256,768]{4,3,2,1,0:T(8,128)(2,1)}, u32[]{:S(2)}) copy-start(bf16[1,1,1,256,768]{4,3,2,1,0:T(8,128)(2,1)} %param.11) | copy-start | bytes 1179652
  62.3 5.0 collective-permute-start.4
  67.4 35.2 %copy-start.2 = (bf16[1,640,768]{2,1,0:T(8,128)(2,1)S(1)}, bf16[1,640,768]{2,1,0:T(8,128)(2,1)}, u32[]{:S(2)}) copy-start(bf16[1,640,768]{2,1,0:T(8,128)(2,1)} %param.12) | copy-start | bytes 2949124
  67.4 12.4 %collective-permute-start.5 = (bf16[256,768]{1,0:T(8,128)(2,1)S(1)}, bf16[256,768]{1,0:T(8,128)(2,1)S(1)}, u32[]{:S(2)}, u32[]{:S(2)}) collective-permute-start(bf16[256,768]{1,0:T(8,128)(2,1)S(1)} %fusion.30), channel_id=1, source_target_pairs={{0,2},{2,0},{1,3},{3,1},{4,6},{6,4},{5,7},{7,5},{8,10},{10,8},{9,1... | collective-permute-start | bytes 1179656 | tf_op jit(solution)/shard_map/ppermute | solution.py:14
  79.9 22.2 %collective-permute-start.6 = (bf16[256,768]{1,0:T(8,128)(2,1)S(1)}, bf16[256,768]{1,0:T(8,128)(2,1)S(1)}, u32[]{:S(2)}, u32[]{:S(2)}) collective-permute-start(bf16[256,768]{1,0:T(8,128)(2,1)S(1)} %fusion.37), channel_id=1, source_target_pairs={{0,4},{4,0},{1,5},{5,1},{2,6},{6,2},{3,7},{7,3},{8,12},{12,8},{9,1... | collective-permute-start | bytes 1179656 | tf_op jit(solution)/shard_map/ppermute | solution.py:14
  103.1 3.5 collective-permute-start.7
  106.7 7.3 %collective-permute-start.8 = (bf16[4,2,16,640]{3,2,0,1:T(8,128)(2,1)S(1)}, bf16[4,2,16,640]{3,2,0,1:T(8,128)(2,1)S(1)}, u32[]{:S(2)}, u32[]{:S(2)}) collective-permute-start(bf16[4,2,16,640]{3,2,0,1:T(8,128)(2,1)S(1)} %select_bitcast_fusion.2), channel_id=1, source_target_pairs={{0,2},{2,0},{1,3},{3,1},{4,6},{6,4},{5,7},{7,5},{8,10},{10,8},{9,1... | collective-permute-start | bytes 491528 | tf_op jit(solution)/shard_map/ppermute | solution.py:14
  110.2 411.7 %reduce-scatter.3.cloned.1.call-start = ((), (), s32[]{:S(2)}) async-start(), calls=%async_computation.2 | async-start | bytes 1044480 | tf_op jit(solution)/shard_map/reduce_scatter | solution.py:118
  114.1 16.9 %copy-start.4 = (bf16[1,1,256,640]{3,2,1,0:T(8,128)(2,1)S(1)}, bf16[1,1,256,640]{3,2,1,0:T(8,128)(2,1)}, u32[]{:S(2)}) copy-start(bf16[1,1,256,640]{3,2,1,0:T(8,128)(2,1)} %param.10) | copy-start | bytes 983044
  114.2 12.5 %collective-permute-start.9 = (bf16[2,4,16,640]{3,2,1,0:T(8,128)(2,1)S(1)}, bf16[2,4,16,640]{3,2,1,0:T(8,128)(2,1)S(1)}, u32[]{:S(2)}, u32[]{:S(2)}) collective-permute-start(bf16[2,4,16,640]{3,2,1,0:T(8,128)(2,1)S(1)} %select_bitcast_fusion.1), channel_id=1, source_target_pairs={{0,4},{4,0},{1,5},{5,1},{2,6},{6,2},{3,7},{7,3},{8,12},{12,8},{9,1... | collective-permute-start | bytes 491528 | tf_op jit(solution)/shard_map/ppermute | solution.py:14
  126.8 14.6 %collective-permute-start.10 = (bf16[1,8,16,640]{3,2,1,0:T(8,128)(2,1)S(1)}, bf16[1,8,16,640]{3,2,1,0:T(8,128)(2,1)S(1)}, u32[]{:S(2)}, u32[]{:S(2)}) collective-permute-start(bf16[1,8,16,640]{3,2,1,0:T(8,128)(2,1)S(1)} %select_bitcast_fusion), channel_id=1, source_target_pairs={{0,8},{8,0},{1,9},{9,1},{2,10},{10,2},{3,11},{11,3},{4,12},{12,4},... | collective-permute-start | bytes 491528 | tf_op jit(solution)/shard_map/ppermute | solution.py:14
  142.7 33.6 %collective-permute-start.11 = (bf16[128,5120]{1,0:T(8,128)(2,1)S(1)}, bf16[128,5120]{1,0:T(8,128)(2,1)S(1)}, u32[]{:S(2)}, u32[]{:S(2)}) collective-permute-start(bf16[128,5120]{1,0:T(8,128)(2,1)S(1)} %fusion), channel_id=1, source_target_pairs={{256,0},{512,256},{768,512},{257,1},{513,257},{769,513},{258,2},{5... | collective-permute-start | bytes 3932168 | tf_op jit(solution)/shard_map/ppermute | solution.py:20
Sparse Core Ops, SparseCore 0:
  110.3 202.2 reduce-scatter.4
  318.7 203.0 reduce-scatter.2
where the time goes:
time: 535 us; the launch traced here: 530 us
  waiting for transfers between devices  459 us (86%)
  starting transfers between devices  42.3 us (8%)
  between operations  14.5 us (3%)
  matrix products  7.26 us (1%)
    reduce_scatter x1, waiting for transfers between devices, body(): lax.psum_scatter(term_up.astype(jnp.bfloat16), 'dp', scatter_dimension=0,...  209 us
    reduce_scatter x1, waiting for transfers between devices, body(): lax.psum_scatter(term_down.astype(jnp.bfloat16), 'dp', scatter_dimension=...  136 us
    ppermute x11, waiting for transfers between devices, partner(): return lax.ppermute(block, axis, route)  81.6 us
    ppermute x11, starting transfers between devices, partner(): return lax.ppermute(block, axis, route)  40.9 us
    ppermute x1, waiting for transfers between devices, from_behind(): return lax.ppermute(x, axis, pairs)  32.3 us
  transfers between devices with their start and end apart: 14, of which 14 were waited for; matrix products, arithmetic and copies ran while one was open for 1% of the time, Pallas kernels for 0%

commit v1 on v0

v1 whole, which is shorter than its diff:
```python
import jax
import jax.numpy as jnp
from jax import lax
from jax.sharding import PartitionSpec as P


def gelu_parts(pre):
    value = pre.astype(jnp.float32)
    cdf = 0.5 * (1.0 + lax.erf(value * 0.7071067811865476))
    dens = jnp.exp(-0.5 * value * value) * 0.3989422804014327
    return (value * cdf, cdf + value * dens)


def exchange(x, axis, groups=None):
    return lax.all_to_all(x, axis, 0, 0, tiled=True, axis_index_groups=groups)


def to_previous(x):
    peers = lax.axis_size("phase")
    return lax.ppermute(x, "phase", [(i, i - 1) for i in range(1, peers)])


def slot_targets(chosen, experts, slots_per):
    tokens = chosen.shape[0]
    flat = chosen.reshape(-1)
    onehot = (flat[:, None] == jnp.arange(experts, dtype=jnp.int32)[None, :]).astype(jnp.int32)
    before = jnp.cumsum(onehot, axis=0) - onehot
    slot = jnp.sum(before * onehot, axis=1)
    return (flat * slots_per + slot).reshape(tokens, 2)


def sum_over_groups(term):
    count = lax.axis_size("dp")
    hid, quarter = term.shape
    pieces = exchange(term, "dp").reshape(count, hid // count, quarter)
    return jnp.sum(pieces.astype(jnp.float32), axis=0).astype(jnp.bfloat16)


def body(grad_out, routes, gates, saved_in, saved_pre, w_up, w_down):
    count = lax.axis_size("expert")
    grads = grad_out[0]
    chosen = routes[0]
    weights = gates[0]
    tokens, width = grads.shape
    quarter = w_up.shape[1]
    split = width // quarter
    experts = count // split
    slots_per = saved_in.shape[2] // count
    all_slots = experts * slots_per
    members = [[e * split + q for q in range(split)] for e in range(experts)]
    share = count * slots_per // split

    grads_after = to_previous(grads)
    chosen_after = to_previous(chosen)

    target = slot_targets(chosen, experts, slots_per)
    slot_ids = jnp.arange(all_slots, dtype=jnp.int32)
    hit = [(target[:, k][None, :] == slot_ids[:, None]) for k in range(2)]
    place = (hit[0] | hit[1]).astype(jnp.bfloat16)
    gate = jnp.sum(
        jnp.where(hit[0], weights[:, 0][None, :], 0.0)
        + jnp.where(hit[1], weights[:, 1][None, :], 0.0),
        axis=1,
        keepdims=True,
    )
    picked = jnp.dot(place, grads, preferred_element_type=jnp.float32)
    packed = (gate * picked).astype(jnp.bfloat16)
    outgoing = (
        packed.reshape(experts, slots_per, split, quarter)
        .transpose(0, 2, 1, 3)
        .reshape(count * slots_per, quarter)
    )
    rows = exchange(outgoing, "expert")

    partial_value = lax.dot_general(
        rows, w_down[0], (((1,), (1,)), ((), ())), preferred_element_type=jnp.float32
    ).astype(jnp.bfloat16)
    part = lax.axis_index("expert") % split
    pre = saved_pre[0, 0, 0]
    _, slope = gelu_parts(lax.dynamic_slice_in_dim(pre, part * share, share, 0))
    shares = exchange(partial_value, "expert", members).reshape(split, share, -1)
    own_grad = (jnp.sum(shares.astype(jnp.float32), axis=0) * slope).astype(jnp.bfloat16)
    hidden_grad = lax.all_gather(own_grad, "expert", axis_index_groups=members, tiled=True)

    act = gelu_parts(pre)[0].astype(jnp.bfloat16)
    term_down = lax.dot_general(
        act, rows, (((0,), (0,)), ((), ())), preferred_element_type=jnp.float32
    ).astype(jnp.bfloat16)
    down = sum_over_groups(term_down)

    back = lax.dot_general(
        hidden_grad, w_up[0], (((1,), (1,)), ((), ())), preferred_element_type=jnp.float32
    ).astype(jnp.bfloat16)
    returned = to_previous(exchange(back, "expert"))

    term_up = lax.dot_general(
        hidden_grad, saved_in[0, 0], (((0,), (0,)), ((), ())), preferred_element_type=jnp.float32
    ).astype(jnp.bfloat16)
    up = sum_over_groups(term_up)

    unpacked = (
        returned.reshape(experts, split, slots_per, quarter)
        .transpose(0, 2, 1, 3)
        .reshape(all_slots, width)
    )
    target_after = slot_targets(chosen_after, experts, slots_per)
    hit_after = [target_after[:, k][:, None] == slot_ids[None, :] for k in range(2)]
    place_after = (hit_after[0] | hit_after[1]).astype(jnp.bfloat16)
    total = grads_after.astype(jnp.float32) + jnp.dot(
        place_after, unpacked, preferred_element_type=jnp.float32
    )
    return (total.astype(jnp.bfloat16)[None], up[None], down[None])


def solution(mesh):
    in_specs = (
        P("phase", ("dp", "expert"), None),
        P("phase", ("dp", "expert"), None),
        P("phase", ("dp", "expert"), None),
        P("phase", "dp", None, "expert"),
        P("phase", "dp", "expert", None, None),
        P("phase", "expert", None),
        P("phase", None, "expert"),
    )
    out_specs = (
        P("phase", ("dp", "expert"), None),
        P("phase", "dp", "expert"),
        P("phase", "dp", "expert"),
    )
    return jax.shard_map(body, mesh=mesh, in_specs=in_specs, out_specs=out_specs, check_vma=False)
```

time: 535 us -> 208 us (0.39)
  waiting for transfers between devices: 459 us -> 110 us
  blocking collectives: 0 us -> 45.1 us
  between operations: 14.5 us -> 0.85 us
  starting transfers between devices: 42.3 us -> 33.9 us
    reduce_scatter x2 -> x0, waiting for transfers between devices: 345 us -> none  [the longest x1 209 us: body(): lax.psum_scatter(term_up.astype(jnp.bfloat16), 'dp', scatter_dimension=0,...]
    ppermute x12 -> x3, waiting for transfers between devices: 114 us -> 61.4 us  [to_previous(): return lax.ppermute(x, 'phase', [(i, i - 1) for i in range(1, peers)])]
    all_to_all x0 -> x4, waiting for transfers between devices: none -> 48.6 us  [exchange(): return lax.all_to_all(x, axis, 0, 0, tiled=True, axis_index_groups=groups)]
    ppermute x12 -> x3, starting transfers between devices: 42.2 us -> 3.88 us  [to_previous(): return lax.ppermute(x, 'phase', [(i, i - 1) for i in range(1, peers)])]
    all_to_all x0 -> x4, starting transfers between devices: none -> 30 us  [exchange(): return lax.all_to_all(x, axis, 0, 0, tiled=True, axis_index_groups=groups)]
    all_to_all x0 -> x1, blocking collectives: none -> 29.6 us  [exchange(): return lax.all_to_all(x, axis, 0, 0, tiled=True, axis_index_groups=groups)]
    all_gather x0 -> x1, blocking collectives: none -> 15.5 us  [body(): lax.all_gather(own_grad, 'expert', axis_index_groups=members, tiled=True)]
  transfers between devices with their start and end apart: 14 -> 7, of which waited for: 14 -> 5; matrix products, arithmetic and copies ran while one was open for 1% -> 4% of each run, Pallas kernels for 0% -> 0%
where the time goes in v1:
time: 208 us
  waiting for transfers between devices  110 us (53%)
  blocking collectives  45.1 us (22%)
  starting transfers between devices  33.9 us (16%)
  matrix products  10 us (5%)
  other arithmetic  4.36 us (2%)
  local copies, waits for them, and re-layouts  3.44 us (2%)
    ppermute x3, waiting for transfers between devices, to_previous(): return lax.ppermute(x, 'phase', [(i, i - 1) for i in range(1, peers)])  61.4 us
    all_to_all x4, waiting for transfers between devices, exchange(): return lax.all_to_all(x, axis, 0, 0, tiled=True, axis_index_groups=groups)  48.6 us
    all_to_all x4, starting transfers between devices, exchange(): return lax.all_to_all(x, axis, 0, 0, tiled=True, axis_index_groups=groups)  30 us
    all_to_all x1, blocking collectives, exchange(): return lax.all_to_all(x, axis, 0, 0, tiled=True, axis_index_groups=groups)  29.6 us
    all_gather x1, blocking collectives, body(): lax.all_gather(own_grad, 'expert', axis_index_groups=members, tiled=True)  15.5 us
  transfers between devices with their start and end apart: 7, of which 5 were waited for; matrix products, arithmetic and copies ran while one was open for 4% of the time, Pallas kernels for 0%

profile of v1, /device:TPU:1, one launch (start us, length us, event | category | flops | bytes accessed | tf_op | source)
XLA Modules:
  0.0 207.7 jit_solution(9653884275102718611)
XLA Ops:
  0.6 0.0 copy-start
  0.6 0.9 copy.19
  1.5 0.1 eq.132
  1.7 0.1 eq.128
  1.8 0.8 slice_bitcast_fusion.1
  2.6 0.6 reduce-window.16
  3.2 0.2 slice_reduce_fusion.4
  3.4 0.2 reduce-window.19
  3.6 0.1 add_bitcast_fusion
  3.7 0.1 reduce_sum.67
  3.8 0.2 slice_reduce_fusion.1
  4.0 0.1 add_reduce_fusion
  4.1 1.6 fusion
  5.9 29.6 %all_to_all.51 = bf16[16,16,640]{2,1,0:T(8,128)(2,1)S(1)} all-to-all(bf16[16,16,640]{2,1,0:T(8,128)(2,1)S(1)} %bitcast.91), channel_id=1, replica_groups=mesh['phase'=4,'dp'=16,'expert'=16] {'expert'}, dimensions={0} | all-to-all | bytes 655360 | tf_op jit(solution)/shard_map/all_to_all | solution.py:15
  35.5 1.2 convolution_convert_fusion.2
  36.7 3.5 %all-to-all-start.1 = ((bf16[8,32,768]{2,1,0:T(8,128)(2,1)}), bf16[8,32,768]{2,1,0:T(8,128)(2,1)S(1)}, u32[]{:S(2)}, u32[]{:S(2)}) async-start(bf16[8,32,768]{2,1,0:T(8,128)(2,1)} %bitcast.11), calls=%async_computation.1 | async-start | bytes 786432 | tf_op jit(solution)/shard_map/all_to_all | solution.py:15
  40.3 11.1 %all-to-all-done.1 = bf16[8,32,768]{2,1,0:T(8,128)(2,1)S(1)} async-done(((bf16[8,32,768]{2,1,0:T(8,128)(2,1)}), bf16[8,32,768]{2,1,0:T(8,128)(2,1)S(1)}, u32[]{:S(2)}, u32[]{:S(2)}) %all-to-all-start.1) | async-done | bytes 393248 | tf_op jit(solution)/shard_map/all_to_all | solution.py:15
  51.4 0.1 convert_reduce_fusion
  51.5 0.9 fusion.21
  52.4 0.0 copy-start.3
  52.4 15.5 %all_gather.3 = bf16[256,768]{1,0:T(8,128)(2,1)S(1)} all-gather(bf16[32,768]{1,0:T(8,128)(2,1)S(1)} %fusion.21), channel_id=1, replica_groups={{0,1,2,3,4,5,6,7},{8,9,10,11,12,13,14,15},{16,17,18,19,20,21,22,23},{24..., dimensions={0}, use_global_device_ids=true | all-gather | bytes 442368 | tf_op jit(solution)/shard_map/all_gather | solution.py:83
  67.8 1.2 convolution_convert_fusion.3
  69.1 3.6 %all-to-all-start.2 = ((bf16[16,16,640]{2,1,0:T(8,128)(2,1)}), bf16[16,16,640]{2,1,0:T(8,128)(2,1)S(1)}, u32[]{:S(2)}, u32[]{:S(2)}) async-start(bf16[16,16,640]{2,1,0:T(8,128)(2,1)} %bitcast.15), calls=%async_computation.2 | async-start | bytes 655360 | tf_op jit(solution)/shard_map/all_to_all | solution.py:15
  72.6 1.5 convolution_convert_fusion
  74.2 11.6 %all-to-all-done.2 = bf16[16,16,640]{2,1,0:T(8,128)(2,1)S(1)} async-done(((bf16[16,16,640]{2,1,0:T(8,128)(2,1)}), bf16[16,16,640]{2,1,0:T(8,128)(2,1)S(1)}, u32[]{:S(2)}, u32[]{:S(2)}) %all-to-all-start.2) | async-done | bytes 327712 | tf_op jit(solution)/shard_map/all_to_all | solution.py:15
  85.7 13.7 %all-to-all-start.4 = ((bf16[16,48,640]{2,1,0:T(8,128)(2,1)}), bf16[16,48,640]{2,1,0:T(8,128)(2,1)S(1)}, u32[]{:S(2)}, u32[]{:S(2)}) async-start(bf16[16,48,640]{2,1,0:T(8,128)(2,1)} %bitcast.24), calls=%async_computation.4 | async-start | bytes 1966080 | tf_op jit(solution)/shard_map/all_to_all | solution.py:15
  99.4 1.5 convolution_convert_fusion.1
  100.9 25.9 %all-to-all-done.4 = bf16[16,48,640]{2,1,0:T(8,128)(2,1)S(1)} async-done(((bf16[16,48,640]{2,1,0:T(8,128)(2,1)}), bf16[16,48,640]{2,1,0:T(8,128)(2,1)S(1)}, u32[]{:S(2)}, u32[]{:S(2)}) %all-to-all-start.4) | async-done | bytes 983072 | tf_op jit(solution)/shard_map/all_to_all | solution.py:15
  126.8 9.2 %all-to-all-start.3 = ((bf16[16,48,640]{2,1,0:T(8,128)(2,1)}), bf16[16,48,640]{2,1,0:T(8,128)(2,1)S(1)}, u32[]{:S(2)}, u32[]{:S(2)}) async-start(bf16[16,48,640]{2,1,0:T(8,128)(2,1)} %bitcast.21), calls=%async_computation.3 | async-start | bytes 1966080 | tf_op jit(solution)/shard_map/all_to_all | solution.py:15
  136.0 1.3 collective-permute-start
  137.3 1.3 collective-permute-start.1
  138.6 52.2 %collective-permute-done.1 = s32[128,2]{1,0:T(8,128)S(1)} collective-permute-done((s32[128,2]{1,0:T(8,128)S(1)}, s32[128,2]{1,0:T(8,128)S(1)}, u32[]{:S(2)}, u32[]{:S(2)}) %collective-permute-start.1) | collective-permute-done | bytes 1056 | tf_op jit(solution)/shard_map/ppermute | solution.py:20
  190.9 0.1 eq.116
  191.0 0.6 reduce-window.14
  191.6 0.2 slice_reduce_fusion.5
  191.9 0.2 reduce-window.15
  192.0 0.1 eq.112
  192.2 0.1 add_bitcast_fusion.1
  192.3 0.1 reduce_sum.65
  192.4 1.3 collective-permute-start.2
  193.7 0.2 slice_reduce_fusion.3
  193.9 9.2 %collective-permute-done.2 = bf16[256,640]{1,0:T(8,128)(2,1)S(1)} collective-permute-done((bf16[256,640]{1,0:T(8,128)(2,1)S(1)}, bf16[256,640]{1,0:T(8,128)(2,1)S(1)}, u32[]{:S(2)}, u32[]{:S(2)}) %collective-permute-start.2) | collective-permute-done | bytes 327712 | tf_op jit(solution)/shard_map/ppermute | solution.py:20
  203.1 0.1 copy.23
  203.2 0.0 collective-permute-done
  203.2 2.9 %fusion.1 = bf16[1,128,5120]{2,1,0:T(8,128)(2,1)} fusion(bf16[128,5120]{1,0:T(8,128)(2,1)} %collective-permute-done, bf16[32,5120]{1,0:T(8,128)(2,1)S(1)} %bitcast.97, s32[128]{0:T(128)S(1)} %get-tuple-element.4, s32[128]{0:T(128)S(1)} %get-tuple-element.3), kind=kOutput, calls=%fused_computation.5 | convolution fusion | flops 43921408 | bytes 2950144 | tf_op jit(solution)/shard_map/dot_general | solution.py:109
  206.2 0.8 reduce_sum.71
  206.9 0.0 all-to-all-done.3
  206.9 0.8 reduce_sum.70
  (15 shorter events, 0.2 us)
Async XLA Ops:
  0.6 34.9 %copy-start = (bf16[1,768,640]{2,1,0:T(8,128)(2,1)S(1)}, bf16[1,768,640]{2,1,0:T(8,128)(2,1)}, u32[]{:S(2)}) copy-start(bf16[1,768,640]{2,1,0:T(8,128)(2,1)} %param.13) | copy-start | bytes 2949124
  36.7 31.1 %copy-start.1 = (bf16[1,640,768]{2,1,0:T(8,128)(2,1)S(1)}, bf16[1,640,768]{2,1,0:T(8,128)(2,1)}, u32[]{:S(2)}) copy-start(bf16[1,640,768]{2,1,0:T(8,128)(2,1)} %param.12) | copy-start | bytes 2949124
  36.7 14.7 %all-to-all-start.1 = ((bf16[8,32,768]{2,1,0:T(8,128)(2,1)}), bf16[8,32,768]{2,1,0:T(8,128)(2,1)S(1)}, u32[]{:S(2)}, u32[]{:S(2)}) async-start(bf16[8,32,768]{2,1,0:T(8,128)(2,1)} %bitcast.11), calls=%async_computation.1 | async-start | bytes 786432 | tf_op jit(solution)/shard_map/all_to_all | solution.py:15
  52.4 20.3 %copy-start.3 = (bf16[1,1,1,256,768]{4,3,2,1,0:T(8,128)(2,1)S(1)}, bf16[1,1,1,256,768]{4,3,2,1,0:T(8,128)(2,1)}, u32[]{:S(2)}) copy-start(bf16[1,1,1,256,768]{4,3,2,1,0:T(8,128)(2,1)} %param.11) | copy-start | bytes 1179652
  69.1 16.7 %all-to-all-start.2 = ((bf16[16,16,640]{2,1,0:T(8,128)(2,1)}), bf16[16,16,640]{2,1,0:T(8,128)(2,1)S(1)}, u32[]{:S(2)}, u32[]{:S(2)}) async-start(bf16[16,16,640]{2,1,0:T(8,128)(2,1)} %bitcast.15), calls=%async_computation.2 | async-start | bytes 655360 | tf_op jit(solution)/shard_map/all_to_all | solution.py:15
  74.2 25.2 %copy-start.2 = (bf16[1,1,256,640]{3,2,1,0:T(8,128)(2,1)S(1)}, bf16[1,1,256,640]{3,2,1,0:T(8,128)(2,1)}, u32[]{:S(2)}) copy-start(bf16[1,1,256,640]{3,2,1,0:T(8,128)(2,1)} %param.10) | copy-start | bytes 983044
  85.7 41.1 %all-to-all-start.4 = ((bf16[16,48,640]{2,1,0:T(8,128)(2,1)}), bf16[16,48,640]{2,1,0:T(8,128)(2,1)S(1)}, u32[]{:S(2)}, u32[]{:S(2)}) async-start(bf16[16,48,640]{2,1,0:T(8,128)(2,1)} %bitcast.24), calls=%async_computation.4 | async-start | bytes 1966080 | tf_op jit(solution)/shard_map/all_to_all | solution.py:15
  126.8 80.1 %all-to-all-start.3 = ((bf16[16,48,640]{2,1,0:T(8,128)(2,1)}), bf16[16,48,640]{2,1,0:T(8,128)(2,1)S(1)}, u32[]{:S(2)}, u32[]{:S(2)}) async-start(bf16[16,48,640]{2,1,0:T(8,128)(2,1)} %bitcast.21), calls=%async_computation.3 | async-start | bytes 1966080 | tf_op jit(solution)/shard_map/all_to_all | solution.py:15
  136.0 67.2 %collective-permute-start = (bf16[128,5120]{1,0:T(8,128)(2,1)}, bf16[128,5120]{1,0:T(8,128)(2,1)}, u32[]{:S(2)}, u32[]{:S(2)}) collective-permute-start(bf16[128,5120]{1,0:T(8,128)(2,1)} %bitcast.93), channel_id=1, source_target_pairs={{256,0},{512,256},{768,512},{257,1},{513,257},{769,513},{258,2},{5... | collective-permute-start | bytes 3932168 | tf_op jit(solution)/shard_map/ppermute | solution.py:20
  137.3 53.5 %collective-permute-start.1 = (s32[128,2]{1,0:T(8,128)S(1)}, s32[128,2]{1,0:T(8,128)S(1)}, u32[]{:S(2)}, u32[]{:S(2)}) collective-permute-start(s32[128,2]{1,0:T(8,128)S(1)} %bitcast.98), channel_id=1, source_target_pairs={{256,0},{512,256},{768,512},{257,1},{513,257},{769,513},{258,2},{5... | collective-permute-start | bytes 3080 | tf_op jit(solution)/shard_map/ppermute | solution.py:20
  192.4 10.7 %collective-permute-start.2 = (bf16[256,640]{1,0:T(8,128)(2,1)S(1)}, bf16[256,640]{1,0:T(8,128)(2,1)S(1)}, u32[]{:S(2)}, u32[]{:S(2)}) collective-permute-start(bf16[256,640]{1,0:T(8,128)(2,1)S(1)} %bitcast.99), channel_id=1, source_target_pairs={{256,0},{512,256},{768,512},{257,1},{513,257},{769,513},{258,2},{5... | collective-permute-start | bytes 983048 | tf_op jit(solution)/shard_map/ppermute | solution.py:20

commit v2 on v1

--- a/solution.py
+++ b/solution.py
@@ -36,6 +36,29 @@
     return jnp.sum(pieces.astype(jnp.float32), axis=0).astype(jnp.bfloat16)
 
 
+def scatter_over_groups(term):
+    count = lax.axis_size("dp")
+    near = count // 2
+    hid, quarter = term.shape
+    piece = hid // count
+    groups = [[h * near + z for z in range(near)] for h in range(2)]
+    ordered = term.reshape(2, near, piece, quarter).transpose(1, 0, 2, 3).reshape(hid, quarter)
+    summed = lax.psum_scatter(
+        ordered, "dp", scatter_dimension=0, axis_index_groups=groups, tiled=True
+    )
+    return summed.reshape(2, piece, quarter)
+
+
+def finish_groups(summed):
+    count = lax.axis_size("dp")
+    near = count // 2
+    half = lax.axis_index("dp") // near
+    away = lax.dynamic_index_in_dim(summed, 1 - half, 0, keepdims=False)
+    keep = lax.dynamic_index_in_dim(summed, half, 0, keepdims=False)
+    got = lax.ppermute(away, "dp", [(i, (i + near) % count) for i in range(count)])
+    return (keep.astype(jnp.float32) + got.astype(jnp.float32)).astype(jnp.bfloat16)
+
+
 def body(grad_out, routes, gates, saved_in, saved_pre, w_up, w_down):
     count = lax.axis_size("expert")
     grads = grad_out[0]
@@ -49,9 +72,7 @@
     all_slots = experts * slots_per
     members = [[e * split + q for q in range(split)] for e in range(experts)]
     share = count * slots_per // split
-
-    grads_after = to_previous(grads)
-    chosen_after = to_previous(chosen)
+    half = tokens // 2
 
     target = slot_targets(chosen, experts, slots_per)
     slot_ids = jnp.arange(all_slots, dtype=jnp.int32)
@@ -70,42 +91,54 @@
         .transpose(0, 2, 1, 3)
         .reshape(count * slots_per, quarter)
     )
+
+    outgoing, upper, target = lax.optimization_barrier((outgoing, grads[:half], target))
+    upper_after = to_previous(upper)
+    target_after = to_previous(target)
     rows = exchange(outgoing, "expert")
+    rows, upper_after, target_after = lax.optimization_barrier((rows, upper_after, target_after))
 
     partial_value = lax.dot_general(
         rows, w_down[0], (((1,), (1,)), ((), ())), preferred_element_type=jnp.float32
     ).astype(jnp.bfloat16)
-    part = lax.axis_index("expert") % split
     pre = saved_pre[0, 0, 0]
-    _, slope = gelu_parts(lax.dynamic_slice_in_dim(pre, part * share, share, 0))
-    shares = exchange(partial_value, "expert", members).reshape(split, share, -1)
-    own_grad = (jnp.sum(shares.astype(jnp.float32), axis=0) * slope).astype(jnp.bfloat16)
-    hidden_grad = lax.all_gather(own_grad, "expert", axis_index_groups=members, tiled=True)
-
     act = gelu_parts(pre)[0].astype(jnp.bfloat16)
     term_down = lax.dot_general(
         act, rows, (((0,), (0,)), ((), ())), preferred_element_type=jnp.float32
     ).astype(jnp.bfloat16)
-    down = sum_over_groups(term_down)
+    down_scattered = scatter_over_groups(term_down)
+
+    part = lax.axis_index("expert") % split
+    _, slope = gelu_parts(lax.dynamic_slice_in_dim(pre, part * share, share, 0))
+    partial_value, lower = lax.optimization_barrier((partial_value, grads[half:]))
+    lower_after = to_previous(lower)
+    shares = exchange(partial_value, "expert", members)
+    shares, lower_after = lax.optimization_barrier((shares, lower_after))
+    own_grad = (
+        jnp.sum(shares.reshape(split, share, -1).astype(jnp.float32), axis=0) * slope
+    ).astype(jnp.bfloat16)
+    hidden_grad = lax.all_gather(own_grad, "expert", axis_index_groups=members, tiled=True)
 
     back = lax.dot_general(
         hidden_grad, w_up[0], (((1,), (1,)), ((), ())), preferred_element_type=jnp.float32
     ).astype(jnp.bfloat16)
-    returned = to_previous(exchange(back, "expert"))
-
+    returned = exchange(back, "expert")
     term_up = lax.dot_general(
         hidden_grad, saved_in[0, 0], (((0,), (0,)), ((), ())), preferred_element_type=jnp.float32
     ).astype(jnp.bfloat16)
+    returned, term_up = lax.optimization_barrier((returned, term_up))
+    returned = to_previous(returned)
     up = sum_over_groups(term_up)
+    down = finish_groups(down_scattered)
 
     unpacked = (
         returned.reshape(experts, split, slots_per, quarter)
         .transpose(0, 2, 1, 3)
         .reshape(all_slots, width)
     )
-    target_after = slot_targets(chosen_after, experts, slots_per)
     hit_after = [target_after[:, k][:, None] == slot_ids[None, :] for k in range(2)]
     place_after = (hit_after[0] | hit_after[1]).astype(jnp.bfloat16)
+    grads_after = jnp.concatenate([upper_after, lower_after], axis=0)
     total = grads_after.astype(jnp.float32) + jnp.dot(
         place_after, unpacked, preferred_element_type=jnp.float32
     )

time: 208 us -> 170 us (0.82)
  waiting for transfers between devices: 110 us -> 74.1 us
  blocking collectives: 45.1 us -> 15 us
  starting transfers between devices: 33.9 us -> 48.6 us
  between operations: 0.85 us -> 14.3 us
  local copies, waits for them, and re-layouts: 3.44 us -> 7.01 us
  matrix products: 10 us -> 7.75 us
    all_to_all x4, waiting for transfers between devices: 48.6 us -> 17.4 us  [exchange(): return lax.all_to_all(x, axis, 0, 0, tiled=True, axis_index_groups=groups)]
    all_to_all x1 -> x0, blocking collectives: 29.6 us -> none  [exchange(): return lax.all_to_all(x, axis, 0, 0, tiled=True, axis_index_groups=groups)]
    all_to_all x4, starting transfers between devices: 30 us -> 39.2 us  [exchange(): return lax.all_to_all(x, axis, 0, 0, tiled=True, axis_index_groups=groups)]
    ppermute x3 -> x4, waiting for transfers between devices: 61.4 us -> 53.8 us  [to_previous(): return lax.ppermute(x, 'phase', [(i, i - 1) for i in range(1, peers)])]
    ppermute x0 -> x1, starting transfers between devices: none -> 4.06 us  [finish_groups(): lax.ppermute(away, 'dp', [(i, (i + near) % count) for i in range(count)])]
    ppermute x0 -> x1, waiting for transfers between devices: none -> 2.92 us  [finish_groups(): lax.ppermute(away, 'dp', [(i, (i + near) % count) for i in range(count)])]
    ppermute x3 -> x4, starting transfers between devices: 3.88 us -> 5.29 us  [to_previous(): return lax.ppermute(x, 'phase', [(i, i - 1) for i in range(1, peers)])]
  transfers between devices with their start and end apart: 7 -> 10, of which waited for: 5 -> 6; matrix products, arithmetic and copies ran while one was open for 4% -> 5% of each run, Pallas kernels for 0% -> 0%
where the time goes in v2:
time: 170 us; the launch traced here: 169 us
  waiting for transfers between devices  74.1 us (44%)
  starting transfers between devices  48.6 us (29%)
  blocking collectives  15 us (9%)
  between operations  14.3 us (8%)
  matrix products  7.75 us (5%)
  local copies, waits for them, and re-layouts  7.01 us (4%)
  other arithmetic  2.54 us (1%)
    ppermute x4, waiting for transfers between devices, to_previous(): return lax.ppermute(x, 'phase', [(i, i - 1) for i in range(1, peers)])  53.8 us
    all_to_all x4, starting transfers between devices, exchange(): return lax.all_to_all(x, axis, 0, 0, tiled=True, axis_index_groups=groups)  39.2 us
    all_to_all x4, waiting for transfers between devices, exchange(): return lax.all_to_all(x, axis, 0, 0, tiled=True, axis_index_groups=groups)  17.4 us
    all_gather x1, blocking collectives, body(): lax.all_gather(own_grad, 'expert', axis_index_groups=members, tiled=True)  15 us
    ppermute x4, starting transfers between devices, to_previous(): return lax.ppermute(x, 'phase', [(i, i - 1) for i in range(1, peers)])  5.29 us
    ppermute x1, starting transfers between devices, finish_groups(): lax.ppermute(away, 'dp', [(i, (i + near) % count) for i in range(count)])  4.06 us
  transfers between devices with their start and end apart: 10, of which 6 were waited for; matrix products, arithmetic and copies ran while one was open for 5% of the time, Pallas kernels for 0%

profile of v2, /device:TPU:1, one launch (start us, length us, event | category | flops | bytes accessed | tf_op | source)
XLA Modules:
  0.0 169.3 jit_solution(14624153131168978188)
XLA Ops:
  7.2 0.0 copy-start
  7.2 0.9 copy.21
  8.0 0.1 eq.91
  8.2 0.1 eq.87
  8.3 0.8 slice_bitcast_fusion.3
  9.1 0.6 reduce-window.6
  9.7 0.2 slice_reduce_fusion.4
  9.9 0.2 reduce-window.9
  10.1 0.1 add_bitcast_fusion
  10.2 0.1 reduce_sum.42
  10.4 0.2 slice_reduce_fusion.1
  10.6 1.5 slice_bitcast_fusion
  12.0 0.1 add_reduce_fusion
  12.2 0.1 copy-done.1
  12.3 0.3 fusion.2
  12.6 0.8 copy.24
  13.4 1.3 collective-permute-start
  14.7 17.5 %all-to-all-start = ((bf16[16,16,640]{2,1,0:T(8,128)(2,1)}), bf16[16,16,640]{2,1,0:T(8,128)(2,1)S(1)}, u32[]{:S(2)}, u32[]{:S(2)}) async-start(bf16[16,16,640]{2,1,0:T(8,128)(2,1)} %bitcast.9), calls=%async_computation | async-start | bytes 655360 | tf_op jit(solution)/shard_map/all_to_all | solution.py:15
  32.2 1.4 collective-permute-start.1
  33.6 5.8 %collective-permute-done.1 = s32[128,2]{1,0:T(8,128)S(1)} collective-permute-done((s32[128,2]{1,0:T(8,128)S(1)}, s32[128,2]{1,0:T(8,128)S(1)}, u32[]{:S(2)}, u32[]{:S(2)}) %collective-permute-start.1) | collective-permute-done | bytes 1056 | tf_op jit(solution)/shard_map/ppermute | solution.py:20
  39.4 5.8 %all-to-all-done = bf16[16,16,640]{2,1,0:T(8,128)(2,1)S(1)} async-done(((bf16[16,16,640]{2,1,0:T(8,128)(2,1)}), bf16[16,16,640]{2,1,0:T(8,128)(2,1)S(1)}, u32[]{:S(2)}, u32[]{:S(2)}) %all-to-all-start) | async-done | bytes 327712 | tf_op jit(solution)/shard_map/all_to_all | solution.py:15
  45.2 1.2 convolution_convert_fusion.2
  46.5 3.4 %all-to-all-start.1 = ((bf16[8,32,768]{2,1,0:T(8,128)(2,1)}), bf16[8,32,768]{2,1,0:T(8,128)(2,1)S(1)}, u32[]{:S(2)}, u32[]{:S(2)}) async-start(bf16[8,32,768]{2,1,0:T(8,128)(2,1)} %bitcast.13), calls=%async_computation.1 | async-start | bytes 786432 | tf_op jit(solution)/shard_map/all_to_all | solution.py:15
  49.9 0.0 reduce-scatter.2.cloned.1.call-start
  49.9 1.3 collective-permute-start.2
  51.3 0.6 convolution_convert_fusion
  51.8 1.0 copy.26
  52.9 0.0 reduce-scatter.2.cloned.1.call-update
  52.9 16.1 %collective-permute-done.2 = bf16[64,5120]{1,0:T(8,128)(2,1)} collective-permute-done((bf16[64,5120]{1,0:T(8,128)(2,1)S(1)}, bf16[64,5120]{1,0:T(8,128)(2,1)}, u32[]{:S(2)}, u32[]{:S(2)}) %collective-permute-start.2) | collective-permute-done | bytes 655392 | tf_op jit(solution)/shard_map/ppermute | solution.py:20
  69.0 0.1 convert_reduce_fusion
  69.0 0.1 fusion.24
  69.1 15.0 %all_gather.3 = bf16[256,768]{1,0:T(8,128)(2,1)S(1)} all-gather(bf16[32,768]{1,0:T(8,128)(2,1)S(1)} %fusion.24), channel_id=1, replica_groups={{0,1,2,3,4,5,6,7},{8,9,10,11,12,13,14,15},{16,17,18,19,20,21,22,23},{24..., dimensions={0}, use_global_device_ids=true | all-gather | bytes 442368 | tf_op jit(solution)/shard_map/all_gather | solution.py:120
  84.2 1.2 convolution_convert_fusion.3
  85.4 4.8 %all-to-all-start.2 = ((bf16[16,16,640]{2,1,0:T(8,128)(2,1)}), bf16[16,16,640]{2,1,0:T(8,128)(2,1)S(1)}, u32[]{:S(2)}, u32[]{:S(2)}) async-start(bf16[16,16,640]{2,1,0:T(8,128)(2,1)} %bitcast.19), calls=%async_computation.2 | async-start | bytes 655360 | tf_op jit(solution)/shard_map/all_to_all | solution.py:15
  90.2 1.5 convolution_convert_fusion.1
  91.7 11.6 %all-to-all-done.2 = bf16[16,16,640]{2,1,0:T(8,128)(2,1)S(1)} async-done(((bf16[16,16,640]{2,1,0:T(8,128)(2,1)}), bf16[16,16,640]{2,1,0:T(8,128)(2,1)S(1)}, u32[]{:S(2)}, u32[]{:S(2)}) %all-to-all-start.2) | async-done | bytes 327712 | tf_op jit(solution)/shard_map/all_to_all | solution.py:15
  103.3 13.5 %all-to-all-start.3 = ((bf16[16,48,640]{2,1,0:T(8,128)(2,1)}), bf16[16,48,640]{2,1,0:T(8,128)(2,1)S(1)}, u32[]{:S(2)}, u32[]{:S(2)}) async-start(bf16[16,48,640]{2,1,0:T(8,128)(2,1)} %bitcast.25), calls=%async_computation.3 | async-start | bytes 1966080 | tf_op jit(solution)/shard_map/all_to_all | solution.py:15
  116.8 1.3 collective-permute-start.3
  118.1 0.2 slice_reduce_fusion.3
  118.3 31.9 %collective-permute-done.3 = bf16[256,640]{1,0:T(8,128)(2,1)S(1)} collective-permute-done((bf16[256,640]{1,0:T(8,128)(2,1)S(1)}, bf16[256,640]{1,0:T(8,128)(2,1)S(1)}, u32[]{:S(2)}, u32[]{:S(2)}) %collective-permute-start.3) | collective-permute-done | bytes 327712 | tf_op jit(solution)/shard_map/ppermute | solution.py:20
  150.2 0.1 copy.25
  150.3 0.0 reduce-scatter.2.cloned.1.call-done
  150.3 0.8 dynamic-slice_bitcast_fusion
  151.2 4.1 %collective-permute-start.4 = (bf16[48,640]{1,0:T(8,128)(2,1)S(1)}, bf16[48,640]{1,0:T(8,128)(2,1)S(1)}, u32[]{:S(2)}, u32[]{:S(2)}) collective-permute-start(bf16[48,640]{1,0:T(8,128)(2,1)S(1)} %dynamic-slice_bitcast_fusion), channel_id=1, source_target_pairs={{0,128},{16,144},{32,160},{48,176},{64,192},{80,208},{96,224},{112... | collective-permute-start | bytes 184328 | tf_op jit(solution)/shard_map/ppermute | solution.py:58
  155.2 2.9 %fusion.1 = bf16[1,128,5120]{2,1,0:T(8,128)(2,1)} fusion(bf16[32,5120]{1,0:T(8,128)(2,1)S(1)} %bitcast.98, bf16[64,5120]{1,0:T(8,128)(2,1)} %collective-permute-done.2, bf16[64,5120]{1,0:T(8,128)(2,1)} %collective-permute-done, s32[128]{0:T(128)S(1)} %get-tuple-element.28, s32[128]{0:T(128)S(1)} %get-tuple-element.27), kind=kOutput, calls=%fused_computation.2 | convolution fusion | flops 45887488 | bytes 2950144 | tf_op jit(solution)/shard_map/dot_general | solution.py:142
  158.2 2.9 %collective-permute-done.4 = bf16[48,640]{1,0:T(8,128)(2,1)S(1)} collective-permute-done((bf16[48,640]{1,0:T(8,128)(2,1)S(1)}, bf16[48,640]{1,0:T(8,128)(2,1)S(1)}, u32[]{:S(2)}, u32[]{:S(2)}) %collective-permute-start.4) | collective-permute-done | bytes 61472 | tf_op jit(solution)/shard_map/ppermute | solution.py:58
  161.1 0.6 fusion.27
  161.7 0.8 reduce_sum.45
  (18 shorter events, 0.1 us)
Async XLA Ops:
  7.2 38.1 %copy-start = (bf16[1,768,640]{2,1,0:T(8,128)(2,1)S(1)}, bf16[1,768,640]{2,1,0:T(8,128)(2,1)}, u32[]{:S(2)}) copy-start(bf16[1,768,640]{2,1,0:T(8,128)(2,1)} %param.13) | copy-start | bytes 2949124
  10.6 1.7 %copy-start.1 = (bf16[1,128,5120]{2,1,0:T(8,128)(2,1)S(1)}, bf16[1,128,5120]{2,1,0:T(8,128)(2,1)}, u32[]{:S(2)}) copy-start(bf16[1,128,5120]{2,1,0:T(8,128)(2,1)} %param.7) | copy-start | bytes 3932164
  13.4 31.8 %collective-permute-start = (bf16[64,5120]{1,0:T(8,128)(2,1)S(1)}, bf16[64,5120]{1,0:T(8,128)(2,1)}, u32[]{:S(2)}, u32[]{:S(2)}) collective-permute-start(bf16[64,5120]{1,0:T(8,128)(2,1)S(1)} %get-tuple-element.16), channel_id=1, source_target_pairs={{256,0},{512,256},{768,512},{257,1},{513,257},{769,513},{258,2},{5... | collective-permute-start | bytes 1966088 | tf_op jit(solution)/shard_map/ppermute | solution.py:20
  14.7 30.5 %all-to-all-start = ((bf16[16,16,640]{2,1,0:T(8,128)(2,1)}), bf16[16,16,640]{2,1,0:T(8,128)(2,1)S(1)}, u32[]{:S(2)}, u32[]{:S(2)}) async-start(bf16[16,16,640]{2,1,0:T(8,128)(2,1)} %bitcast.9), calls=%async_computation | async-start | bytes 655360 | tf_op jit(solution)/shard_map/all_to_all | solution.py:15
  32.2 19.1 %copy-start.5 = (bf16[1,1,1,256,768]{4,3,2,1,0:T(8,128)(2,1)S(1)}, bf16[1,1,1,256,768]{4,3,2,1,0:T(8,128)(2,1)}, u32[]{:S(2)}) copy-start(bf16[1,1,1,256,768]{4,3,2,1,0:T(8,128)(2,1)} %param.11) | copy-start | bytes 1179652
  32.2 7.2 %collective-permute-start.1 = (s32[128,2]{1,0:T(8,128)S(1)}, s32[128,2]{1,0:T(8,128)S(1)}, u32[]{:S(2)}, u32[]{:S(2)}) collective-permute-start(s32[128,2]{1,0:T(8,128)S(1)} %bitcast_add_fusion), channel_id=1, source_target_pairs={{256,0},{512,256},{768,512},{257,1},{513,257},{769,513},{258,2},{5... | collective-permute-start | bytes 3080 | tf_op jit(solution)/shard_map/ppermute | solution.py:20
  46.5 22.5 %all-to-all-start.1 = ((bf16[8,32,768]{2,1,0:T(8,128)(2,1)}), bf16[8,32,768]{2,1,0:T(8,128)(2,1)S(1)}, u32[]{:S(2)}, u32[]{:S(2)}) async-start(bf16[8,32,768]{2,1,0:T(8,128)(2,1)} %bitcast.13), calls=%async_computation.1 | async-start | bytes 786432 | tf_op jit(solution)/shard_map/all_to_all | solution.py:15
  49.9 100.4 %reduce-scatter.2.cloned.1.call-start = ((), (), s32[]{:S(2)}) async-start(), calls=%async_computation.5 | async-start | bytes 1105920 | tf_op jit(solution)/shard_map/reduce_scatter | solution.py:46
  49.9 19.0 %collective-permute-start.2 = (bf16[64,5120]{1,0:T(8,128)(2,1)S(1)}, bf16[64,5120]{1,0:T(8,128)(2,1)}, u32[]{:S(2)}, u32[]{:S(2)}) collective-permute-start(bf16[64,5120]{1,0:T(8,128)(2,1)S(1)} %get-tuple-element.21), channel_id=1, source_target_pairs={{256,0},{512,256},{768,512},{257,1},{513,257},{769,513},{258,2},{5... | collective-permute-start | bytes 1966088 | tf_op jit(solution)/shard_map/ppermute | solution.py:20
  52.9 31.3 %copy-start.2 = (bf16[1,640,768]{2,1,0:T(8,128)(2,1)S(1)}, bf16[1,640,768]{2,1,0:T(8,128)(2,1)}, u32[]{:S(2)}) copy-start(bf16[1,640,768]{2,1,0:T(8,128)(2,1)} %param.12) | copy-start | bytes 2949124
  69.1 21.1 %copy-start.3 = (bf16[1,1,256,640]{3,2,1,0:T(8,128)(2,1)S(1)}, bf16[1,1,256,640]{3,2,1,0:T(8,128)(2,1)}, u32[]{:S(2)}) copy-start(bf16[1,1,256,640]{3,2,1,0:T(8,128)(2,1)} %param.10) | copy-start | bytes 983044
  85.4 17.9 %all-to-all-start.2 = ((bf16[16,16,640]{2,1,0:T(8,128)(2,1)}), bf16[16,16,640]{2,1,0:T(8,128)(2,1)S(1)}, u32[]{:S(2)}, u32[]{:S(2)}) async-start(bf16[16,16,640]{2,1,0:T(8,128)(2,1)} %bitcast.19), calls=%async_computation.2 | async-start | bytes 655360 | tf_op jit(solution)/shard_map/all_to_all | solution.py:15
  103.3 58.5 %all-to-all-start.3 = ((bf16[16,48,640]{2,1,0:T(8,128)(2,1)}), bf16[16,48,640]{2,1,0:T(8,128)(2,1)S(1)}, u32[]{:S(2)}, u32[]{:S(2)}) async-start(bf16[16,48,640]{2,1,0:T(8,128)(2,1)} %bitcast.25), calls=%async_computation.3 | async-start | bytes 1966080 | tf_op jit(solution)/shard_map/all_to_all | solution.py:15
  116.8 33.4 %collective-permute-start.3 = (bf16[256,640]{1,0:T(8,128)(2,1)S(1)}, bf16[256,640]{1,0:T(8,128)(2,1)S(1)}, u32[]{:S(2)}, u32[]{:S(2)}) collective-permute-start(bf16[256,640]{1,0:T(8,128)(2,1)S(1)} %bitcast.100), channel_id=1, source_target_pairs={{256,0},{512,256},{768,512},{257,1},{513,257},{769,513},{258,2},{5... | collective-permute-start | bytes 983048 | tf_op jit(solution)/shard_map/ppermute | solution.py:20
  151.2 9.9 %collective-permute-start.4 = (bf16[48,640]{1,0:T(8,128)(2,1)S(1)}, bf16[48,640]{1,0:T(8,128)(2,1)S(1)}, u32[]{:S(2)}, u32[]{:S(2)}) collective-permute-start(bf16[48,640]{1,0:T(8,128)(2,1)S(1)} %dynamic-slice_bitcast_fusion), channel_id=1, source_target_pairs={{0,128},{16,144},{32,160},{48,176},{64,192},{80,208},{96,224},{112... | collective-permute-start | bytes 184328 | tf_op jit(solution)/shard_map/ppermute | solution.py:58
  155.2 5.9 %copy-start.4 = (bf16[96,640]{1,0:T(8,128)(2,1)S(1)}, bf16[96,640]{1,0:T(8,128)(2,1)}, u32[]{:S(2)}) copy-start(bf16[96,640]{1,0:T(8,128)(2,1)} %reduce-scatter.2.cloned.1.call-done) | copy-start | bytes 368644
Sparse Core Ops, SparseCore 0:
  54.7 41.8 reduce-scatter.1

commit v3 on v1

--- a/solution.py
+++ b/solution.py
@@ -29,11 +29,46 @@
     return (flat * slots_per + slot).reshape(tokens, 2)
 
 
-def sum_over_groups(term):
+def along_z(term, steps):
     count = lax.axis_size("dp")
+    near = count // 2
     hid, quarter = term.shape
-    pieces = exchange(term, "dp").reshape(count, hid // count, quarter)
-    return jnp.sum(pieces.astype(jnp.float32), axis=0).astype(jnp.bfloat16)
+    blocks = term.reshape(2, near, hid // count, quarter)
+    here = lax.axis_index("dp") % near
+    arrived = []
+    for k in steps:
+        block = lax.dynamic_index_in_dim(blocks, (here + k) % near, 1, keepdims=False)
+        block = block.reshape(hid // near, quarter)
+        if k:
+            pairs = [
+                (h * near + z, h * near + (z + k) % near) for h in range(2) for z in range(near)
+            ]
+            block = lax.ppermute(block, "dp", pairs)
+        arrived.append(block)
+    return arrived
+
+
+def add_up(blocks):
+    total = blocks[0].astype(jnp.float32)
+    for block in blocks[1:]:
+        total = total + block.astype(jnp.float32)
+    return total
+
+
+def across_x(sums):
+    count = lax.axis_size("dp")
+    near = count // 2
+    side = lax.axis_index("dp") // near
+    both = jnp.stack([s.reshape(2, s.shape[0] // 2, s.shape[1]) for s in sums], axis=1)
+    away = jnp.where(side == 1, both[0], both[1]).astype(jnp.bfloat16)
+    keep = jnp.where(side == 1, both[1], both[0])
+    got = lax.ppermute(away, "dp", [(i, (i + near) % count) for i in range(count)])
+    out = (keep + got.astype(jnp.float32)).astype(jnp.bfloat16)
+    return [out[i] for i in range(len(sums))]
+
+
+def hold(*values):
+    return lax.optimization_barrier(values)
 
 
 def body(grad_out, routes, gates, saved_in, saved_pre, w_up, w_down):
@@ -49,9 +84,10 @@
     all_slots = experts * slots_per
     members = [[e * split + q for q in range(split)] for e in range(experts)]
     share = count * slots_per // split
-
-    grads_after = to_previous(grads)
-    chosen_after = to_previous(chosen)
+    near = lax.axis_size("dp") // 2
+    steps = sorted(range(1, near), key=lambda k: min(k, near - k))
+    short, long = steps[: near // 2], steps[near // 2 :]
+    cuts = (tokens // 2, tokens * 3 // 4)
 
     target = slot_targets(chosen, experts, slots_per)
     slot_ids = jnp.arange(all_slots, dtype=jnp.int32)
@@ -70,42 +106,59 @@
         .transpose(0, 2, 1, 3)
         .reshape(count * slots_per, quarter)
     )
+
+    outgoing, target, first_part = hold(outgoing, target, grads[: cuts[0]])
+    first_after = to_previous(first_part)
+    target_after = to_previous(target)
     rows = exchange(outgoing, "expert")
+    rows, first_after, target_after = hold(rows, first_after, target_after)
 
     partial_value = lax.dot_general(
         rows, w_down[0], (((1,), (1,)), ((), ())), preferred_element_type=jnp.float32
     ).astype(jnp.bfloat16)
-    part = lax.axis_index("expert") % split
     pre = saved_pre[0, 0, 0]
-    _, slope = gelu_parts(lax.dynamic_slice_in_dim(pre, part * share, share, 0))
-    shares = exchange(partial_value, "expert", members).reshape(split, share, -1)
-    own_grad = (jnp.sum(shares.astype(jnp.float32), axis=0) * slope).astype(jnp.bfloat16)
-    hidden_grad = lax.all_gather(own_grad, "expert", axis_index_groups=members, tiled=True)
-
     act = gelu_parts(pre)[0].astype(jnp.bfloat16)
     term_down = lax.dot_general(
         act, rows, (((0,), (0,)), ((), ())), preferred_element_type=jnp.float32
     ).astype(jnp.bfloat16)
-    down = sum_over_groups(term_down)
+    part = lax.axis_index("expert") % split
+    _, slope = gelu_parts(lax.dynamic_slice_in_dim(pre, part * share, share, 0))
+    partial_value, second_part = hold(partial_value, grads[cuts[0] : cuts[1]])
+    shares = exchange(partial_value, "expert", members)
+    second_after = to_previous(second_part)
+    down_blocks = along_z(term_down, [0] + short)
+    shares, second_after, *down_blocks = hold(shares, second_after, *down_blocks)
+    own_grad = (
+        jnp.sum(shares.reshape(split, share, -1).astype(jnp.float32), axis=0) * slope
+    ).astype(jnp.bfloat16)
+    own_grad, third_part, term_down = hold(own_grad, grads[cuts[1] :], term_down)
+    hidden_grad = exchange(jnp.tile(own_grad, (split, 1)), "expert", members)
+    third_after = to_previous(third_part)
+    down_rest = along_z(term_down, long)
+    hidden_grad, third_after, *down_rest = hold(hidden_grad, third_after, *down_rest)
 
     back = lax.dot_general(
         hidden_grad, w_up[0], (((1,), (1,)), ((), ())), preferred_element_type=jnp.float32
     ).astype(jnp.bfloat16)
-    returned = to_previous(exchange(back, "expert"))
-
     term_up = lax.dot_general(
         hidden_grad, saved_in[0, 0], (((0,), (0,)), ((), ())), preferred_element_type=jnp.float32
     ).astype(jnp.bfloat16)
-    up = sum_over_groups(term_up)
+    returned = exchange(back, "expert")
+    up_blocks = along_z(term_up, [0] + short)
+    returned, term_up, *up_blocks = hold(returned, term_up, *up_blocks)
+    returned = to_previous(returned)
+    up_rest = along_z(term_up, long)
+    returned, *up_rest = hold(returned, *up_rest)
+    down, up = across_x([add_up(down_blocks + down_rest), add_up(up_blocks + up_rest)])
 
     unpacked = (
         returned.reshape(experts, split, slots_per, quarter)
         .transpose(0, 2, 1, 3)
         .reshape(all_slots, width)
     )
-    target_after = slot_targets(chosen_after, experts, slots_per)
     hit_after = [target_after[:, k][:, None] == slot_ids[None, :] for k in range(2)]
     place_after = (hit_after[0] | hit_after[1]).astype(jnp.bfloat16)
+    grads_after = jnp.concatenate([first_after, second_after, third_after], axis=0)
     total = grads_after.astype(jnp.float32) + jnp.dot(
         place_after, unpacked, preferred_element_type=jnp.float32
     )

time: 208 us -> 181 us (0.87)
  the two profiles are of different devices: /device:TPU:1 before, /device:TPU:11 now
where the time goes in v3:
time: 181 us; the launch traced here: 180 us
  starting transfers between devices  102 us (56%)
  waiting for transfers between devices  54.8 us (30%)
  local copies, waits for them, and re-layouts  10.7 us (6%)
  matrix products  6.71 us (4%)
  other arithmetic  4.36 us (2%)
    ppermute x14, starting transfers between devices, along_z(): block = lax.ppermute(block, 'dp', pairs)  61 us
    ppermute x14, waiting for transfers between devices, along_z(): block = lax.ppermute(block, 'dp', pairs)  31.5 us
    all_to_all x4, starting transfers between devices, exchange(): return lax.all_to_all(x, axis, 0, 0, tiled=True, axis_index_groups=groups)  28.3 us
    ppermute x5, starting transfers between devices, to_previous(): return lax.ppermute(x, 'phase', [(i, i - 1) for i in range(1, peers)])  10.7 us
    ppermute x1, waiting for transfers between devices, across_x(): lax.ppermute(away, 'dp', [(i, (i + near) % count) for i in range(count)])  8.18 us
    ppermute x5, waiting for transfers between devices, to_previous(): return lax.ppermute(x, 'phase', [(i, i - 1) for i in range(1, peers)])  7.99 us
    all_to_all x4, waiting for transfers between devices, exchange(): return lax.all_to_all(x, axis, 0, 0, tiled=True, axis_index_groups=groups)  7.15 us
  transfers between devices with their start and end apart: 24, of which 12 were waited for; matrix products, arithmetic and copies ran while one was open for 5% of the time, Pallas kernels for 0%

profile of v3, /device:TPU:11, one launch (start us, length us, event | category | flops | bytes accessed | tf_op | source)
XLA Modules:
  0.0 180.1 jit_solution(4761410303148581977)
XLA Ops:
  0.7 0.9 copy.19
  1.9 0.8 slice_bitcast_fusion.4
  4.1 1.1 slice_bitcast_fusion
  5.7 0.8 copy.22
  6.5 8.2 %all-to-all-start = ((bf16[16,16,640]{2,1,0:T(8,128)(2,1)}), bf16[16,16,640]{2,1,0:T(8,128)(2,1)S(1)}, u32[]{:S(2)}, u32[]{:S(2)}) async-start(bf16[16,16,640]{2,1,0:T(8,128)(2,1)} %bitcast.9), calls=%async_computation | async-start | bytes 655360 | tf_op jit(solution)/shard_map/all_to_all | solution.py:15
  14.7 3.1 %collective-permute-start.1 = (s32[128,2]{1,0:T(8,128)S(1)}, s32[128,2]{1,0:T(8,128)S(1)}, u32[]{:S(2)}, u32[]{:S(2)}) collective-permute-start(s32[128,2]{1,0:T(8,128)S(1)} %bitcast_add_fusion.1), channel_id=1, source_target_pairs={{256,0},{512,256},{768,512},{257,1},{513,257},{769,513},{258,2},{5... | collective-permute-start | bytes 3080 | tf_op jit(solution)/shard_map/ppermute | solution.py:20
  17.8 1.9 %collective-permute-start = (bf16[64,5120]{1,0:T(8,128)(2,1)S(1)}, bf16[64,5120]{1,0:T(8,128)(2,1)}, u32[]{:S(2)}, u32[]{:S(2)}) collective-permute-start(bf16[64,5120]{1,0:T(8,128)(2,1)S(1)} %slice_bitcast_fusion), channel_id=1, source_target_pairs={{256,0},{512,256},{768,512},{257,1},{513,257},{769,513},{258,2},{5... | collective-permute-start | bytes 1966088 | tf_op jit(solution)/shard_map/ppermute | solution.py:20
  19.7 0.9 slice_bitcast_fusion.1
  20.6 7.1 %all-to-all-done = bf16[16,16,640]{2,1,0:T(8,128)(2,1)S(1)} async-done(((bf16[16,16,640]{2,1,0:T(8,128)(2,1)}), bf16[16,16,640]{2,1,0:T(8,128)(2,1)S(1)}, u32[]{:S(2)}, u32[]{:S(2)}) %all-to-all-start) | async-done | bytes 327712 | tf_op jit(solution)/shard_map/all_to_all | solution.py:15
  27.8 8.0 %collective-permute-done = bf16[64,5120]{1,0:T(8,128)(2,1)} collective-permute-done((bf16[64,5120]{1,0:T(8,128)(2,1)S(1)}, bf16[64,5120]{1,0:T(8,128)(2,1)}, u32[]{:S(2)}, u32[]{:S(2)}) %collective-permute-start) | collective-permute-done | bytes 655392 | tf_op jit(solution)/shard_map/ppermute | solution.py:20
  35.8 1.3 convolution_convert_fusion.2
  37.1 5.9 %all-to-all-start.1 = ((bf16[8,32,768]{2,1,0:T(8,128)(2,1)}), bf16[8,32,768]{2,1,0:T(8,128)(2,1)S(1)}, u32[]{:S(2)}, u32[]{:S(2)}) async-start(bf16[8,32,768]{2,1,0:T(8,128)(2,1)} %bitcast.13), calls=%async_computation.1 | async-start | bytes 786432 | tf_op jit(solution)/shard_map/all_to_all | solution.py:15
  43.0 1.9 %collective-permute-start.2 = (bf16[32,5120]{1,0:T(8,128)(2,1)S(1)}, bf16[32,5120]{1,0:T(8,128)(2,1)S(1)}, u32[]{:S(2)}, u32[]{:S(2)}) collective-permute-start(bf16[32,5120]{1,0:T(8,128)(2,1)S(1)} %copy-done.5), channel_id=1, source_target_pairs={{256,0},{512,256},{768,512},{257,1},{513,257},{769,513},{258,2},{5... | collective-permute-start | bytes 983048 | tf_op jit(solution)/shard_map/ppermute | solution.py:20
  45.5 0.9 copy-done.2
  46.5 7.8 %collective-permute-start.5 = (bf16[96,640]{1,0:T(8,128)(2,1)S(1)}, bf16[96,640]{1,0:T(8,128)(2,1)S(1)}, u32[]{:S(2)}, u32[]{:S(2)}) collective-permute-start(bf16[96,640]{1,0:T(8,128)(2,1)S(1)} %bitcast.138), channel_id=1, source_target_pairs={{0,32},{16,48},{32,64},{48,80},{64,96},{80,112},{96,0},{112,16},{1... | collective-permute-start | bytes 368648 | tf_op jit(solution)/shard_map/ppermute | solution.py:46
  54.3 10.4 %collective-permute-start.6 = (bf16[96,640]{1,0:T(8,128)(2,1)S(1)}, bf16[96,640]{1,0:T(8,128)(2,1)S(1)}, u32[]{:S(2)}, u32[]{:S(2)}) collective-permute-start(bf16[96,640]{1,0:T(8,128)(2,1)S(1)} %bitcast.137), channel_id=1, source_target_pairs={{0,96},{16,112},{32,0},{48,16},{64,32},{80,48},{96,64},{112,80},{1... | collective-permute-start | bytes 368648 | tf_op jit(solution)/shard_map/ppermute | solution.py:46
  64.7 5.2 %collective-permute-start.4 = (bf16[96,640]{1,0:T(8,128)(2,1)S(1)}, bf16[96,640]{1,0:T(8,128)(2,1)S(1)}, u32[]{:S(2)}, u32[]{:S(2)}) collective-permute-start(bf16[96,640]{1,0:T(8,128)(2,1)S(1)} %bitcast.136), channel_id=1, source_target_pairs={{0,112},{16,0},{32,16},{48,32},{64,48},{80,64},{96,80},{112,96},{1... | collective-permute-start | bytes 368648 | tf_op jit(solution)/shard_map/ppermute | solution.py:46
  69.9 1.9 %collective-permute-start.3 = (bf16[96,640]{1,0:T(8,128)(2,1)S(1)}, bf16[96,640]{1,0:T(8,128)(2,1)S(1)}, u32[]{:S(2)}, u32[]{:S(2)}) collective-permute-start(bf16[96,640]{1,0:T(8,128)(2,1)S(1)} %bitcast.135), channel_id=1, source_target_pairs={{0,16},{16,32},{32,48},{48,64},{64,80},{80,96},{96,112},{112,0},{1... | collective-permute-start | bytes 368648 | tf_op jit(solution)/shard_map/ppermute | solution.py:46
  71.9 1.9 %collective-permute-done.4 = bf16[96,640]{1,0:T(8,128)(2,1)S(1)} collective-permute-done((bf16[96,640]{1,0:T(8,128)(2,1)S(1)}, bf16[96,640]{1,0:T(8,128)(2,1)S(1)}, u32[]{:S(2)}, u32[]{:S(2)}) %collective-permute-start.4) | collective-permute-done | bytes 122912 | tf_op jit(solution)/shard_map/ppermute | solution.py:46
  73.8 2.9 %collective-permute-done.3 = bf16[96,640]{1,0:T(8,128)(2,1)S(1)} collective-permute-done((bf16[96,640]{1,0:T(8,128)(2,1)S(1)}, bf16[96,640]{1,0:T(8,128)(2,1)S(1)}, u32[]{:S(2)}, u32[]{:S(2)}) %collective-permute-start.3) | collective-permute-done | bytes 122912 | tf_op jit(solution)/shard_map/ppermute | solution.py:46
  77.4 0.9 fusion.26
  78.3 0.8 tile.2
  79.1 7.4 %all-to-all-start.2 = ((bf16[8,32,768]{2,1,0:T(8,128)(2,1)}), bf16[8,32,768]{2,1,0:T(8,128)(2,1)S(1)}, u32[]{:S(2)}, u32[]{:S(2)}) async-start(bf16[8,32,768]{2,1,0:T(8,128)(2,1)} %tile.2), calls=%async_computation.2 | async-start | bytes 786432 | tf_op jit(solution)/shard_map/all_to_all | solution.py:15
  86.5 1.9 %collective-permute-start.7 = (bf16[32,5120]{1,0:T(8,128)(2,1)S(1)}, bf16[32,5120]{1,0:T(8,128)(2,1)}, u32[]{:S(2)}, u32[]{:S(2)}) collective-permute-start(bf16[32,5120]{1,0:T(8,128)(2,1)S(1)} %copy-done.4), channel_id=1, source_target_pairs={{256,0},{512,256},{768,512},{257,1},{513,257},{769,513},{258,2},{5... | collective-permute-start | bytes 983048 | tf_op jit(solution)/shard_map/ppermute | solution.py:20
  88.5 1.1 constant_dynamic-slice_fusion.8
  89.6 2.1 %collective-permute-start.9 = (bf16[96,640]{1,0:T(8,128)(2,1)S(1)}, bf16[96,640]{1,0:T(8,128)(2,1)S(1)}, u32[]{:S(2)}, u32[]{:S(2)}) collective-permute-start(bf16[96,640]{1,0:T(8,128)(2,1)S(1)} %bitcast.134), channel_id=1, source_target_pairs={{0,80},{16,96},{32,112},{48,0},{64,16},{80,32},{96,48},{112,64},{1... | collective-permute-start | bytes 368648 | tf_op jit(solution)/shard_map/ppermute | solution.py:46
  91.6 4.6 %collective-permute-start.10 = (bf16[96,640]{1,0:T(8,128)(2,1)S(1)}, bf16[96,640]{1,0:T(8,128)(2,1)}, u32[]{:S(2)}, u32[]{:S(2)}) collective-permute-start(bf16[96,640]{1,0:T(8,128)(2,1)S(1)} %bitcast.133), channel_id=1, source_target_pairs={{0,64},{16,80},{32,96},{48,112},{64,0},{80,16},{96,32},{112,48},{1... | collective-permute-start | bytes 368648 | tf_op jit(solution)/shard_map/ppermute | solution.py:46
  96.3 2.5 %collective-permute-start.8 = (bf16[96,640]{1,0:T(8,128)(2,1)S(1)}, bf16[96,640]{1,0:T(8,128)(2,1)}, u32[]{:S(2)}, u32[]{:S(2)}) collective-permute-start(bf16[96,640]{1,0:T(8,128)(2,1)S(1)} %bitcast.132), channel_id=1, source_target_pairs={{0,48},{16,64},{32,80},{48,96},{64,112},{80,0},{96,16},{112,32},{1... | collective-permute-start | bytes 368648 | tf_op jit(solution)/shard_map/ppermute | solution.py:46
  98.7 1.7 collective-permute-done.9
  100.5 7.9 %collective-permute-done.10 = bf16[96,640]{1,0:T(8,128)(2,1)} collective-permute-done((bf16[96,640]{1,0:T(8,128)(2,1)S(1)}, bf16[96,640]{1,0:T(8,128)(2,1)}, u32[]{:S(2)}, u32[]{:S(2)}) %collective-permute-start.10) | collective-permute-done | bytes 122912 | tf_op jit(solution)/shard_map/ppermute | solution.py:46
  108.4 1.2 convolution_convert_fusion.3
  109.6 6.8 %all-to-all-start.3 = ((bf16[16,16,640]{2,1,0:T(8,128)(2,1)}), bf16[16,16,640]{2,1,0:T(8,128)(2,1)S(1)}, u32[]{:S(2)}, u32[]{:S(2)}) async-start(bf16[16,16,640]{2,1,0:T(8,128)(2,1)} %bitcast.33), calls=%async_computation.3 | async-start | bytes 655360 | tf_op jit(solution)/shard_map/all_to_all | solution.py:15
  117.0 0.8 constant_dynamic-slice_fusion.3
  117.8 7.8 %collective-permute-start.13 = (bf16[96,640]{1,0:T(8,128)(2,1)}, bf16[96,640]{1,0:T(8,128)(2,1)S(1)}, u32[]{:S(2)}, u32[]{:S(2)}) collective-permute-start(bf16[96,640]{1,0:T(8,128)(2,1)} %bitcast.40), channel_id=1, source_target_pairs={{0,32},{16,48},{32,64},{48,80},{64,96},{80,112},{96,0},{112,16},{1... | collective-permute-start | bytes 368648 | tf_op jit(solution)/shard_map/ppermute | solution.py:46
  125.6 1.9 %collective-permute-start.14 = (bf16[96,640]{1,0:T(8,128)(2,1)}, bf16[96,640]{1,0:T(8,128)(2,1)S(1)}, u32[]{:S(2)}, u32[]{:S(2)}) collective-permute-start(bf16[96,640]{1,0:T(8,128)(2,1)} %bitcast.41), channel_id=1, source_target_pairs={{0,96},{16,112},{32,0},{48,16},{64,32},{80,48},{96,64},{112,80},{1... | collective-permute-start | bytes 368648 | tf_op jit(solution)/shard_map/ppermute | solution.py:46
  127.5 3.1 %collective-permute-start.12 = (bf16[96,640]{1,0:T(8,128)(2,1)}, bf16[96,640]{1,0:T(8,128)(2,1)}, u32[]{:S(2)}, u32[]{:S(2)}) collective-permute-start(bf16[96,640]{1,0:T(8,128)(2,1)} %bitcast.39), channel_id=1, source_target_pairs={{0,112},{16,0},{32,16},{48,32},{64,48},{80,64},{96,80},{112,96},{1... | collective-permute-start | bytes 368648 | tf_op jit(solution)/shard_map/ppermute | solution.py:46
  130.6 2.2 %collective-permute-start.11 = (bf16[96,640]{1,0:T(8,128)(2,1)}, bf16[96,640]{1,0:T(8,128)(2,1)}, u32[]{:S(2)}, u32[]{:S(2)}) collective-permute-start(bf16[96,640]{1,0:T(8,128)(2,1)} %bitcast.38), channel_id=1, source_target_pairs={{0,16},{16,32},{32,48},{48,64},{64,80},{80,96},{96,112},{112,0},{1... | collective-permute-start | bytes 368648 | tf_op jit(solution)/shard_map/ppermute | solution.py:46
  133.2 4.0 %collective-permute-done.12 = bf16[96,640]{1,0:T(8,128)(2,1)} collective-permute-done((bf16[96,640]{1,0:T(8,128)(2,1)}, bf16[96,640]{1,0:T(8,128)(2,1)}, u32[]{:S(2)}, u32[]{:S(2)}) %collective-permute-start.12) | collective-permute-done | bytes 122912 | tf_op jit(solution)/shard_map/ppermute | solution.py:46
  137.7 1.9 %collective-permute-start.15 = (bf16[256,640]{1,0:T(8,128)(2,1)S(1)}, bf16[256,640]{1,0:T(8,128)(2,1)S(1)}, u32[]{:S(2)}, u32[]{:S(2)}) collective-permute-start(bf16[256,640]{1,0:T(8,128)(2,1)S(1)} %bitcast.126), channel_id=1, source_target_pairs={{256,0},{512,256},{768,512},{257,1},{513,257},{769,513},{258,2},{5... | collective-permute-start | bytes 983048 | tf_op jit(solution)/shard_map/ppermute | solution.py:20
  139.7 3.6 %collective-permute-start.17 = (bf16[96,640]{1,0:T(8,128)(2,1)S(1)}, bf16[96,640]{1,0:T(8,128)(2,1)S(1)}, u32[]{:S(2)}, u32[]{:S(2)}) collective-permute-start(bf16[96,640]{1,0:T(8,128)(2,1)S(1)} %bitcast.131), channel_id=1, source_target_pairs={{0,80},{16,96},{32,112},{48,0},{64,16},{80,32},{96,48},{112,64},{1... | collective-permute-start | bytes 368648 | tf_op jit(solution)/shard_map/ppermute | solution.py:46
  143.3 4.0 %collective-permute-start.18 = (bf16[96,640]{1,0:T(8,128)(2,1)S(1)}, bf16[96,640]{1,0:T(8,128)(2,1)S(1)}, u32[]{:S(2)}, u32[]{:S(2)}) collective-permute-start(bf16[96,640]{1,0:T(8,128)(2,1)S(1)} %bitcast.130), channel_id=1, source_target_pairs={{0,64},{16,80},{32,96},{48,112},{64,0},{80,16},{96,32},{112,48},{1... | collective-permute-start | bytes 368648 | tf_op jit(solution)/shard_map/ppermute | solution.py:46
  147.4 4.1 %collective-permute-start.16 = (bf16[96,640]{1,0:T(8,128)(2,1)S(1)}, bf16[96,640]{1,0:T(8,128)(2,1)S(1)}, u32[]{:S(2)}, u32[]{:S(2)}) collective-permute-start(bf16[96,640]{1,0:T(8,128)(2,1)S(1)} %bitcast.129), channel_id=1, source_target_pairs={{0,48},{16,64},{32,80},{48,96},{64,112},{80,0},{96,16},{112,32},{1... | collective-permute-start | bytes 368648 | tf_op jit(solution)/shard_map/ppermute | solution.py:46
  151.5 1.1 convert_add_fusion.1
  153.0 12.0 %collective-permute-done.16 = bf16[96,640]{1,0:T(8,128)(2,1)S(1)} collective-permute-done((bf16[96,640]{1,0:T(8,128)(2,1)S(1)}, bf16[96,640]{1,0:T(8,128)(2,1)S(1)}, u32[]{:S(2)}, u32[]{:S(2)}) %collective-permute-start.16) | collective-permute-done | bytes 122912 | tf_op jit(solution)/shard_map/ppermute | solution.py:46
  165.1 1.1 convert_add_fusion
  166.3 2.1 %collective-permute-start.19 = (bf16[2,48,640]{2,1,0:T(8,128)(2,1)S(1)}, bf16[2,48,640]{2,1,0:T(8,128)(2,1)S(1)}, u32[]{:S(2)}, u32[]{:S(2)}) collective-permute-start(bf16[2,48,640]{2,1,0:T(8,128)(2,1)S(1)} %fusion.18), channel_id=1, source_target_pairs={{0,128},{16,144},{32,160},{48,176},{64,192},{80,208},{96,224},{112... | collective-permute-start | bytes 368648 | tf_op jit(solution)/shard_map/ppermute | solution.py:65
  168.4 2.8 %fusion.1 = bf16[1,128,5120]{2,1,0:T(8,128)(2,1)} fusion(bf16[32,5120]{1,0:T(8,128)(2,1)S(1)} %bitcast.128, bf16[32,5120]{1,0:T(8,128)(2,1)} %collective-permute-done.7, bf16[32,5120]{1,0:T(8,128)(2,1)S(1)} %copy-done.23, bf16[64,5120]{1,0:T(8,128)(2,1)} %collective-permute-done, s32[128]{0:T(128)S(1)} %get-tuple-element.72, s32[128]{0:T(128)S(1)} %get-tuple-element.71), kind=kOutput, calls=%fused_computation.2 | convolution fusion | flops 47198208 | bytes 2950144 | tf_op jit(solution)/shard_map/dot_general | solution.py:162
  171.2 8.2 %collective-permute-done.19 = bf16[2,48,640]{2,1,0:T(8,128)(2,1)S(1)} collective-permute-done((bf16[2,48,640]{2,1,0:T(8,128)(2,1)S(1)}, bf16[2,48,640]{2,1,0:T(8,128)(2,1)S(1)}, u32[]{:S(2)}, u32[]{:S(2)}) %collective-permute-start.19) | collective-permute-done | bytes 122912 | tf_op jit(solution)/shard_map/ppermute | solution.py:65
  (87 shorter events, 6.2 us)
Async XLA Ops:
  0.6 35.1 %copy-start = (bf16[1,768,640]{2,1,0:T(8,128)(2,1)S(1)}, bf16[1,768,640]{2,1,0:T(8,128)(2,1)}, u32[]{:S(2)}) copy-start(bf16[1,768,640]{2,1,0:T(8,128)(2,1)} %param.13) | copy-start | bytes 2949124
  0.6 4.7 %copy-start.1 = (bf16[1,128,5120]{2,1,0:T(8,128)(2,1)S(1)}, bf16[1,128,5120]{2,1,0:T(8,128)(2,1)}, u32[]{:S(2)}) copy-start(bf16[1,128,5120]{2,1,0:T(8,128)(2,1)} %param.7) | copy-start | bytes 3932164
  6.5 21.3 %all-to-all-start = ((bf16[16,16,640]{2,1,0:T(8,128)(2,1)}), bf16[16,16,640]{2,1,0:T(8,128)(2,1)S(1)}, u32[]{:S(2)}, u32[]{:S(2)}) async-start(bf16[16,16,640]{2,1,0:T(8,128)(2,1)} %bitcast.9), calls=%async_computation | async-start | bytes 655360 | tf_op jit(solution)/shard_map/all_to_all | solution.py:15
  14.7 5.9 %collective-permute-start.1 = (s32[128,2]{1,0:T(8,128)S(1)}, s32[128,2]{1,0:T(8,128)S(1)}, u32[]{:S(2)}, u32[]{:S(2)}) collective-permute-start(s32[128,2]{1,0:T(8,128)S(1)} %bitcast_add_fusion.1), channel_id=1, source_target_pairs={{256,0},{512,256},{768,512},{257,1},{513,257},{769,513},{258,2},{5... | collective-permute-start | bytes 3080 | tf_op jit(solution)/shard_map/ppermute | solution.py:20
  17.8 18.0 %collective-permute-start = (bf16[64,5120]{1,0:T(8,128)(2,1)S(1)}, bf16[64,5120]{1,0:T(8,128)(2,1)}, u32[]{:S(2)}, u32[]{:S(2)}) collective-permute-start(bf16[64,5120]{1,0:T(8,128)(2,1)S(1)} %slice_bitcast_fusion), channel_id=1, source_target_pairs={{256,0},{512,256},{768,512},{257,1},{513,257},{769,513},{258,2},{5... | collective-permute-start | bytes 1966088 | tf_op jit(solution)/shard_map/ppermute | solution.py:20
  35.8 7.2 %copy-start.5 = (bf16[32,5120]{1,0:T(8,128)(2,1)S(1)}, bf16[32,5120]{1,0:T(8,128)(2,1)}, u32[]{:S(2)}) copy-start(bf16[32,5120]{1,0:T(8,128)(2,1)} %get-tuple-element.43) | copy-start | bytes 983044
  35.8 9.1 %copy-start.21 = (bf16[1,1,1,256,768]{4,3,2,1,0:T(8,128)(2,1)S(1)}, bf16[1,1,1,256,768]{4,3,2,1,0:T(8,128)(2,1)}, u32[]{:S(2)}) copy-start(bf16[1,1,1,256,768]{4,3,2,1,0:T(8,128)(2,1)} %param.11) | copy-start | bytes 1179652
  37.1 39.7 %all-to-all-start.1 = ((bf16[8,32,768]{2,1,0:T(8,128)(2,1)}), bf16[8,32,768]{2,1,0:T(8,128)(2,1)S(1)}, u32[]{:S(2)}, u32[]{:S(2)}) async-start(bf16[8,32,768]{2,1,0:T(8,128)(2,1)} %bitcast.13), calls=%async_computation.1 | async-start | bytes 786432 | tf_op jit(solution)/shard_map/all_to_all | solution.py:15
  43.0 33.7 %collective-permute-start.2 = (bf16[32,5120]{1,0:T(8,128)(2,1)S(1)}, bf16[32,5120]{1,0:T(8,128)(2,1)S(1)}, u32[]{:S(2)}, u32[]{:S(2)}) collective-permute-start(bf16[32,5120]{1,0:T(8,128)(2,1)S(1)} %copy-done.5), channel_id=1, source_target_pairs={{256,0},{512,256},{768,512},{257,1},{513,257},{769,513},{258,2},{5... | collective-permute-start | bytes 983048 | tf_op jit(solution)/shard_map/ppermute | solution.py:20
  45.5 0.9 copy-start.2
  46.4 40.1 %copy-start.4 = (bf16[32,5120]{1,0:T(8,128)(2,1)S(1)}, bf16[32,5120]{1,0:T(8,128)(2,1)}, u32[]{:S(2)}) copy-start(bf16[32,5120]{1,0:T(8,128)(2,1)} %get-tuple-element.47) | copy-start | bytes 983044
  46.5 25.3 %collective-permute-start.5 = (bf16[96,640]{1,0:T(8,128)(2,1)S(1)}, bf16[96,640]{1,0:T(8,128)(2,1)S(1)}, u32[]{:S(2)}, u32[]{:S(2)}) collective-permute-start(bf16[96,640]{1,0:T(8,128)(2,1)S(1)} %bitcast.138), channel_id=1, source_target_pairs={{0,32},{16,48},{32,64},{48,80},{64,96},{80,112},{96,0},{112,16},{1... | collective-permute-start | bytes 368648 | tf_op jit(solution)/shard_map/ppermute | solution.py:46
  54.3 17.6 %collective-permute-start.6 = (bf16[96,640]{1,0:T(8,128)(2,1)S(1)}, bf16[96,640]{1,0:T(8,128)(2,1)S(1)}, u32[]{:S(2)}, u32[]{:S(2)}) collective-permute-start(bf16[96,640]{1,0:T(8,128)(2,1)S(1)} %bitcast.137), channel_id=1, source_target_pairs={{0,96},{16,112},{32,0},{48,16},{64,32},{80,48},{96,64},{112,80},{1... | collective-permute-start | bytes 368648 | tf_op jit(solution)/shard_map/ppermute | solution.py:46
  64.7 9.1 %collective-permute-start.4 = (bf16[96,640]{1,0:T(8,128)(2,1)S(1)}, bf16[96,640]{1,0:T(8,128)(2,1)S(1)}, u32[]{:S(2)}, u32[]{:S(2)}) collective-permute-start(bf16[96,640]{1,0:T(8,128)(2,1)S(1)} %bitcast.136), channel_id=1, source_target_pairs={{0,112},{16,0},{32,16},{48,32},{64,48},{80,64},{96,80},{112,96},{1... | collective-permute-start | bytes 368648 | tf_op jit(solution)/shard_map/ppermute | solution.py:46
  69.9 6.8 %collective-permute-start.3 = (bf16[96,640]{1,0:T(8,128)(2,1)S(1)}, bf16[96,640]{1,0:T(8,128)(2,1)S(1)}, u32[]{:S(2)}, u32[]{:S(2)}) collective-permute-start(bf16[96,640]{1,0:T(8,128)(2,1)S(1)} %bitcast.135), channel_id=1, source_target_pairs={{0,16},{16,32},{32,48},{48,64},{64,80},{80,96},{96,112},{112,0},{1... | collective-permute-start | bytes 368648 | tf_op jit(solution)/shard_map/ppermute | solution.py:46
  71.8 4.9 %copy-start.7 = (bf16[96,640]{1,0:T(8,128)(2,1)}, bf16[96,640]{1,0:T(8,128)(2,1)S(1)}, u32[]{:S(2)}) copy-start(bf16[96,640]{1,0:T(8,128)(2,1)S(1)} %collective-permute-done.5) | copy-start | bytes 368644
  71.8 4.9 %copy-start.9 = (bf16[96,640]{1,0:T(8,128)(2,1)}, bf16[96,640]{1,0:T(8,128)(2,1)S(1)}, u32[]{:S(2)}) copy-start(bf16[96,640]{1,0:T(8,128)(2,1)S(1)} %collective-permute-done.6) | copy-start | bytes 368644
  73.8 3.0 %copy-start.11 = (bf16[96,640]{1,0:T(8,128)(2,1)}, bf16[96,640]{1,0:T(8,128)(2,1)S(1)}, u32[]{:S(2)}) copy-start(bf16[96,640]{1,0:T(8,128)(2,1)S(1)} %collective-permute-done.4) | copy-start | bytes 368644
  76.7 0.6 copy-start.13
  76.7 11.8 %copy-start.22 = (bf16[32,5120]{1,0:T(8,128)(2,1)}, bf16[32,5120]{1,0:T(8,128)(2,1)S(1)}, u32[]{:S(2)}) copy-start(bf16[32,5120]{1,0:T(8,128)(2,1)S(1)} %collective-permute-done.2) | copy-start | bytes 983044
  77.3 31.0 %copy-start.3 = (bf16[1,640,768]{2,1,0:T(8,128)(2,1)S(1)}, bf16[1,640,768]{2,1,0:T(8,128)(2,1)}, u32[]{:S(2)}) copy-start(bf16[1,640,768]{2,1,0:T(8,128)(2,1)} %param.12) | copy-start | bytes 2949124
  79.1 29.2 %all-to-all-start.2 = ((bf16[8,32,768]{2,1,0:T(8,128)(2,1)}), bf16[8,32,768]{2,1,0:T(8,128)(2,1)S(1)}, u32[]{:S(2)}, u32[]{:S(2)}) async-start(bf16[8,32,768]{2,1,0:T(8,128)(2,1)} %tile.2), calls=%async_computation.2 | async-start | bytes 786432 | tf_op jit(solution)/shard_map/all_to_all | solution.py:15
  86.5 21.8 %collective-permute-start.7 = (bf16[32,5120]{1,0:T(8,128)(2,1)S(1)}, bf16[32,5120]{1,0:T(8,128)(2,1)}, u32[]{:S(2)}, u32[]{:S(2)}) collective-permute-start(bf16[32,5120]{1,0:T(8,128)(2,1)S(1)} %copy-done.4), channel_id=1, source_target_pairs={{256,0},{512,256},{768,512},{257,1},{513,257},{769,513},{258,2},{5... | collective-permute-start | bytes 983048 | tf_op jit(solution)/shard_map/ppermute | solution.py:20
  89.6 26.9 %copy-start.6 = (bf16[1,1,256,640]{3,2,1,0:T(8,128)(2,1)S(1)}, bf16[1,1,256,640]{3,2,1,0:T(8,128)(2,1)}, u32[]{:S(2)}) copy-start(bf16[1,1,256,640]{3,2,1,0:T(8,128)(2,1)} %param.10) | copy-start | bytes 983044
  89.6 10.9 %collective-permute-start.9 = (bf16[96,640]{1,0:T(8,128)(2,1)S(1)}, bf16[96,640]{1,0:T(8,128)(2,1)S(1)}, u32[]{:S(2)}, u32[]{:S(2)}) collective-permute-start(bf16[96,640]{1,0:T(8,128)(2,1)S(1)} %bitcast.134), channel_id=1, source_target_pairs={{0,80},{16,96},{32,112},{48,0},{64,16},{80,32},{96,48},{112,64},{1... | collective-permute-start | bytes 368648 | tf_op jit(solution)/shard_map/ppermute | solution.py:46
  91.6 16.7 %collective-permute-start.10 = (bf16[96,640]{1,0:T(8,128)(2,1)S(1)}, bf16[96,640]{1,0:T(8,128)(2,1)}, u32[]{:S(2)}, u32[]{:S(2)}) collective-permute-start(bf16[96,640]{1,0:T(8,128)(2,1)S(1)} %bitcast.133), channel_id=1, source_target_pairs={{0,64},{16,80},{32,96},{48,112},{64,0},{80,16},{96,32},{112,48},{1... | collective-permute-start | bytes 368648 | tf_op jit(solution)/shard_map/ppermute | solution.py:46
  96.3 12.1 %collective-permute-start.8 = (bf16[96,640]{1,0:T(8,128)(2,1)S(1)}, bf16[96,640]{1,0:T(8,128)(2,1)}, u32[]{:S(2)}, u32[]{:S(2)}) collective-permute-start(bf16[96,640]{1,0:T(8,128)(2,1)S(1)} %bitcast.132), channel_id=1, source_target_pairs={{0,48},{16,64},{32,80},{48,96},{64,112},{80,0},{96,16},{112,32},{1... | collective-permute-start | bytes 368648 | tf_op jit(solution)/shard_map/ppermute | solution.py:46
  100.5 7.9 %copy-start.15 = (bf16[96,640]{1,0:T(8,128)(2,1)}, bf16[96,640]{1,0:T(8,128)(2,1)S(1)}, u32[]{:S(2)}) copy-start(bf16[96,640]{1,0:T(8,128)(2,1)S(1)} %collective-permute-done.9) | copy-start | bytes 368644
  109.6 28.1 %all-to-all-start.3 = ((bf16[16,16,640]{2,1,0:T(8,128)(2,1)}), bf16[16,16,640]{2,1,0:T(8,128)(2,1)S(1)}, u32[]{:S(2)}, u32[]{:S(2)}) async-start(bf16[16,16,640]{2,1,0:T(8,128)(2,1)} %bitcast.33), calls=%async_computation.3 | async-start | bytes 655360 | tf_op jit(solution)/shard_map/all_to_all | solution.py:15
  116.9 34.5 %copy-start.8 = (bf16[96,640]{1,0:T(8,128)(2,1)S(1)}, bf16[96,640]{1,0:T(8,128)(2,1)}, u32[]{:S(2)}) copy-start(bf16[96,640]{1,0:T(8,128)(2,1)} %copy-done.7) | copy-start | bytes 368644
  116.9 34.5 %copy-start.10 = (bf16[96,640]{1,0:T(8,128)(2,1)S(1)}, bf16[96,640]{1,0:T(8,128)(2,1)}, u32[]{:S(2)}) copy-start(bf16[96,640]{1,0:T(8,128)(2,1)} %copy-done.9) | copy-start | bytes 368644
  117.0 34.5 %copy-start.12 = (bf16[96,640]{1,0:T(8,128)(2,1)S(1)}, bf16[96,640]{1,0:T(8,128)(2,1)}, u32[]{:S(2)}) copy-start(bf16[96,640]{1,0:T(8,128)(2,1)} %copy-done.11) | copy-start | bytes 368644
  117.0 34.5 %copy-start.14 = (bf16[96,640]{1,0:T(8,128)(2,1)S(1)}, bf16[96,640]{1,0:T(8,128)(2,1)}, u32[]{:S(2)}) copy-start(bf16[96,640]{1,0:T(8,128)(2,1)} %copy-done.13) | copy-start | bytes 368644
  117.0 34.5 %copy-start.16 = (bf16[96,640]{1,0:T(8,128)(2,1)S(1)}, bf16[96,640]{1,0:T(8,128)(2,1)}, u32[]{:S(2)}) copy-start(bf16[96,640]{1,0:T(8,128)(2,1)} %copy-done.15) | copy-start | bytes 368644
  117.8 15.2 %collective-permute-start.13 = (bf16[96,640]{1,0:T(8,128)(2,1)}, bf16[96,640]{1,0:T(8,128)(2,1)S(1)}, u32[]{:S(2)}, u32[]{:S(2)}) collective-permute-start(bf16[96,640]{1,0:T(8,128)(2,1)} %bitcast.40), channel_id=1, source_target_pairs={{0,32},{16,48},{32,64},{48,80},{64,96},{80,112},{96,0},{112,16},{1... | collective-permute-start | bytes 368648 | tf_op jit(solution)/shard_map/ppermute | solution.py:46
  125.6 7.6 %collective-permute-start.14 = (bf16[96,640]{1,0:T(8,128)(2,1)}, bf16[96,640]{1,0:T(8,128)(2,1)S(1)}, u32[]{:S(2)}, u32[]{:S(2)}) collective-permute-start(bf16[96,640]{1,0:T(8,128)(2,1)} %bitcast.41), channel_id=1, source_target_pairs={{0,96},{16,112},{32,0},{48,16},{64,32},{80,48},{96,64},{112,80},{1... | collective-permute-start | bytes 368648 | tf_op jit(solution)/shard_map/ppermute | solution.py:46
  127.5 9.6 %collective-permute-start.12 = (bf16[96,640]{1,0:T(8,128)(2,1)}, bf16[96,640]{1,0:T(8,128)(2,1)}, u32[]{:S(2)}, u32[]{:S(2)}) collective-permute-start(bf16[96,640]{1,0:T(8,128)(2,1)} %bitcast.39), channel_id=1, source_target_pairs={{0,112},{16,0},{32,16},{48,32},{64,48},{80,64},{96,80},{112,96},{1... | collective-permute-start | bytes 368648 | tf_op jit(solution)/shard_map/ppermute | solution.py:46
  130.6 7.2 %collective-permute-start.11 = (bf16[96,640]{1,0:T(8,128)(2,1)}, bf16[96,640]{1,0:T(8,128)(2,1)}, u32[]{:S(2)}, u32[]{:S(2)}) collective-permute-start(bf16[96,640]{1,0:T(8,128)(2,1)} %bitcast.38), channel_id=1, source_target_pairs={{0,16},{16,32},{32,48},{48,64},{64,80},{80,96},{96,112},{112,0},{1... | collective-permute-start | bytes 368648 | tf_op jit(solution)/shard_map/ppermute | solution.py:46
  133.0 14.3 %copy-start.17 = (bf16[96,640]{1,0:T(8,128)(2,1)}, bf16[96,640]{1,0:T(8,128)(2,1)S(1)}, u32[]{:S(2)}) copy-start(bf16[96,640]{1,0:T(8,128)(2,1)S(1)} %collective-permute-done.13) | copy-start | bytes 368644
  133.2 14.2 %copy-start.19 = (bf16[96,640]{1,0:T(8,128)(2,1)}, bf16[96,640]{1,0:T(8,128)(2,1)S(1)}, u32[]{:S(2)}) copy-start(bf16[96,640]{1,0:T(8,128)(2,1)S(1)} %collective-permute-done.14) | copy-start | bytes 368644
  137.7 27.2 %collective-permute-start.15 = (bf16[256,640]{1,0:T(8,128)(2,1)S(1)}, bf16[256,640]{1,0:T(8,128)(2,1)S(1)}, u32[]{:S(2)}, u32[]{:S(2)}) collective-permute-start(bf16[256,640]{1,0:T(8,128)(2,1)S(1)} %bitcast.126), channel_id=1, source_target_pairs={{256,0},{512,256},{768,512},{257,1},{513,257},{769,513},{258,2},{5... | collective-permute-start | bytes 983048 | tf_op jit(solution)/shard_map/ppermute | solution.py:20
  139.7 12.9 %collective-permute-start.17 = (bf16[96,640]{1,0:T(8,128)(2,1)S(1)}, bf16[96,640]{1,0:T(8,128)(2,1)S(1)}, u32[]{:S(2)}, u32[]{:S(2)}) collective-permute-start(bf16[96,640]{1,0:T(8,128)(2,1)S(1)} %bitcast.131), channel_id=1, source_target_pairs={{0,80},{16,96},{32,112},{48,0},{64,16},{80,32},{96,48},{112,64},{1... | collective-permute-start | bytes 368648 | tf_op jit(solution)/shard_map/ppermute | solution.py:46
  143.3 9.6 %collective-permute-start.18 = (bf16[96,640]{1,0:T(8,128)(2,1)S(1)}, bf16[96,640]{1,0:T(8,128)(2,1)S(1)}, u32[]{:S(2)}, u32[]{:S(2)}) collective-permute-start(bf16[96,640]{1,0:T(8,128)(2,1)S(1)} %bitcast.130), channel_id=1, source_target_pairs={{0,64},{16,80},{32,96},{48,112},{64,0},{80,16},{96,32},{112,48},{1... | collective-permute-start | bytes 368648 | tf_op jit(solution)/shard_map/ppermute | solution.py:46
  147.4 17.6 %collective-permute-start.16 = (bf16[96,640]{1,0:T(8,128)(2,1)S(1)}, bf16[96,640]{1,0:T(8,128)(2,1)S(1)}, u32[]{:S(2)}, u32[]{:S(2)}) collective-permute-start(bf16[96,640]{1,0:T(8,128)(2,1)S(1)} %bitcast.129), channel_id=1, source_target_pairs={{0,48},{16,64},{32,80},{48,96},{64,112},{80,0},{96,16},{112,32},{1... | collective-permute-start | bytes 368648 | tf_op jit(solution)/shard_map/ppermute | solution.py:46
  151.5 13.6 %copy-start.18 = (bf16[96,640]{1,0:T(8,128)(2,1)S(1)}, bf16[96,640]{1,0:T(8,128)(2,1)}, u32[]{:S(2)}) copy-start(bf16[96,640]{1,0:T(8,128)(2,1)} %copy-done.17) | copy-start | bytes 368644
  151.5 13.6 %copy-start.20 = (bf16[96,640]{1,0:T(8,128)(2,1)S(1)}, bf16[96,640]{1,0:T(8,128)(2,1)}, u32[]{:S(2)}) copy-start(bf16[96,640]{1,0:T(8,128)(2,1)} %copy-done.19) | copy-start | bytes 368644
  165.0 3.3 %copy-start.23 = (bf16[32,5120]{1,0:T(8,128)(2,1)S(1)}, bf16[32,5120]{1,0:T(8,128)(2,1)}, u32[]{:S(2)}) copy-start(bf16[32,5120]{1,0:T(8,128)(2,1)} %copy-done.22) | copy-start | bytes 983044
  166.3 13.1 %collective-permute-start.19 = (bf16[2,48,640]{2,1,0:T(8,128)(2,1)S(1)}, bf16[2,48,640]{2,1,0:T(8,128)(2,1)S(1)}, u32[]{:S(2)}, u32[]{:S(2)}) collective-permute-start(bf16[2,48,640]{2,1,0:T(8,128)(2,1)S(1)} %fusion.18), channel_id=1, source_target_pairs={{0,128},{16,144},{32,160},{48,176},{64,192},{80,208},{96,224},{112... | collective-permute-start | bytes 368648 | tf_op jit(solution)/shard_map/ppermute | solution.py:65

commit v4 on v1

--- a/solution.py
+++ b/solution.py
@@ -20,6 +20,15 @@
     return lax.ppermute(x, "phase", [(i, i - 1) for i in range(1, peers)])
 
 
+def partner(block, axis, bit):
+    count = lax.axis_size(axis)
+    return lax.ppermute(block, axis, [(i, i ^ (1 << bit)) for i in range(count)])
+
+
+def hold(*values):
+    return lax.optimization_barrier(values)
+
+
 def slot_targets(chosen, experts, slots_per):
     tokens = chosen.shape[0]
     flat = chosen.reshape(-1)
@@ -29,15 +38,49 @@
     return (flat * slots_per + slot).reshape(tokens, 2)
 
 
-def sum_over_groups(term):
+def exchange_pieces(term):
+    return exchange(term, "dp")
+
+
+def add_pieces(pieces):
     count = lax.axis_size("dp")
-    hid, quarter = term.shape
-    pieces = exchange(term, "dp").reshape(count, hid // count, quarter)
+    hid, quarter = pieces.shape
+    pieces = pieces.reshape(count, hid // count, quarter)
     return jnp.sum(pieces.astype(jnp.float32), axis=0).astype(jnp.bfloat16)
+
+
+def split_by(mine, lower, upper):
+    keep = jnp.where(mine == 1, upper, lower)
+    away = jnp.where(mine == 1, lower, upper)
+    return keep, away
+
+
+def gather_columns(buffer, levels, position):
+    size = buffer.shape[0]
+    rest = buffer.shape[1:]
+    for level in range(levels):
+        mine = position >> level & 1
+        shaped = buffer.reshape((size >> level + 1, 2, 1 << level) + rest)
+        keep, away = split_by(mine, shaped[:, 0], shaped[:, 1])
+        got = partner(away, "expert", level)
+        first = jnp.where(mine == 1, got, keep)
+        second = jnp.where(mine == 1, keep, got)
+        buffer = jnp.stack([first, second], axis=1).reshape((size,) + rest)
+    return buffer
+
+
+def behind(block, flip):
+    sections = lax.axis_size("phase")
+    count = lax.axis_size("expert")
+    pairs = [
+        (s * count + i, (s - 1) * count + (i ^ flip)) for s in range(1, sections) for i in range(count)
+    ]
+    return lax.ppermute(block, ("phase", "expert"), pairs)
 
 
 def body(grad_out, routes, gates, saved_in, saved_pre, w_up, w_down):
     count = lax.axis_size("expert")
+    position = lax.axis_index("expert")
     grads = grad_out[0]
     chosen = routes[0]
     weights = gates[0]
@@ -47,11 +90,9 @@
     experts = count // split
     slots_per = saved_in.shape[2] // count
     all_slots = experts * slots_per
-    members = [[e * split + q for q in range(split)] for e in range(experts)]
-    share = count * slots_per // split
-
-    grads_after = to_previous(grads)
-    chosen_after = to_previous(chosen)
+    levels = split.bit_length() - 1
+    cut = tokens // 2
+    rows_all = count * slots_per
 
     target = slot_targets(chosen, experts, slots_per)
     slot_ids = jnp.arange(all_slots, dtype=jnp.int32)
@@ -70,45 +111,68 @@
         .transpose(0, 2, 1, 3)
         .reshape(count * slots_per, quarter)
     )
+    mark = jnp.pad(place, ((0, 0), (0, width - tokens)))
+
+    first_part = jnp.concatenate([mark, grads[:cut]], axis=0)
+    outgoing, first_part = hold(outgoing, first_part)
+    first_after = to_previous(first_part)
     rows = exchange(outgoing, "expert")
+    rows, first_after = hold(rows, first_after)
 
     partial_value = lax.dot_general(
         rows, w_down[0], (((1,), (1,)), ((), ())), preferred_element_type=jnp.float32
-    ).astype(jnp.bfloat16)
-    part = lax.axis_index("expert") % split
+    )
     pre = saved_pre[0, 0, 0]
-    _, slope = gelu_parts(lax.dynamic_slice_in_dim(pre, part * share, share, 0))
-    shares = exchange(partial_value, "expert", members).reshape(split, share, -1)
-    own_grad = (jnp.sum(shares.astype(jnp.float32), axis=0) * slope).astype(jnp.bfloat16)
-    hidden_grad = lax.all_gather(own_grad, "expert", axis_index_groups=members, tiled=True)
-
-    act = gelu_parts(pre)[0].astype(jnp.bfloat16)
+    act, slope = gelu_parts(pre)
+    act = act.astype(jnp.bfloat16)
     term_down = lax.dot_general(
         act, rows, (((0,), (0,)), ((), ())), preferred_element_type=jnp.float32
     ).astype(jnp.bfloat16)
-    down = sum_over_groups(term_down)
+    down_pieces = exchange_pieces(term_down)
 
-    back = lax.dot_general(
-        hidden_grad, w_up[0], (((1,), (1,)), ((), ())), preferred_element_type=jnp.float32
-    ).astype(jnp.bfloat16)
-    returned = to_previous(exchange(back, "expert"))
+    core = position & 1
+    half = rows_all // 2
+    keep, away = split_by(core, partial_value[:half], partial_value[half:])
+    value = keep + partner(away.astype(jnp.bfloat16), "expert", 0).astype(jnp.float32)
+    for level in range(1, levels):
+        value = value + partner(value.astype(jnp.bfloat16), "expert", level).astype(jnp.float32)
+    own_slope = jnp.where(core == 1, slope[half:], slope[:half])
+    own_grad = (value * own_slope).astype(jnp.bfloat16)
+    other_grad = partner(own_grad, "expert", 0)
+    hidden_grad = jnp.concatenate(
+        [jnp.where(core == 1, other_grad, own_grad), jnp.where(core == 1, own_grad, other_grad)],
+        axis=0,
+    )
+    second_after = to_previous(grads[cut:])
+    hidden_grad, second_after = hold(hidden_grad, second_after)
 
     term_up = lax.dot_general(
         hidden_grad, saved_in[0, 0], (((0,), (0,)), ((), ())), preferred_element_type=jnp.float32
     ).astype(jnp.bfloat16)
-    up = sum_over_groups(term_up)
+    back = lax.dot_general(
+        hidden_grad, w_up[0], (((1,), (1,)), ((), ())), preferred_element_type=jnp.float32
+    ).astype(jnp.bfloat16)
+    term_up, down_pieces = hold(term_up, down_pieces)
+    up_pieces = exchange_pieces(term_up)
+    down = add_pieces(down_pieces)
 
+    shaped = back.reshape(experts, split, slots_per, quarter).transpose(1, 0, 2, 3)
+    gathered = gather_columns(shaped, levels, position)
+    mine = position >> levels
+    keep, away = split_by(mine, gathered[:, 0], gathered[:, 1])
+    kept = behind(keep, 0)
+    got = behind(away, split)
+    first = jnp.where(mine == 1, got, kept)
+    second = jnp.where(mine == 1, kept, got)
     unpacked = (
-        returned.reshape(experts, split, slots_per, quarter)
-        .transpose(0, 2, 1, 3)
-        .reshape(all_slots, width)
+        jnp.stack([first, second], axis=0).transpose(0, 2, 1, 3).reshape(all_slots, width)
     )
-    target_after = slot_targets(chosen_after, experts, slots_per)
-    hit_after = [target_after[:, k][:, None] == slot_ids[None, :] for k in range(2)]
-    place_after = (hit_after[0] | hit_after[1]).astype(jnp.bfloat16)
-    total = grads_after.astype(jnp.float32) + jnp.dot(
-        place_after, unpacked, preferred_element_type=jnp.float32
+    place_after = first_after[:all_slots, :tokens]
+    grads_after = jnp.concatenate([first_after[all_slots:], second_after], axis=0)
+    total = grads_after.astype(jnp.float32) + lax.dot_general(
+        place_after, unpacked, (((0,), (0,)), ((), ())), preferred_element_type=jnp.float32
     )
+    up = add_pieces(up_pieces)
     return (total.astype(jnp.bfloat16)[None], up[None], down[None])
 
 

time: 208 us -> 167 us (0.80)
  blocking collectives: 45.1 us -> 0 us
  waiting for transfers between devices: 110 us -> 76.1 us
  starting transfers between devices: 33.9 us -> 62.6 us
  local copies, waits for them, and re-layouts: 3.44 us -> 8.66 us
  other arithmetic: 4.36 us -> 8.49 us
    ppermute x3 -> x2, waiting for transfers between devices: 61.4 us -> 0.01 us  [to_previous(): return lax.ppermute(x, 'phase', [(i, i - 1) for i in range(1, peers)])]
    ppermute x0 -> x9, waiting for transfers between devices: none -> 48.4 us  [the longest x7 28.7 us: partner(): return lax.ppermute(block, axis, [(i, i ^ 1 << bit) for i in range(count)])]
    all_to_all x1 -> x0, blocking collectives: 29.6 us -> none  [exchange(): return lax.all_to_all(x, axis, 0, 0, tiled=True, axis_index_groups=groups)]
    all_to_all x4 -> x3, waiting for transfers between devices: 48.6 us -> 27.8 us  [exchange(): return lax.all_to_all(x, axis, 0, 0, tiled=True, axis_index_groups=groups)]
    ppermute x0 -> x9, starting transfers between devices: none -> 17.3 us  [the longest x7 14.7 us: partner(): return lax.ppermute(block, axis, [(i, i ^ 1 << bit) for i in range(count)])]
    all_gather x1 -> x0, blocking collectives: 15.5 us -> none  [body(): lax.all_gather(own_grad, 'expert', axis_index_groups=members, tiled=True)]
    all_to_all x4 -> x3, starting transfers between devices: 30 us -> 42.7 us  [exchange(): return lax.all_to_all(x, axis, 0, 0, tiled=True, axis_index_groups=groups)]
    another operation x4 -> x8, other arithmetic: 1.6 us -> 4.39 us  [the longest x4 3.51 us: gather_columns(): buffer = jnp.stack([first, second], axis=1).reshape((size,) + rest)]
  transfers between devices with their start and end apart: 7 -> 14, of which waited for: 5 -> 9; matrix products, arithmetic and copies ran while one was open for 4% -> 10% of each run, Pallas kernels for 0% -> 0%
where the time goes in v4:
time: 167 us; the launch traced here: 165 us
  waiting for transfers between devices  76.1 us (46%)
  starting transfers between devices  62.6 us (37%)
  local copies, waits for them, and re-layouts  8.66 us (5%)
  other arithmetic  8.49 us (5%)
  matrix products  8.22 us (5%)
    all_to_all x3, starting transfers between devices, exchange(): return lax.all_to_all(x, axis, 0, 0, tiled=True, axis_index_groups=groups)  42.7 us
    ppermute x7, waiting for transfers between devices, partner(): return lax.ppermute(block, axis, [(i, i ^ 1 << bit) for i in range(count)])  28.7 us
    all_to_all x3, waiting for transfers between devices, exchange(): return lax.all_to_all(x, axis, 0, 0, tiled=True, axis_index_groups=groups)  27.8 us
    ppermute x2, waiting for transfers between devices, behind(): return lax.ppermute(block, ('phase', 'expert'), pairs)  19.7 us
    ppermute x7, starting transfers between devices, partner(): return lax.ppermute(block, axis, [(i, i ^ 1 << bit) for i in range(count)])  14.7 us
    another operation x4, other arithmetic, gather_columns(): buffer = jnp.stack([first, second], axis=1).reshape((size,) + rest)  3.51 us
  transfers between devices with their start and end apart: 14, of which 9 were waited for; matrix products, arithmetic and copies ran while one was open for 10% of the time, Pallas kernels for 0%

profile of v4, /device:TPU:1, one launch (start us, length us, event | category | flops | bytes accessed | tf_op | source)
XLA Modules:
  0.0 165.2 jit_solution(4800125988646762736)
XLA Ops:
  0.6 0.9 copy.38
  1.8 0.6 reduce-window.6
  2.4 0.2 slice_reduce_fusion.2
  3.3 0.8 slice_bitcast_fusion.3
  4.0 2.3 %slice_bitcast_fusion = (bf16[64,5120]{1,0:T(8,128)(2,1)}, bf16[64,5120]{1,0:T(8,128)(2,1)S(1)}) fusion(bf16[1,128,5120]{2,1,0:T(8,128)(2,1)} %param.7), kind=kLoop, calls=%fused_computation.25 | loop fusion | bytes 2621440 | tf_op jit(solution)/shard_map/slice | solution.py:146
  6.5 0.3 fusion.2
  6.9 0.8 copy.41
  7.7 1.3 collective-permute-start
  9.0 17.5 %all-to-all-start = ((bf16[16,16,640]{2,1,0:T(8,128)(2,1)}), bf16[16,16,640]{2,1,0:T(8,128)(2,1)S(1)}, u32[]{:S(2)}, u32[]{:S(2)}) async-start(bf16[16,16,640]{2,1,0:T(8,128)(2,1)} %bitcast.9), calls=%async_computation | async-start | bytes 655360 | tf_op jit(solution)/shard_map/all_to_all | solution.py:15
  26.5 13.0 %all-to-all-done = bf16[16,16,640]{2,1,0:T(8,128)(2,1)S(1)} async-done(((bf16[16,16,640]{2,1,0:T(8,128)(2,1)}), bf16[16,16,640]{2,1,0:T(8,128)(2,1)S(1)}, u32[]{:S(2)}, u32[]{:S(2)}) %all-to-all-start) | async-done | bytes 327712 | tf_op jit(solution)/shard_map/all_to_all | solution.py:15
  39.6 0.5 fusion.5
  40.1 0.4 copy-done.2
  40.5 2.0 %collective-permute-start.1 = (bf16[128,768]{1,0:T(8,128)(2,1)S(1)}, bf16[128,768]{1,0:T(8,128)(2,1)S(1)}, u32[]{:S(2)}, u32[]{:S(2)}) collective-permute-start(bf16[128,768]{1,0:T(8,128)(2,1)S(1)} %select_convert_fusion), channel_id=1, source_target_pairs={{0,1},{1,0},{2,3},{3,2},{4,5},{5,4},{6,7},{7,6},{8,9},{9,8},{10,11... | collective-permute-start | bytes 589832 | tf_op jit(solution)/shard_map/ppermute | solution.py:25
  42.6 1.4 collective-permute-done.1
  44.0 1.9 %collective-permute-start.2 = (bf16[128,768]{1,0:T(8,128)(2,1)S(1)}, bf16[128,768]{1,0:T(8,128)(2,1)S(1)}, u32[]{:S(2)}, u32[]{:S(2)}) collective-permute-start(bf16[128,768]{1,0:T(8,128)(2,1)S(1)} %get-tuple-element.24), channel_id=1, source_target_pairs={{0,2},{1,3},{2,0},{3,1},{4,6},{5,7},{6,4},{7,5},{8,10},{9,11},{10,... | collective-permute-start | bytes 589832 | tf_op jit(solution)/shard_map/ppermute | solution.py:25
  46.0 1.3 collective-permute-start.5
  47.3 5.1 %collective-permute-done.2 = bf16[128,768]{1,0:T(8,128)(2,1)S(1)} collective-permute-done((bf16[128,768]{1,0:T(8,128)(2,1)S(1)}, bf16[128,768]{1,0:T(8,128)(2,1)S(1)}, u32[]{:S(2)}, u32[]{:S(2)}) %collective-permute-start.2) | collective-permute-done | bytes 196640 | tf_op jit(solution)/shard_map/ppermute | solution.py:25
  52.4 1.9 %collective-permute-start.3 = (bf16[128,768]{1,0:T(8,128)(2,1)S(1)}, bf16[128,768]{1,0:T(8,128)(2,1)S(1)}, u32[]{:S(2)}, u32[]{:S(2)}) collective-permute-start(bf16[128,768]{1,0:T(8,128)(2,1)S(1)} %fusion.19), channel_id=1, source_target_pairs={{0,4},{1,5},{2,6},{3,7},{4,0},{5,1},{6,2},{7,3},{8,12},{9,13},{10,... | collective-permute-start | bytes 589832 | tf_op jit(solution)/shard_map/ppermute | solution.py:25
  54.4 0.3 fusion.12
  54.7 11.4 %collective-permute-done.3 = bf16[128,768]{1,0:T(8,128)(2,1)S(1)} collective-permute-done((bf16[128,768]{1,0:T(8,128)(2,1)S(1)}, bf16[128,768]{1,0:T(8,128)(2,1)S(1)}, u32[]{:S(2)}, u32[]{:S(2)}) %collective-permute-start.3) | collective-permute-done | bytes 196640 | tf_op jit(solution)/shard_map/ppermute | solution.py:25
  66.2 2.4 %collective-permute-start.4 = (bf16[128,768]{1,0:T(8,128)(2,1)S(1)}, bf16[128,768]{1,0:T(8,128)(2,1)S(1)}, u32[]{:S(2)}, u32[]{:S(2)}) collective-permute-start(bf16[128,768]{1,0:T(8,128)(2,1)S(1)} %fusion.16), channel_id=1, source_target_pairs={{0,1},{1,0},{2,3},{3,2},{4,5},{5,4},{6,7},{7,6},{8,9},{9,8},{10,11... | collective-permute-start | bytes 589832 | tf_op jit(solution)/shard_map/ppermute | solution.py:25
  68.6 1.6 convolution_convert_fusion
  70.2 16.1 %all-to-all-start.1 = ((bf16[16,48,640]{2,1,0:T(8,128)(2,1)}), bf16[16,48,640]{2,1,0:T(8,128)(2,1)S(1)}, u32[]{:S(2)}, u32[]{:S(2)}) async-start(bf16[16,48,640]{2,1,0:T(8,128)(2,1)} %bitcast.45), calls=%async_computation.1 | async-start | bytes 1966080 | tf_op jit(solution)/shard_map/all_to_all | solution.py:15
  86.4 1.7 %convolution_convert_fusion.2 = bf16[256,640]{1,0:T(8,128)(2,1)S(1)} fusion(bf16[256,768]{1,0:T(8,128)(2,1)S(1)} %pad_maximum_fusion.1, bf16[1,640,768]{2,1,0:T(8,128)(2,1)} %param.12), kind=kOutput, calls=%fused_computation.13 | convolution fusion | flops 251822080 | bytes 1703936 | tf_op jit(solution)/shard_map/dot_general | solution.py:152
  88.1 2.2 %collective-permute-start.6 = (bf16[4,1,2,16,640]{4,3,0,2,1:T(8,128)(2,1)S(1)}, bf16[4,1,2,16,640]{4,3,0,2,1:T(8,128)(2,1)S(1)}, u32[]{:S(2)}, u32[]{:S(2)}) collective-permute-start(bf16[4,1,2,16,640]{4,3,0,2,1:T(8,128)(2,1)S(1)} %fusion.26), channel_id=1, source_target_pairs={{0,1},{1,0},{2,3},{3,2},{4,5},{5,4},{6,7},{7,6},{8,9},{9,8},{10,11... | collective-permute-start | bytes 491528 | tf_op jit(solution)/shard_map/ppermute | solution.py:25
  90.4 1.1 collective-permute-done.6
  91.5 0.3 copy.46
  91.7 0.3 copy.47
  92.0 1.5 fusion.23
  93.5 2.3 %collective-permute-start.7 = (bf16[2,2,2,16,640]{4,1,3,2,0:T(2,128)(2,1)}, bf16[2,2,2,16,640]{4,1,3,2,0:T(2,128)(2,1)S(1)}, u32[]{:S(2)}, u32[]{:S(2)}) collective-permute-start(bf16[2,2,2,16,640]{4,1,3,2,0:T(2,128)(2,1)} %get-tuple-element.21), channel_id=1, source_target_pairs={{0,2},{1,3},{2,0},{3,1},{4,6},{5,7},{6,4},{7,5},{8,10},{9,11},{10,... | collective-permute-start | bytes 491528 | tf_op jit(solution)/shard_map/ppermute | solution.py:25
  95.8 1.5 convolution_convert_fusion.1
  97.3 14.7 %all-to-all-done.1 = bf16[16,48,640]{2,1,0:T(8,128)(2,1)S(1)} async-done(((bf16[16,48,640]{2,1,0:T(8,128)(2,1)}), bf16[16,48,640]{2,1,0:T(8,128)(2,1)S(1)}, u32[]{:S(2)}, u32[]{:S(2)}) %all-to-all-start.1) | async-done | bytes 983072 | tf_op jit(solution)/shard_map/all_to_all | solution.py:15
  112.0 9.2 %all-to-all-start.2 = ((bf16[16,48,640]{2,1,0:T(8,128)(2,1)}), bf16[16,48,640]{2,1,0:T(8,128)(2,1)S(1)}, u32[]{:S(2)}, u32[]{:S(2)}) async-start(bf16[16,48,640]{2,1,0:T(8,128)(2,1)} %bitcast.47), calls=%async_computation.2 | async-start | bytes 1966080 | tf_op jit(solution)/shard_map/all_to_all | solution.py:15
  121.2 0.3 fusion.21
  121.5 1.2 pad_maximum_fusion.2
  122.7 1.1 reshape_reshape.4
  123.9 1.9 %collective-permute-start.8 = (bf16[1,4,2,16,640]{4,1,3,2,0:T(4,128)(2,1)S(1)}, bf16[1,4,2,16,640]{4,1,3,2,0:T(4,128)(2,1)}, u32[]{:S(2)}, u32[]{:S(2)}) collective-permute-start(bf16[1,4,2,16,640]{4,1,3,2,0:T(4,128)(2,1)S(1)} %select_bitcast_fusion.4), channel_id=1, source_target_pairs={{0,4},{1,5},{2,6},{3,7},{4,0},{5,1},{6,2},{7,3},{8,12},{9,13},{10,... | collective-permute-start | bytes 491528 | tf_op jit(solution)/shard_map/ppermute | solution.py:25
  125.8 9.7 %collective-permute-done.8 = bf16[1,4,2,16,640]{4,1,3,2,0:T(4,128)(2,1)} collective-permute-done((bf16[1,4,2,16,640]{4,1,3,2,0:T(4,128)(2,1)S(1)}, bf16[1,4,2,16,640]{4,1,3,2,0:T(4,128)(2,1)}, u32[]{:S(2)}, u32[]{:S(2)}) %collective-permute-start.8) | collective-permute-done | bytes 163872 | tf_op jit(solution)/shard_map/ppermute | solution.py:25
  135.5 1.1 fusion.27
  136.5 1.0 pad_maximum_fusion.3
  137.5 1.1 reshape.171
  138.6 1.3 collective-permute-start.10
  139.9 1.3 collective-permute-start.9
  141.2 8.7 %collective-permute-done.10 = bf16[8,16,640]{2,0,1:T(8,128)(2,1)S(1)} collective-permute-done((bf16[8,16,640]{2,0,1:T(8,128)(2,1)S(1)}, bf16[8,16,640]{2,0,1:T(8,128)(2,1)S(1)}, u32[]{:S(2)}, u32[]{:S(2)}) %collective-permute-start.10) | collective-permute-done | bytes 163872 | tf_op jit(solution)/shard_map/ppermute | solution.py:78
  150.0 10.9 %collective-permute-done.9 = bf16[8,16,640]{2,0,1:T(8,128)(2,1)S(1)} collective-permute-done((bf16[8,16,640]{2,0,1:T(8,128)(2,1)S(1)}, bf16[8,16,640]{2,0,1:T(8,128)(2,1)S(1)}, u32[]{:S(2)}, u32[]{:S(2)}) %collective-permute-start.9) | collective-permute-done | bytes 163872 | tf_op jit(solution)/shard_map/ppermute | solution.py:78
  161.0 2.7 %fusion.1 = bf16[1,128,5120]{2,1,0:T(8,128)(2,1)} fusion(bf16[32,5120]{1,0:T(8,128)(2,1)S(1)} %bitcast.159, bf16[64,5120]{1,0:T(8,128)(2,1)} %collective-permute-done.5, bf16[64,5120]{1,0:T(8,128)(2,1)S(1)} %slice-done, bf16[96,5120]{1,0:T(8,128)(2,1)S(1)} %copy-done.3), kind=kOutput, calls=%fused_computation.2 | convolution fusion | flops 45875200 | bytes 2957312 | tf_op jit(solution)/shard_map/dot_general | solution.py:172
  163.7 0.8 reduce_sum.48
  164.5 0.8 reduce_sum.47
  (47 shorter events, 1.8 us)
Async XLA Ops:
  0.6 38.9 %copy-start = (bf16[1,768,640]{2,1,0:T(8,128)(2,1)S(1)}, bf16[1,768,640]{2,1,0:T(8,128)(2,1)}, u32[]{:S(2)}) copy-start(bf16[1,768,640]{2,1,0:T(8,128)(2,1)} %param.13) | copy-start | bytes 2949124
  4.0 2.5 %copy-start.1 = (bf16[1,128,5120]{2,1,0:T(8,128)(2,1)S(1)}, bf16[1,128,5120]{2,1,0:T(8,128)(2,1)}, u32[]{:S(2)}) copy-start(bf16[1,128,5120]{2,1,0:T(8,128)(2,1)} %param.7) | copy-start | bytes 3932164
  7.7 31.8 %collective-permute-start = (bf16[96,5120]{1,0:T(8,128)(2,1)S(1)}, bf16[96,5120]{1,0:T(8,128)(2,1)S(1)}, u32[]{:S(2)}, u32[]{:S(2)}) collective-permute-start(bf16[96,5120]{1,0:T(8,128)(2,1)S(1)} %pad_maximum_fusion), channel_id=1, source_target_pairs={{256,0},{512,256},{768,512},{257,1},{513,257},{769,513},{258,2},{5... | collective-permute-start | bytes 2949128 | tf_op jit(solution)/shard_map/ppermute | solution.py:20
  9.0 30.5 %all-to-all-start = ((bf16[16,16,640]{2,1,0:T(8,128)(2,1)}), bf16[16,16,640]{2,1,0:T(8,128)(2,1)S(1)}, u32[]{:S(2)}, u32[]{:S(2)}) async-start(bf16[16,16,640]{2,1,0:T(8,128)(2,1)} %bitcast.9), calls=%async_computation | async-start | bytes 655360 | tf_op jit(solution)/shard_map/all_to_all | solution.py:15
  39.6 0.9 copy-start.2
  40.1 5.9 %copy-start.4 = (bf16[64,5120]{1,0:T(8,128)(2,1)S(1)}, bf16[64,5120]{1,0:T(8,128)(2,1)}, u32[]{:S(2)}) copy-start(bf16[64,5120]{1,0:T(8,128)(2,1)} %get-tuple-element.26) | copy-start | bytes 1966084
  40.5 13.9 %copy-start.5 = (bf16[1,1,1,256,768]{4,3,2,1,0:T(8,128)(2,1)S(1)}, bf16[1,1,1,256,768]{4,3,2,1,0:T(8,128)(2,1)}, u32[]{:S(2)}) copy-start(bf16[1,1,1,256,768]{4,3,2,1,0:T(8,128)(2,1)} %param.11) | copy-start | bytes 1179652
  40.5 3.5 %collective-permute-start.1 = (bf16[128,768]{1,0:T(8,128)(2,1)S(1)}, bf16[128,768]{1,0:T(8,128)(2,1)S(1)}, u32[]{:S(2)}, u32[]{:S(2)}) collective-permute-start(bf16[128,768]{1,0:T(8,128)(2,1)S(1)} %select_convert_fusion), channel_id=1, source_target_pairs={{0,1},{1,0},{2,3},{3,2},{4,5},{5,4},{6,7},{7,6},{8,9},{9,8},{10,11... | collective-permute-start | bytes 589832 | tf_op jit(solution)/shard_map/ppermute | solution.py:25
  44.0 8.4 %collective-permute-start.2 = (bf16[128,768]{1,0:T(8,128)(2,1)S(1)}, bf16[128,768]{1,0:T(8,128)(2,1)S(1)}, u32[]{:S(2)}, u32[]{:S(2)}) collective-permute-start(bf16[128,768]{1,0:T(8,128)(2,1)S(1)} %get-tuple-element.24), channel_id=1, source_target_pairs={{0,2},{1,3},{2,0},{3,1},{4,6},{5,7},{6,4},{7,5},{8,10},{9,11},{10,... | collective-permute-start | bytes 589832 | tf_op jit(solution)/shard_map/ppermute | solution.py:25
  46.0 40.4 %collective-permute-start.5 = (bf16[64,5120]{1,0:T(8,128)(2,1)S(1)}, bf16[64,5120]{1,0:T(8,128)(2,1)}, u32[]{:S(2)}, u32[]{:S(2)}) collective-permute-start(bf16[64,5120]{1,0:T(8,128)(2,1)S(1)} %copy-done.4), channel_id=1, source_target_pairs={{256,0},{512,256},{768,512},{257,1},{513,257},{769,513},{258,2},{5... | collective-permute-start | bytes 1966088 | tf_op jit(solution)/shard_map/ppermute | solution.py:20
  52.4 13.7 %collective-permute-start.3 = (bf16[128,768]{1,0:T(8,128)(2,1)S(1)}, bf16[128,768]{1,0:T(8,128)(2,1)S(1)}, u32[]{:S(2)}, u32[]{:S(2)}) collective-permute-start(bf16[128,768]{1,0:T(8,128)(2,1)S(1)} %fusion.19), channel_id=1, source_target_pairs={{0,4},{1,5},{2,6},{3,7},{4,0},{5,1},{6,2},{7,3},{8,12},{9,13},{10,... | collective-permute-start | bytes 589832 | tf_op jit(solution)/shard_map/ppermute | solution.py:25
  66.2 20.1 %collective-permute-start.4 = (bf16[128,768]{1,0:T(8,128)(2,1)S(1)}, bf16[128,768]{1,0:T(8,128)(2,1)S(1)}, u32[]{:S(2)}, u32[]{:S(2)}) collective-permute-start(bf16[128,768]{1,0:T(8,128)(2,1)S(1)} %fusion.16), channel_id=1, source_target_pairs={{0,1},{1,0},{2,3},{3,2},{4,5},{5,4},{6,7},{7,6},{8,9},{9,8},{10,11... | collective-permute-start | bytes 589832 | tf_op jit(solution)/shard_map/ppermute | solution.py:25
  70.2 41.8 %all-to-all-start.1 = ((bf16[16,48,640]{2,1,0:T(8,128)(2,1)}), bf16[16,48,640]{2,1,0:T(8,128)(2,1)S(1)}, u32[]{:S(2)}, u32[]{:S(2)}) async-start(bf16[16,48,640]{2,1,0:T(8,128)(2,1)} %bitcast.45), calls=%async_computation.1 | async-start | bytes 1966080 | tf_op jit(solution)/shard_map/all_to_all | solution.py:15
  88.1 3.3 %collective-permute-start.6 = (bf16[4,1,2,16,640]{4,3,0,2,1:T(8,128)(2,1)S(1)}, bf16[4,1,2,16,640]{4,3,0,2,1:T(8,128)(2,1)S(1)}, u32[]{:S(2)}, u32[]{:S(2)}) collective-permute-start(bf16[4,1,2,16,640]{4,3,0,2,1:T(8,128)(2,1)S(1)} %fusion.26), channel_id=1, source_target_pairs={{0,1},{1,0},{2,3},{3,2},{4,5},{5,4},{6,7},{7,6},{8,9},{9,8},{10,11... | collective-permute-start | bytes 491528 | tf_op jit(solution)/shard_map/ppermute | solution.py:25
  90.3 5.4 %copy-start.6 = (bf16[1,1,256,640]{3,2,1,0:T(8,128)(2,1)S(1)}, bf16[1,1,256,640]{3,2,1,0:T(8,128)(2,1)}, u32[]{:S(2)}) copy-start(bf16[1,1,256,640]{3,2,1,0:T(8,128)(2,1)} %param.10) | copy-start | bytes 983044
  93.5 27.7 %collective-permute-start.7 = (bf16[2,2,2,16,640]{4,1,3,2,0:T(2,128)(2,1)}, bf16[2,2,2,16,640]{4,1,3,2,0:T(2,128)(2,1)S(1)}, u32[]{:S(2)}, u32[]{:S(2)}) collective-permute-start(bf16[2,2,2,16,640]{4,1,3,2,0:T(2,128)(2,1)} %get-tuple-element.21), channel_id=1, source_target_pairs={{0,2},{1,3},{2,0},{3,1},{4,6},{5,7},{6,4},{7,5},{8,10},{9,11},{10,... | collective-permute-start | bytes 491528 | tf_op jit(solution)/shard_map/ppermute | solution.py:25
  112.0 52.5 %all-to-all-start.2 = ((bf16[16,48,640]{2,1,0:T(8,128)(2,1)}), bf16[16,48,640]{2,1,0:T(8,128)(2,1)S(1)}, u32[]{:S(2)}, u32[]{:S(2)}) async-start(bf16[16,48,640]{2,1,0:T(8,128)(2,1)} %bitcast.47), calls=%async_computation.2 | async-start | bytes 1966080 | tf_op jit(solution)/shard_map/all_to_all | solution.py:15
  123.9 11.6 %collective-permute-start.8 = (bf16[1,4,2,16,640]{4,1,3,2,0:T(4,128)(2,1)S(1)}, bf16[1,4,2,16,640]{4,1,3,2,0:T(4,128)(2,1)}, u32[]{:S(2)}, u32[]{:S(2)}) collective-permute-start(bf16[1,4,2,16,640]{4,1,3,2,0:T(4,128)(2,1)S(1)} %select_bitcast_fusion.4), channel_id=1, source_target_pairs={{0,4},{1,5},{2,6},{3,7},{4,0},{5,1},{6,2},{7,3},{8,12},{9,13},{10,... | collective-permute-start | bytes 491528 | tf_op jit(solution)/shard_map/ppermute | solution.py:25
  138.6 11.3 %collective-permute-start.10 = (bf16[8,16,640]{2,0,1:T(8,128)(2,1)S(1)}, bf16[8,16,640]{2,0,1:T(8,128)(2,1)S(1)}, u32[]{:S(2)}, u32[]{:S(2)}) collective-permute-start(bf16[8,16,640]{2,0,1:T(8,128)(2,1)S(1)} %get-tuple-element.39), channel_id=1, source_target_pairs={{256,0},{257,1},{258,2},{259,3},{260,4},{261,5},{262,6},{263,7},{2... | collective-permute-start | bytes 491528 | tf_op jit(solution)/shard_map/ppermute | solution.py:78
  139.9 21.0 %collective-permute-start.9 = (bf16[8,16,640]{2,0,1:T(8,128)(2,1)S(1)}, bf16[8,16,640]{2,0,1:T(8,128)(2,1)S(1)}, u32[]{:S(2)}, u32[]{:S(2)}) collective-permute-start(bf16[8,16,640]{2,0,1:T(8,128)(2,1)S(1)} %get-tuple-element.38), channel_id=1, source_target_pairs={{256,8},{257,9},{258,10},{259,11},{260,12},{261,13},{262,14},{263,... | collective-permute-start | bytes 491528 | tf_op jit(solution)/shard_map/ppermute | solution.py:78
  141.2 19.8 %copy-start.3 = (bf16[96,5120]{1,0:T(8,128)(2,1)S(1)}, bf16[96,5120]{1,0:T(8,128)(2,1)}, u32[]{:S(2)}) copy-start(bf16[96,5120]{1,0:T(8,128)(2,1)} %copy-done.2) | copy-start | bytes 2949124
  141.2 19.8 %slice-start = ((bf16[96,5120]{1,0:T(8,128)(2,1)}), bf16[64,5120]{1,0:T(8,128)(2,1)S(1)}, s32[]{:S(2)}) async-start(bf16[96,5120]{1,0:T(8,128)(2,1)} %copy-done.2), calls=%async_computation.3 | async-start | bytes 1310720 | tf_op jit(solution)/shard_map/slice | solution.py:171

commit v5 on v4

--- a/solution.py
+++ b/solution.py
@@ -38,35 +38,38 @@
     return (flat * slots_per + slot).reshape(tokens, 2)
 
 
-def exchange_pieces(term):
-    return exchange(term, "dp")
+def scatter_along_z(term):
+    count = lax.axis_size("dp")
+    near = count // 2
+    hid, quarter = term.shape
+    groups = [[h * near + z for z in range(near)] for h in range(2)]
+    ordered = term.reshape(2, near, hid // count, quarter).transpose(1, 0, 2, 3)
+    return exchange(ordered.reshape(hid, quarter), "dp", groups)
 
 
 def add_pieces(pieces):
+    near = lax.axis_size("dp") // 2
+    hid, quarter = pieces.shape
+    pieces = pieces.reshape(near, 2, hid // (2 * near), quarter)
+    return jnp.sum(pieces.astype(jnp.float32), axis=0)
+
+
+def across_x(sums):
     count = lax.axis_size("dp")
-    hid, quarter = pieces.shape
-    pieces = pieces.reshape(count, hid // count, quarter)
-    return jnp.sum(pieces.astype(jnp.float32), axis=0).astype(jnp.bfloat16)
+    near = count // 2
+    side = lax.axis_index("dp") // near
+    away = jnp.stack([jnp.where(side == 1, s[0], s[1]).astype(jnp.bfloat16) for s in sums])
+    got = lax.ppermute(away, "dp", [(i, (i + near) % count) for i in range(count)])
+    return [
+        (jnp.where(side == 1, s[1], s[0]) + got[i].astype(jnp.float32)).astype(jnp.bfloat16)
+        for i, s in enumerate(sums)
+    ]
 
 
 def split_by(mine, lower, upper):
     keep = jnp.where(mine == 1, upper, lower)
     away = jnp.where(mine == 1, lower, upper)
     return keep, away
-
-
-def gather_columns(buffer, levels, position):
-    size = buffer.shape[0]
-    rest = buffer.shape[1:]
-    for level in range(levels):
-        mine = position >> level & 1
-        shaped = buffer.reshape((size >> level + 1, 2, 1 << level) + rest)
-        keep, away = split_by(mine, shaped[:, 0], shaped[:, 1])
-        got = partner(away, "expert", level)
-        first = jnp.where(mine == 1, got, keep)
-        second = jnp.where(mine == 1, keep, got)
-        buffer = jnp.stack([first, second], axis=1).reshape((size,) + rest)
-    return buffer
 
 
 def behind(block, flip):
@@ -91,7 +94,6 @@
     slots_per = saved_in.shape[2] // count
     all_slots = experts * slots_per
     levels = split.bit_length() - 1
-    cut = tokens // 2
     rows_all = count * slots_per
 
     target = slot_targets(chosen, experts, slots_per)
@@ -111,13 +113,10 @@
         .transpose(0, 2, 1, 3)
         .reshape(count * slots_per, quarter)
     )
-    mark = jnp.pad(place, ((0, 0), (0, width - tokens)))
-
-    first_part = jnp.concatenate([mark, grads[:cut]], axis=0)
-    outgoing, first_part = hold(outgoing, first_part)
-    first_after = to_previous(first_part)
+    outgoing, place = hold(outgoing, place)
+    place_after = to_previous(place)
     rows = exchange(outgoing, "expert")
-    rows, first_after = hold(rows, first_after)
+    rows, place_after = hold(rows, place_after)
 
     partial_value = lax.dot_general(
         rows, w_down[0], (((1,), (1,)), ((), ())), preferred_element_type=jnp.float32
@@ -128,7 +127,7 @@
     term_down = lax.dot_general(
         act, rows, (((0,), (0,)), ((), ())), preferred_element_type=jnp.float32
     ).astype(jnp.bfloat16)
-    down_pieces = exchange_pieces(term_down)
+    down_pieces = scatter_along_z(term_down)
 
     core = position & 1
     half = rows_all // 2
@@ -143,36 +142,52 @@
         [jnp.where(core == 1, other_grad, own_grad), jnp.where(core == 1, own_grad, other_grad)],
         axis=0,
     )
-    second_after = to_previous(grads[cut:])
-    hidden_grad, second_after = hold(hidden_grad, second_after)
+    hidden_grad, down_pieces = hold(hidden_grad, down_pieces)
+    grads_after = to_previous(grads)
 
     term_up = lax.dot_general(
         hidden_grad, saved_in[0, 0], (((0,), (0,)), ((), ())), preferred_element_type=jnp.float32
     ).astype(jnp.bfloat16)
+    out_block = jnp.arange(rows_all, dtype=jnp.int32)[:, None]
+    in_block = jnp.arange(rows_all, dtype=jnp.int32)[None, :]
+    bits = levels + 1
+    goes = sum(
+        (out_block // slots_per >> (bits - 1 - b) & 1) << b for b in range(bits)
+    )
+    same = ((goes ^ position) == in_block // slots_per) & (
+        out_block % slots_per == in_block % slots_per
+    )
+    ordered = jnp.dot(
+        same.astype(jnp.bfloat16), hidden_grad, preferred_element_type=jnp.float32
+    ).astype(jnp.bfloat16)
     back = lax.dot_general(
-        hidden_grad, w_up[0], (((1,), (1,)), ((), ())), preferred_element_type=jnp.float32
-    ).astype(jnp.bfloat16)
-    term_up, down_pieces = hold(term_up, down_pieces)
-    up_pieces = exchange_pieces(term_up)
-    down = add_pieces(down_pieces)
-
-    shaped = back.reshape(experts, split, slots_per, quarter).transpose(1, 0, 2, 3)
-    gathered = gather_columns(shaped, levels, position)
+        ordered, w_up[0], (((1,), (1,)), ((), ())), preferred_element_type=jnp.float32
+    ).astype(jnp.bfloat16)
+    up_pieces = scatter_along_z(term_up)
+
+    buffer = back.reshape(1, count, slots_per, quarter)
+    for level in range(levels):
+        middle = buffer.shape[1] // 2
+        got = partner(buffer[:, middle:], "expert", level)
+        buffer = jnp.concatenate([buffer[:, :middle], got], axis=0)
+        if level == 0:
+            buffer, grads_after = hold(buffer, grads_after)
+    kept = behind(buffer[:, 0], 0)
+    got = behind(buffer[:, 1], split)
+    blocks = jnp.stack([kept, got]).transpose(0, 2, 1, 3)
+    for level in range(levels):
+        shaped = blocks.reshape(
+            experts, slots_per, split >> (level + 1), 2, 1 << level, quarter
+        )
+        blocks = jnp.where((position >> level & 1) == 1, jnp.flip(shaped, 3), shaped)
+    unpacked = blocks.reshape(all_slots, width)
     mine = position >> levels
-    keep, away = split_by(mine, gathered[:, 0], gathered[:, 1])
-    kept = behind(keep, 0)
-    got = behind(away, split)
-    first = jnp.where(mine == 1, got, kept)
-    second = jnp.where(mine == 1, kept, got)
-    unpacked = (
-        jnp.stack([first, second], axis=0).transpose(0, 2, 1, 3).reshape(all_slots, width)
-    )
-    place_after = first_after[:all_slots, :tokens]
-    grads_after = jnp.concatenate([first_after[all_slots:], second_after], axis=0)
+    place_after = place_after.reshape(experts, slots_per, tokens)
+    place_after = jnp.where(mine == 1, place_after[::-1], place_after).reshape(all_slots, tokens)
     total = grads_after.astype(jnp.float32) + lax.dot_general(
         place_after, unpacked, (((0,), (0,)), ((), ())), preferred_element_type=jnp.float32
     )
-    up = add_pieces(up_pieces)
+    down, up = across_x([add_pieces(down_pieces), add_pieces(up_pieces)])
     return (total.astype(jnp.bfloat16)[None], up[None], down[None])
 
 

time: 167 us -> 140 us (0.84)
  the two profiles are of different devices: /device:TPU:1 before, /device:TPU:12 now
where the time goes in v5:
time: 140 us; the launch traced here: 139 us
  starting transfers between devices  67.5 us (48%)
  waiting for transfers between devices  49.7 us (36%)
  other arithmetic  8.11 us (6%)
  matrix products  7.15 us (5%)
  local copies, waits for them, and re-layouts  5.99 us (4%)
    all_to_all x3, starting transfers between devices, exchange(): return lax.all_to_all(x, axis, 0, 0, tiled=True, axis_index_groups=groups)  31.3 us
    ppermute x7, waiting for transfers between devices, partner(): return lax.ppermute(block, axis, [(i, i ^ 1 << bit) for i in range(count)])  22.5 us
    ppermute x7, starting transfers between devices, partner(): return lax.ppermute(block, axis, [(i, i ^ 1 << bit) for i in range(count)])  18 us
    all_to_all x3, waiting for transfers between devices, exchange(): return lax.all_to_all(x, axis, 0, 0, tiled=True, axis_index_groups=groups)  9.66 us
    ppermute x2, waiting for transfers between devices, behind(): return lax.ppermute(block, ('phase', 'expert'), pairs)  8.24 us
    ppermute x2, starting transfers between devices, behind(): return lax.ppermute(block, ('phase', 'expert'), pairs)  8.23 us
    ppermute x2, starting transfers between devices, to_previous(): return lax.ppermute(x, 'phase', [(i, i - 1) for i in range(1, peers)])  6.69 us
    ppermute x1, waiting for transfers between devices, across_x(): lax.ppermute(away, 'dp', [(i, (i + near) % count) for i in range(count)])  5.29 us
  transfers between devices with their start and end apart: 15, of which 11 were waited for; matrix products, arithmetic and copies ran while one was open for 9% of the time, Pallas kernels for 0%

profile of v5, /device:TPU:12, one launch (start us, length us, event | category | flops | bytes accessed | tf_op | source)
XLA Modules:
  0.0 139.5 jit_solution(11392622183432551540)
XLA Ops:
  0.6 0.9 copy.27
  1.8 0.8 slice_bitcast_fusion.1
  2.6 0.6 reduce-window.6
  3.2 0.2 slice_reduce_fusion.2
  3.4 0.2 reduce-window.9
  3.8 0.2 slice_reduce_fusion.1
  4.1 1.6 %fusion = bf16[32,5120]{1,0:T(8,128)(2,1)S(1)} fusion(f32[32]{0:T(128)S(1)} %add_reduce_fusion, s32[128]{0:T(128)S(1)} %get-tuple-element.20, s32[128]{0:T(128)S(1)} %get-tuple-element.19, bf16[1,128,5120]{2,1,0:T(8,128)(2,1)} %param.7), kind=kOutput, calls=%fused_computation.1 | convolution fusion | flops 42283008 | bytes 1639552 | tf_op jit(solution)/shard_map/dot_general | solution.py:109
  5.8 0.8 copy.30
  6.6 7.7 %all-to-all-start = ((bf16[16,16,640]{2,1,0:T(8,128)(2,1)}), bf16[16,16,640]{2,1,0:T(8,128)(2,1)S(1)}, u32[]{:S(2)}, u32[]{:S(2)}) async-start(bf16[16,16,640]{2,1,0:T(8,128)(2,1)} %bitcast.8), calls=%async_computation | async-start | bytes 655360 | tf_op jit(solution)/shard_map/all_to_all | solution.py:15
  14.3 3.3 %collective-permute-start = (bf16[32,128]{1,0:T(8,128)(2,1)S(1)}, bf16[32,128]{1,0:T(8,128)(2,1)S(1)}, u32[]{:S(2)}, u32[]{:S(2)}) collective-permute-start(bf16[32,128]{1,0:T(8,128)(2,1)S(1)} %fusion.39), channel_id=1, source_target_pairs={{256,0},{512,256},{768,512},{257,1},{513,257},{769,513},{258,2},{5... | collective-permute-start | bytes 24584 | tf_op jit(solution)/shard_map/ppermute | solution.py:20
  17.6 2.2 %collective-permute-done = bf16[32,128]{1,0:T(8,128)(2,1)S(1)} collective-permute-done((bf16[32,128]{1,0:T(8,128)(2,1)S(1)}, bf16[32,128]{1,0:T(8,128)(2,1)S(1)}, u32[]{:S(2)}, u32[]{:S(2)}) %collective-permute-start) | collective-permute-done | bytes 8224 | tf_op jit(solution)/shard_map/ppermute | solution.py:20
  19.8 6.9 %all-to-all-done = bf16[16,16,640]{2,1,0:T(8,128)(2,1)S(1)} async-done(((bf16[16,16,640]{2,1,0:T(8,128)(2,1)}), bf16[16,16,640]{2,1,0:T(8,128)(2,1)S(1)}, u32[]{:S(2)}, u32[]{:S(2)}) %all-to-all-start) | async-done | bytes 327712 | tf_op jit(solution)/shard_map/all_to_all | solution.py:15
  26.7 0.5 fusion.3
  27.2 3.0 %collective-permute-start.1 = (bf16[128,768]{1,0:T(8,128)(2,1)S(1)}, bf16[128,768]{1,0:T(8,128)(2,1)S(1)}, u32[]{:S(2)}, u32[]{:S(2)}) collective-permute-start(bf16[128,768]{1,0:T(8,128)(2,1)S(1)} %select_convert_fusion), channel_id=1, source_target_pairs={{0,1},{1,0},{2,3},{3,2},{4,5},{5,4},{6,7},{7,6},{8,9},{9,8},{10,11... | collective-permute-start | bytes 589832 | tf_op jit(solution)/shard_map/ppermute | solution.py:25
  30.2 0.6 convolution_convert_fusion.1
  30.8 1.0 copy.31
  31.8 16.7 %all-to-all-start.1 = ((bf16[8,96,640]{2,1,0:T(8,128)(2,1)}), bf16[8,96,640]{2,1,0:T(8,128)(2,1)S(1)}, u32[]{:S(2)}, u32[]{:S(2)}) async-start(bf16[8,96,640]{2,1,0:T(8,128)(2,1)} %bitcast.102), calls=%async_computation.1 | async-start | bytes 1966080 | tf_op jit(solution)/shard_map/all_to_all | solution.py:15
  48.6 1.9 %collective-permute-start.2 = (bf16[128,768]{1,0:T(8,128)(2,1)S(1)}, bf16[128,768]{1,0:T(8,128)(2,1)S(1)}, u32[]{:S(2)}, u32[]{:S(2)}) collective-permute-start(bf16[128,768]{1,0:T(8,128)(2,1)S(1)} %get-tuple-element.21), channel_id=1, source_target_pairs={{0,2},{1,3},{2,0},{3,1},{4,6},{5,7},{6,4},{7,5},{8,10},{9,11},{10,... | collective-permute-start | bytes 589832 | tf_op jit(solution)/shard_map/ppermute | solution.py:25
  50.5 3.4 %collective-permute-start.6 = (bf16[128,5120]{1,0:T(8,128)(2,1)}, bf16[128,5120]{1,0:T(8,128)(2,1)}, u32[]{:S(2)}, u32[]{:S(2)}) collective-permute-start(bf16[128,5120]{1,0:T(8,128)(2,1)} %bitcast.107), channel_id=1, source_target_pairs={{256,0},{512,256},{768,512},{257,1},{513,257},{769,513},{258,2},{5... | collective-permute-start | bytes 3932168 | tf_op jit(solution)/shard_map/ppermute | solution.py:20
  53.9 3.1 %collective-permute-done.2 = bf16[128,768]{1,0:T(8,128)(2,1)S(1)} collective-permute-done((bf16[128,768]{1,0:T(8,128)(2,1)S(1)}, bf16[128,768]{1,0:T(8,128)(2,1)S(1)}, u32[]{:S(2)}, u32[]{:S(2)}) %collective-permute-start.2) | collective-permute-done | bytes 196640 | tf_op jit(solution)/shard_map/ppermute | solution.py:25
  57.1 2.8 %collective-permute-start.3 = (bf16[128,768]{1,0:T(8,128)(2,1)S(1)}, bf16[128,768]{1,0:T(8,128)(2,1)S(1)}, u32[]{:S(2)}, u32[]{:S(2)}) collective-permute-start(bf16[128,768]{1,0:T(8,128)(2,1)S(1)} %fusion.17), channel_id=1, source_target_pairs={{0,4},{1,5},{2,6},{3,7},{4,0},{5,1},{6,2},{7,3},{8,12},{9,13},{10,... | collective-permute-start | bytes 589832 | tf_op jit(solution)/shard_map/ppermute | solution.py:25
  59.9 0.3 fusion.10
  60.2 9.5 %collective-permute-done.3 = bf16[128,768]{1,0:T(8,128)(2,1)S(1)} collective-permute-done((bf16[128,768]{1,0:T(8,128)(2,1)S(1)}, bf16[128,768]{1,0:T(8,128)(2,1)S(1)}, u32[]{:S(2)}, u32[]{:S(2)}) %collective-permute-start.3) | collective-permute-done | bytes 196640 | tf_op jit(solution)/shard_map/ppermute | solution.py:25
  69.8 1.9 %collective-permute-start.4 = (bf16[128,768]{1,0:T(8,128)(2,1)S(1)}, bf16[128,768]{1,0:T(8,128)(2,1)S(1)}, u32[]{:S(2)}, u32[]{:S(2)}) collective-permute-start(bf16[128,768]{1,0:T(8,128)(2,1)S(1)} %fusion.14), channel_id=1, source_target_pairs={{0,1},{1,0},{2,3},{3,2},{4,5},{5,4},{6,7},{7,6},{8,9},{9,8},{10,11... | collective-permute-start | bytes 589832 | tf_op jit(solution)/shard_map/ppermute | solution.py:25
  71.8 1.4 collective-permute-done.4
  73.2 2.8 %all-to-all-done.1 = bf16[8,96,640]{2,1,0:T(8,128)(2,1)S(1)} async-done(((bf16[8,96,640]{2,1,0:T(8,128)(2,1)}), bf16[8,96,640]{2,1,0:T(8,128)(2,1)S(1)}, u32[]{:S(2)}, u32[]{:S(2)}) %all-to-all-start.1) | async-done | bytes 983072 | tf_op jit(solution)/shard_map/all_to_all | solution.py:15
  76.0 1.9 %convolution_convert_fusion.3 = bf16[256,640]{1,0:T(8,128)(2,1)S(1)} fusion(bf16[256,768]{1,0:T(8,128)(2,1)S(1)} %pad_maximum_fusion, bf16[1,640,768]{2,1,0:T(8,128)(2,1)} %param.12, s32[256]{0:T(256)S(1)} %get-tuple-element.37, s32[256]{0:T(256)S(1)} %get-tuple-element.38, s32[256]{0:T(256)S(1)} %add_xor_fusion), kind=kOutput, calls=%fused_computation.14 | convolution fusion | flops 352878592 | bytes 1707008 | tf_op jit(solution)/shard_map/dot_general | solution.py:163
  78.0 1.9 %collective-permute-start.5 = (bf16[1,8,16,640]{3,2,1,0:T(8,128)(2,1)S(1)}, bf16[1,8,16,640]{3,2,1,0:T(8,128)(2,1)S(1)}, u32[]{:S(2)}, u32[]{:S(2)}) collective-permute-start(bf16[1,8,16,640]{3,2,1,0:T(8,128)(2,1)S(1)} %get-tuple-element.32), channel_id=1, source_target_pairs={{0,1},{1,0},{2,3},{3,2},{4,5},{5,4},{6,7},{7,6},{8,9},{9,8},{10,11... | collective-permute-start | bytes 491528 | tf_op jit(solution)/shard_map/ppermute | solution.py:25
  79.9 1.3 collective-permute-done.5
  81.3 1.8 %collective-permute-done.6 = bf16[128,5120]{1,0:T(8,128)(2,1)} collective-permute-done((bf16[128,5120]{1,0:T(8,128)(2,1)}, bf16[128,5120]{1,0:T(8,128)(2,1)}, u32[]{:S(2)}, u32[]{:S(2)}) %collective-permute-start.6) | collective-permute-done | bytes 1310752 | tf_op jit(solution)/shard_map/ppermute | solution.py:20
  83.2 3.6 %collective-permute-start.7 = (bf16[2,4,16,640]{3,2,1,0:T(8,128)(2,1)S(1)}, bf16[2,4,16,640]{3,2,1,0:T(8,128)(2,1)S(1)}, u32[]{:S(2)}, u32[]{:S(2)}) collective-permute-start(bf16[2,4,16,640]{3,2,1,0:T(8,128)(2,1)S(1)} %get-tuple-element.30), channel_id=1, source_target_pairs={{0,2},{1,3},{2,0},{3,1},{4,6},{5,7},{6,4},{7,5},{8,10},{9,11},{10,... | collective-permute-start | bytes 491528 | tf_op jit(solution)/shard_map/ppermute | solution.py:25
  86.8 0.5 convolution_convert_fusion
  87.4 1.0 copy.34
  88.4 6.9 %all-to-all-start.2 = ((bf16[8,96,640]{2,1,0:T(8,128)(2,1)}), bf16[8,96,640]{2,1,0:T(8,128)(2,1)}, u32[]{:S(2)}, u32[]{:S(2)}) async-start(bf16[8,96,640]{2,1,0:T(8,128)(2,1)} %bitcast.32), calls=%async_computation.2 | async-start | bytes 1966080 | tf_op jit(solution)/shard_map/all_to_all | solution.py:15
  95.4 2.8 %collective-permute-start.8 = (bf16[4,2,16,640]{3,2,1,0:T(8,128)(2,1)S(1)}, bf16[4,2,16,640]{3,2,1,0:T(8,128)(2,1)S(1)}, u32[]{:S(2)}, u32[]{:S(2)}) collective-permute-start(bf16[4,2,16,640]{3,2,1,0:T(8,128)(2,1)S(1)} %get-tuple-element.28), channel_id=1, source_target_pairs={{0,4},{1,5},{2,6},{3,7},{4,0},{5,1},{6,2},{7,3},{8,12},{9,13},{10,... | collective-permute-start | bytes 491528 | tf_op jit(solution)/shard_map/ppermute | solution.py:25
  98.3 7.1 %collective-permute-done.8 = bf16[4,2,16,640]{3,2,1,0:T(8,128)(2,1)S(1)} collective-permute-done((bf16[4,2,16,640]{3,2,1,0:T(8,128)(2,1)S(1)}, bf16[4,2,16,640]{3,2,1,0:T(8,128)(2,1)S(1)}, u32[]{:S(2)}, u32[]{:S(2)}) %collective-permute-start.8) | collective-permute-done | bytes 163872 | tf_op jit(solution)/shard_map/ppermute | solution.py:25
  105.5 3.3 %collective-permute-start.9 = (bf16[8,16,640]{2,1,0:T(8,128)(2,1)S(1)}, bf16[8,16,640]{2,1,0:T(8,128)(2,1)S(1)}, u32[]{:S(2)}, u32[]{:S(2)}) collective-permute-start(bf16[8,16,640]{2,1,0:T(8,128)(2,1)S(1)} %get-tuple-element.25), channel_id=1, source_target_pairs={{256,0},{257,1},{258,2},{259,3},{260,4},{261,5},{262,6},{263,7},{2... | collective-permute-start | bytes 491528 | tf_op jit(solution)/shard_map/ppermute | solution.py:81
  108.9 4.9 %collective-permute-start.10 = (bf16[8,16,640]{2,1,0:T(8,128)(2,1)S(1)}, bf16[8,16,640]{2,1,0:T(8,128)(2,1)S(1)}, u32[]{:S(2)}, u32[]{:S(2)}) collective-permute-start(bf16[8,16,640]{2,1,0:T(8,128)(2,1)S(1)} %get-tuple-element.26), channel_id=1, source_target_pairs={{256,8},{257,9},{258,10},{259,11},{260,12},{261,13},{262,14},{263,... | collective-permute-start | bytes 491528 | tf_op jit(solution)/shard_map/ppermute | solution.py:81
  113.8 8.2 %collective-permute-done.10 = bf16[8,16,640]{2,1,0:T(8,128)(2,1)S(1)} collective-permute-done((bf16[8,16,640]{2,1,0:T(8,128)(2,1)S(1)}, bf16[8,16,640]{2,1,0:T(8,128)(2,1)S(1)}, u32[]{:S(2)}, u32[]{:S(2)}) %collective-permute-start.10) | collective-permute-done | bytes 163872 | tf_op jit(solution)/shard_map/ppermute | solution.py:81
  122.1 0.3 copy.33
  122.4 0.4 broadcast_select_fusion
  123.1 0.2 reshape.235
  123.4 2.0 %fusion.53 = f32[128,5120]{1,0:T(8,128)} fusion(bf16[32,128]{1,0:T(8,128)(2,1)S(1)} %bitcast.115, bf16[32,5120]{1,0:T(8,128)(2,1)S(1)} %reshape.235), kind=kOutput, calls=%fused_computation.98 | convolution fusion | flops 41943040 | bytes 2957312 | tf_op jit(solution)/shard_map/dot_general | solution.py:187
  125.4 1.4 convert_reduce_fusion.1
  126.8 3.3 %collective-permute-start.11 = (bf16[2,48,640]{2,1,0:T(8,128)(2,1)S(1)}, bf16[2,48,640]{2,1,0:T(8,128)(2,1)S(1)}, u32[]{:S(2)}, u32[]{:S(2)}) collective-permute-start(bf16[2,48,640]{2,1,0:T(8,128)(2,1)S(1)} %pad_maximum_fusion.5), channel_id=1, source_target_pairs={{0,128},{16,144},{32,160},{48,176},{64,192},{80,208},{96,224},{112... | collective-permute-start | bytes 368648 | tf_op jit(solution)/shard_map/ppermute | solution.py:62
  130.1 3.4 %fusion.1 = bf16[1,128,5120]{2,1,0:T(8,128)(2,1)} fusion(f32[128,5120]{1,0:T(8,128)} %fusion.53, bf16[128,5120]{1,0:T(8,128)(2,1)} %collective-permute-done.6), kind=kLoop, calls=%fused_computation.12 | loop fusion | flops 1966080 | bytes 5242880 | tf_op jit(solution)/shard_map/broadcast_in_dim | solution.py:191
  133.5 5.3 %collective-permute-done.11 = bf16[2,48,640]{2,1,0:T(8,128)(2,1)S(1)} collective-permute-done((bf16[2,48,640]{2,1,0:T(8,128)(2,1)S(1)}, bf16[2,48,640]{2,1,0:T(8,128)(2,1)S(1)}, u32[]{:S(2)}, u32[]{:S(2)}) %collective-permute-start.11) | collective-permute-done | bytes 122912 | tf_op jit(solution)/shard_map/ppermute | solution.py:62
  138.8 0.7 add_convert_fusion.1
  (42 shorter events, 1.8 us)
Async XLA Ops:
  0.6 26.0 %copy-start = (bf16[1,768,640]{2,1,0:T(8,128)(2,1)S(1)}, bf16[1,768,640]{2,1,0:T(8,128)(2,1)}, u32[]{:S(2)}) copy-start(bf16[1,768,640]{2,1,0:T(8,128)(2,1)} %param.13) | copy-start | bytes 2949124
  5.8 24.4 %copy-start.1 = (bf16[1,1,1,256,768]{4,3,2,1,0:T(8,128)(2,1)S(1)}, bf16[1,1,1,256,768]{4,3,2,1,0:T(8,128)(2,1)}, u32[]{:S(2)}) copy-start(bf16[1,1,1,256,768]{4,3,2,1,0:T(8,128)(2,1)} %param.11) | copy-start | bytes 1179652
  6.6 20.1 %all-to-all-start = ((bf16[16,16,640]{2,1,0:T(8,128)(2,1)}), bf16[16,16,640]{2,1,0:T(8,128)(2,1)S(1)}, u32[]{:S(2)}, u32[]{:S(2)}) async-start(bf16[16,16,640]{2,1,0:T(8,128)(2,1)} %bitcast.8), calls=%async_computation | async-start | bytes 655360 | tf_op jit(solution)/shard_map/all_to_all | solution.py:15
  14.3 5.5 %collective-permute-start = (bf16[32,128]{1,0:T(8,128)(2,1)S(1)}, bf16[32,128]{1,0:T(8,128)(2,1)S(1)}, u32[]{:S(2)}, u32[]{:S(2)}) collective-permute-start(bf16[32,128]{1,0:T(8,128)(2,1)S(1)} %fusion.39), channel_id=1, source_target_pairs={{256,0},{512,256},{768,512},{257,1},{513,257},{769,513},{258,2},{5... | collective-permute-start | bytes 24584 | tf_op jit(solution)/shard_map/ppermute | solution.py:20
  27.2 21.3 %collective-permute-start.1 = (bf16[128,768]{1,0:T(8,128)(2,1)S(1)}, bf16[128,768]{1,0:T(8,128)(2,1)S(1)}, u32[]{:S(2)}, u32[]{:S(2)}) collective-permute-start(bf16[128,768]{1,0:T(8,128)(2,1)S(1)} %select_convert_fusion), channel_id=1, source_target_pairs={{0,1},{1,0},{2,3},{3,2},{4,5},{5,4},{6,7},{7,6},{8,9},{9,8},{10,11... | collective-permute-start | bytes 589832 | tf_op jit(solution)/shard_map/ppermute | solution.py:25
  31.8 44.2 %all-to-all-start.1 = ((bf16[8,96,640]{2,1,0:T(8,128)(2,1)}), bf16[8,96,640]{2,1,0:T(8,128)(2,1)S(1)}, u32[]{:S(2)}, u32[]{:S(2)}) async-start(bf16[8,96,640]{2,1,0:T(8,128)(2,1)} %bitcast.102), calls=%async_computation.1 | async-start | bytes 1966080 | tf_op jit(solution)/shard_map/all_to_all | solution.py:15
  48.6 8.4 %collective-permute-start.2 = (bf16[128,768]{1,0:T(8,128)(2,1)S(1)}, bf16[128,768]{1,0:T(8,128)(2,1)S(1)}, u32[]{:S(2)}, u32[]{:S(2)}) collective-permute-start(bf16[128,768]{1,0:T(8,128)(2,1)S(1)} %get-tuple-element.21), channel_id=1, source_target_pairs={{0,2},{1,3},{2,0},{3,1},{4,6},{5,7},{6,4},{7,5},{8,10},{9,11},{10,... | collective-permute-start | bytes 589832 | tf_op jit(solution)/shard_map/ppermute | solution.py:25
  50.5 32.6 %collective-permute-start.6 = (bf16[128,5120]{1,0:T(8,128)(2,1)}, bf16[128,5120]{1,0:T(8,128)(2,1)}, u32[]{:S(2)}, u32[]{:S(2)}) collective-permute-start(bf16[128,5120]{1,0:T(8,128)(2,1)} %bitcast.107), channel_id=1, source_target_pairs={{256,0},{512,256},{768,512},{257,1},{513,257},{769,513},{258,2},{5... | collective-permute-start | bytes 3932168 | tf_op jit(solution)/shard_map/ppermute | solution.py:20
  57.1 12.7 %collective-permute-start.3 = (bf16[128,768]{1,0:T(8,128)(2,1)S(1)}, bf16[128,768]{1,0:T(8,128)(2,1)S(1)}, u32[]{:S(2)}, u32[]{:S(2)}) collective-permute-start(bf16[128,768]{1,0:T(8,128)(2,1)S(1)} %fusion.17), channel_id=1, source_target_pairs={{0,4},{1,5},{2,6},{3,7},{4,0},{5,1},{6,2},{7,3},{8,12},{9,13},{10,... | collective-permute-start | bytes 589832 | tf_op jit(solution)/shard_map/ppermute | solution.py:25
  69.8 3.3 %collective-permute-start.4 = (bf16[128,768]{1,0:T(8,128)(2,1)S(1)}, bf16[128,768]{1,0:T(8,128)(2,1)S(1)}, u32[]{:S(2)}, u32[]{:S(2)}) collective-permute-start(bf16[128,768]{1,0:T(8,128)(2,1)S(1)} %fusion.14), channel_id=1, source_target_pairs={{0,1},{1,0},{2,3},{3,2},{4,5},{5,4},{6,7},{7,6},{8,9},{9,8},{10,11... | collective-permute-start | bytes 589832 | tf_op jit(solution)/shard_map/ppermute | solution.py:25
  76.0 10.8 %copy-start.2 = (bf16[1,1,256,640]{3,2,1,0:T(8,128)(2,1)S(1)}, bf16[1,1,256,640]{3,2,1,0:T(8,128)(2,1)}, u32[]{:S(2)}) copy-start(bf16[1,1,256,640]{3,2,1,0:T(8,128)(2,1)} %param.10) | copy-start | bytes 983044
  78.0 3.3 %collective-permute-start.5 = (bf16[1,8,16,640]{3,2,1,0:T(8,128)(2,1)S(1)}, bf16[1,8,16,640]{3,2,1,0:T(8,128)(2,1)S(1)}, u32[]{:S(2)}, u32[]{:S(2)}) collective-permute-start(bf16[1,8,16,640]{3,2,1,0:T(8,128)(2,1)S(1)} %get-tuple-element.32), channel_id=1, source_target_pairs={{0,1},{1,0},{2,3},{3,2},{4,5},{5,4},{6,7},{7,6},{8,9},{9,8},{10,11... | collective-permute-start | bytes 491528 | tf_op jit(solution)/shard_map/ppermute | solution.py:25
  83.2 12.1 %collective-permute-start.7 = (bf16[2,4,16,640]{3,2,1,0:T(8,128)(2,1)S(1)}, bf16[2,4,16,640]{3,2,1,0:T(8,128)(2,1)S(1)}, u32[]{:S(2)}, u32[]{:S(2)}) collective-permute-start(bf16[2,4,16,640]{3,2,1,0:T(8,128)(2,1)S(1)} %get-tuple-element.30), channel_id=1, source_target_pairs={{0,2},{1,3},{2,0},{3,1},{4,6},{5,7},{6,4},{7,5},{8,10},{9,11},{10,... | collective-permute-start | bytes 491528 | tf_op jit(solution)/shard_map/ppermute | solution.py:25
  88.4 37.0 %all-to-all-start.2 = ((bf16[8,96,640]{2,1,0:T(8,128)(2,1)}), bf16[8,96,640]{2,1,0:T(8,128)(2,1)}, u32[]{:S(2)}, u32[]{:S(2)}) async-start(bf16[8,96,640]{2,1,0:T(8,128)(2,1)} %bitcast.32), calls=%async_computation.2 | async-start | bytes 1966080 | tf_op jit(solution)/shard_map/all_to_all | solution.py:15
  95.4 10.1 %collective-permute-start.8 = (bf16[4,2,16,640]{3,2,1,0:T(8,128)(2,1)S(1)}, bf16[4,2,16,640]{3,2,1,0:T(8,128)(2,1)S(1)}, u32[]{:S(2)}, u32[]{:S(2)}) collective-permute-start(bf16[4,2,16,640]{3,2,1,0:T(8,128)(2,1)S(1)} %get-tuple-element.28), channel_id=1, source_target_pairs={{0,4},{1,5},{2,6},{3,7},{4,0},{5,1},{6,2},{7,3},{8,12},{9,13},{10,... | collective-permute-start | bytes 491528 | tf_op jit(solution)/shard_map/ppermute | solution.py:25
  105.5 8.3 %collective-permute-start.9 = (bf16[8,16,640]{2,1,0:T(8,128)(2,1)S(1)}, bf16[8,16,640]{2,1,0:T(8,128)(2,1)S(1)}, u32[]{:S(2)}, u32[]{:S(2)}) collective-permute-start(bf16[8,16,640]{2,1,0:T(8,128)(2,1)S(1)} %get-tuple-element.25), channel_id=1, source_target_pairs={{256,0},{257,1},{258,2},{259,3},{260,4},{261,5},{262,6},{263,7},{2... | collective-permute-start | bytes 491528 | tf_op jit(solution)/shard_map/ppermute | solution.py:81
  108.9 13.2 %collective-permute-start.10 = (bf16[8,16,640]{2,1,0:T(8,128)(2,1)S(1)}, bf16[8,16,640]{2,1,0:T(8,128)(2,1)S(1)}, u32[]{:S(2)}, u32[]{:S(2)}) collective-permute-start(bf16[8,16,640]{2,1,0:T(8,128)(2,1)S(1)} %get-tuple-element.26), channel_id=1, source_target_pairs={{256,8},{257,9},{258,10},{259,11},{260,12},{261,13},{262,14},{263,... | collective-permute-start | bytes 491528 | tf_op jit(solution)/shard_map/ppermute | solution.py:81
  126.8 12.0 %collective-permute-start.11 = (bf16[2,48,640]{2,1,0:T(8,128)(2,1)S(1)}, bf16[2,48,640]{2,1,0:T(8,128)(2,1)S(1)}, u32[]{:S(2)}, u32[]{:S(2)}) collective-permute-start(bf16[2,48,640]{2,1,0:T(8,128)(2,1)S(1)} %pad_maximum_fusion.5), channel_id=1, source_target_pairs={{0,128},{16,144},{32,160},{48,176},{64,192},{80,208},{96,224},{112... | collective-permute-start | bytes 368648 | tf_op jit(solution)/shard_map/ppermute | solution.py:62

commit v6 on v5

--- a/solution.py
+++ b/solution.py
@@ -1,6 +1,8 @@
 import jax
 import jax.numpy as jnp
 from jax import lax
+from jax.experimental import pallas as pl
+from jax.experimental.pallas import tpu as pltpu
 from jax.sharding import PartitionSpec as P
 
 
@@ -27,15 +29,6 @@
 
 def hold(*values):
     return lax.optimization_barrier(values)
-
-
-def slot_targets(chosen, experts, slots_per):
-    tokens = chosen.shape[0]
-    flat = chosen.reshape(-1)
-    onehot = (flat[:, None] == jnp.arange(experts, dtype=jnp.int32)[None, :]).astype(jnp.int32)
-    before = jnp.cumsum(onehot, axis=0) - onehot
-    slot = jnp.sum(before * onehot, axis=1)
-    return (flat * slots_per + slot).reshape(tokens, 2)
 
 
 def scatter_along_z(term):
@@ -54,11 +47,15 @@
     return jnp.sum(pieces.astype(jnp.float32), axis=0)
 
 
-def across_x(sums):
+def leaving_x(sums):
+    side = lax.axis_index("dp") // (lax.axis_size("dp") // 2)
+    return jnp.stack([jnp.where(side == 1, s[0], s[1]).astype(jnp.bfloat16) for s in sums])
+
+
+def across_x(sums, away):
     count = lax.axis_size("dp")
     near = count // 2
     side = lax.axis_index("dp") // near
-    away = jnp.stack([jnp.where(side == 1, s[0], s[1]).astype(jnp.bfloat16) for s in sums])
     got = lax.ppermute(away, "dp", [(i, (i + near) % count) for i in range(count)])
     return [
         (jnp.where(side == 1, s[1], s[0]) + got[i].astype(jnp.float32)).astype(jnp.bfloat16)
@@ -79,6 +76,39 @@
         (s * count + i, (s - 1) * count + (i ^ flip)) for s in range(1, sections) for i in range(count)
     ]
     return lax.ppermute(block, ("phase", "expert"), pairs)
+
+
+def combine_kernel(spot, grads, place, kept, got, out):
+    quarter = kept.shape[2]
+    odd = spot[0] & 1
+    for c in range(2):
+        columns = slice(c * quarter, (c + 1) * quarter)
+        rows = jnp.concatenate([kept[c ^ odd], got[c ^ odd]], axis=0)
+        added = jnp.dot(place[...], rows, preferred_element_type=jnp.float32)
+        out[:, columns] = (grads[:, columns].astype(jnp.float32) + added).astype(out.dtype)
+
+
+def combine(spot, grads, place, kept, got):
+    tokens, width = grads.shape
+    split, slots_per, quarter = kept.shape
+    wide = pl.BlockSpec((tokens, 2 * quarter), lambda i, spot: (0, i ^ (spot[0] >> 1)))
+    pair = pl.BlockSpec((2, slots_per, quarter), lambda i, spot: (i, 0, 0))
+    return pl.pallas_call(
+        combine_kernel,
+        grid_spec=pltpu.PrefetchScalarGridSpec(
+            num_scalar_prefetch=1,
+            grid=(split // 2,),
+            in_specs=[wide, pl.BlockSpec(place.shape, lambda i, spot: (0, 0)), pair, pair],
+            out_specs=wide,
+        ),
+        out_shape=jax.ShapeDtypeStruct(grads.shape, grads.dtype),
+        cost_estimate=pl.CostEstimate(
+            flops=4 * tokens * slots_per * width,
+            bytes_accessed=4 * tokens * width + 4 * slots_per * width,
+            transcendentals=0,
+        ),
+        name="combine",
+    )(spot.astype(jnp.int32).reshape(1), grads, place, kept, got)
 
 
 def body(grad_out, routes, gates, saved_in, saved_pre, w_up, w_down):
@@ -96,16 +126,19 @@
     levels = split.bit_length() - 1
     rows_all = count * slots_per
 
-    target = slot_targets(chosen, experts, slots_per)
-    slot_ids = jnp.arange(all_slots, dtype=jnp.int32)
-    hit = [(target[:, k][None, :] == slot_ids[:, None]) for k in range(2)]
-    place = (hit[0] | hit[1]).astype(jnp.bfloat16)
-    gate = jnp.sum(
-        jnp.where(hit[0], weights[:, 0][None, :], 0.0)
-        + jnp.where(hit[1], weights[:, 1][None, :], 0.0),
-        axis=1,
-        keepdims=True,
-    )
+    expert_ids = jnp.arange(experts, dtype=jnp.int32)[:, None]
+    slot_ids = jnp.arange(slots_per, dtype=jnp.int32)[None, :, None]
+    names = [chosen[:, k][None, :] == expert_ids for k in range(2)]
+    named = names[0] | names[1]
+    token_ids = jnp.arange(tokens, dtype=jnp.int32)
+    earlier = (token_ids[:, None] < token_ids[None, :]).astype(jnp.bfloat16)
+    slot = jnp.dot(
+        named.astype(jnp.bfloat16), earlier, preferred_element_type=jnp.float32
+    ).astype(jnp.int32)
+    hit = named[:, None, :] & (slot[:, None, :] == slot_ids)
+    place = hit.astype(jnp.bfloat16).reshape(all_slots, tokens)
+    pair_gate = jnp.where(names[0], weights[:, 0][None, :], weights[:, 1][None, :])
+    gate = jnp.sum(jnp.where(hit, pair_gate[:, None, :], 0.0), axis=2).reshape(all_slots, 1)
     picked = jnp.dot(place, grads, preferred_element_type=jnp.float32)
     packed = (gate * picked).astype(jnp.bfloat16)
     outgoing = (
@@ -127,12 +160,13 @@
     term_down = lax.dot_general(
         act, rows, (((0,), (0,)), ((), ())), preferred_element_type=jnp.float32
     ).astype(jnp.bfloat16)
-    down_pieces = scatter_along_z(term_down)
 
     core = position & 1
     half = rows_all // 2
     keep, away = split_by(core, partial_value[:half], partial_value[half:])
     value = keep + partner(away.astype(jnp.bfloat16), "expert", 0).astype(jnp.float32)
+    value, term_down = hold(value, term_down)
+    down_pieces = scatter_along_z(term_down)
     for level in range(1, levels):
         value = value + partner(value.astype(jnp.bfloat16), "expert", level).astype(jnp.float32)
     own_slope = jnp.where(core == 1, slope[half:], slope[:half])
@@ -142,7 +176,6 @@
         [jnp.where(core == 1, other_grad, own_grad), jnp.where(core == 1, own_grad, other_grad)],
         axis=0,
     )
-    hidden_grad, down_pieces = hold(hidden_grad, down_pieces)
     grads_after = to_previous(grads)
 
     term_up = lax.dot_general(
@@ -163,7 +196,6 @@
     back = lax.dot_general(
         ordered, w_up[0], (((1,), (1,)), ((), ())), preferred_element_type=jnp.float32
     ).astype(jnp.bfloat16)
-    up_pieces = scatter_along_z(term_up)
 
     buffer = back.reshape(1, count, slots_per, quarter)
     for level in range(levels):
@@ -171,24 +203,20 @@
         got = partner(buffer[:, middle:], "expert", level)
         buffer = jnp.concatenate([buffer[:, :middle], got], axis=0)
         if level == 0:
+            buffer, down_pieces, term_up = hold(buffer, down_pieces, term_up)
+            up_pieces = scatter_along_z(term_up)
+        if level == 1:
             buffer, grads_after = hold(buffer, grads_after)
     kept = behind(buffer[:, 0], 0)
     got = behind(buffer[:, 1], split)
-    blocks = jnp.stack([kept, got]).transpose(0, 2, 1, 3)
-    for level in range(levels):
-        shaped = blocks.reshape(
-            experts, slots_per, split >> (level + 1), 2, 1 << level, quarter
-        )
-        blocks = jnp.where((position >> level & 1) == 1, jnp.flip(shaped, 3), shaped)
-    unpacked = blocks.reshape(all_slots, width)
+    sums = [add_pieces(down_pieces), add_pieces(up_pieces)]
+    kept, got, away = hold(kept, got, leaving_x(sums))
     mine = position >> levels
     place_after = place_after.reshape(experts, slots_per, tokens)
     place_after = jnp.where(mine == 1, place_after[::-1], place_after).reshape(all_slots, tokens)
-    total = grads_after.astype(jnp.float32) + lax.dot_general(
-        place_after, unpacked, (((0,), (0,)), ((), ())), preferred_element_type=jnp.float32
-    )
-    down, up = across_x([add_pieces(down_pieces), add_pieces(up_pieces)])
-    return (total.astype(jnp.bfloat16)[None], up[None], down[None])
+    total = combine(position & (split - 1), grads_after, place_after.T, kept, got)
+    down, up = across_x(sums, away)
+    return (total[None], up[None], down[None])
 
 
 def solution(mesh):

time: 140 us -> 136 us (0.971)
  other arithmetic: 8.11 us -> 2.82 us
  Pallas kernels: 0 us -> 3.92 us
  starting transfers between devices: 67.5 us -> 64.7 us
    pallas_call x0 -> x1, Pallas kernels: none -> 3.92 us  [combine(): pl.pallas_call(combine_kernel, grid_spec=pltpu.PrefetchScalarGridSpec(num...]
    broadcast_in_dim x1 -> x0, other arithmetic: 3.42 us -> none  [body(): return (total.astype(jnp.bfloat16)[None], up[None], down[None])]
    all_to_all x3, starting transfers between devices: 31.3 us -> 27.9 us  [exchange(): return lax.all_to_all(x, axis, 0, 0, tiled=True, axis_index_groups=groups)]
    all_to_all x3, waiting for transfers between devices: 9.66 us -> 11.8 us  [exchange(): return lax.all_to_all(x, axis, 0, 0, tiled=True, axis_index_groups=groups)]
    dot_general x1, matrix products: 2.02 us -> 0.13 us  [body(): jnp.dot(named.astype(jnp.bfloat16), earlier, preferred_element_type=jnp.f...]
    ppermute x2, waiting for transfers between devices: 4.03 us -> 2.19 us  [to_previous(): return lax.ppermute(x, 'phase', [(i, i - 1) for i in range(1, peers)])]
    ppermute x7, starting transfers between devices: 18 us -> 19.7 us  [partner(): return lax.ppermute(block, axis, [(i, i ^ 1 << bit) for i in range(count)])]
    ppermute x7, waiting for transfers between devices: 22.5 us -> 24 us  [partner(): return lax.ppermute(block, axis, [(i, i ^ 1 << bit) for i in range(count)])]
  transfers between devices with their start and end apart: 15 -> 15, of which waited for: 11 -> 10; matrix products, arithmetic and copies ran while one was open for 9% -> 7% of each run, Pallas kernels for 0% -> 3%
where the time goes in v6:
time: 136 us; the launch traced here: 135 us
  starting transfers between devices  64.7 us (48%)
  waiting for transfers between devices  50 us (37%)
  matrix products  6.19 us (5%)
  local copies, waits for them, and re-layouts  6.08 us (4%)
  Pallas kernels  3.92 us (3%)
  other arithmetic  2.82 us (2%)
    all_to_all x3, starting transfers between devices, exchange(): return lax.all_to_all(x, axis, 0, 0, tiled=True, axis_index_groups=groups)  27.9 us
    ppermute x7, waiting for transfers between devices, partner(): return lax.ppermute(block, axis, [(i, i ^ 1 << bit) for i in range(count)])  24 us
    ppermute x7, starting transfers between devices, partner(): return lax.ppermute(block, axis, [(i, i ^ 1 << bit) for i in range(count)])  19.7 us
    all_to_all x3, waiting for transfers between devices, exchange(): return lax.all_to_all(x, axis, 0, 0, tiled=True, axis_index_groups=groups)  11.8 us
    ppermute x2, waiting for transfers between devices, behind(): return lax.ppermute(block, ('phase', 'expert'), pairs)  7.74 us
    ppermute x2, starting transfers between devices, behind(): return lax.ppermute(block, ('phase', 'expert'), pairs)  7.15 us
    ppermute x2, starting transfers between devices, to_previous(): return lax.ppermute(x, 'phase', [(i, i - 1) for i in range(1, peers)])  6.71 us
    ppermute x1, waiting for transfers between devices, across_x(): lax.ppermute(away, 'dp', [(i, (i + near) % count) for i in range(count)])  4.29 us
  transfers between devices with their start and end apart: 15, of which 10 were waited for; matrix products, arithmetic and copies ran while one was open for 7% of the time, Pallas kernels for 3%

profile of v6, /device:TPU:12, one launch (start us, length us, event | category | flops | bytes accessed | tf_op | source)
XLA Modules:
  0.0 134.7 jit_solution(11187568319797422690)
XLA Ops:
  0.6 0.8 slice_bitcast_fusion.3
  1.4 0.1 convolution_convert_fusion.4
  1.6 0.8 slice_bitcast_fusion.1
  2.4 0.1 select_reduce_fusion
  2.4 0.1 mul.46
  2.5 1.6 %fusion = bf16[32,5120]{1,0:T(8,128)(2,1)S(1)} fusion(pred[32,128]{1,0:T(8,128)(4,1)S(1)} %bitcast.95, f32[32]{0:T(128)S(1)} %mul.46, bf16[1,128,5120]{2,1,0:T(8,128)(2,1)} %param.7), kind=kOutput, calls=%fused_computation.1 | convolution fusion | flops 42270720 | bytes 1642624 | tf_op jit(solution)/shard_map/dot_general | solution.py:142
  4.2 0.8 copy.11
  5.0 0.1 eq.139
  5.1 7.7 %all-to-all-start = ((bf16[16,16,640]{2,1,0:T(8,128)(2,1)}), bf16[16,16,640]{2,1,0:T(8,128)(2,1)S(1)}, u32[]{:S(2)}, u32[]{:S(2)}) async-start(bf16[16,16,640]{2,1,0:T(8,128)(2,1)} %bitcast.13), calls=%async_computation | async-start | bytes 655360 | tf_op jit(solution)/shard_map/all_to_all | solution.py:17
  12.8 3.3 %collective-permute-start = (bf16[32,128]{1,0:T(8,128)(2,1)S(1)}, bf16[32,128]{1,0:T(8,128)(2,1)S(1)}, u32[]{:S(2)}, u32[]{:S(2)}) collective-permute-start(bf16[32,128]{1,0:T(8,128)(2,1)S(1)} %fusion.38), channel_id=1, source_target_pairs={{256,0},{512,256},{768,512},{257,1},{513,257},{769,513},{258,2},{5... | collective-permute-start | bytes 24584 | tf_op jit(solution)/shard_map/ppermute | solution.py:22
  16.2 2.2 %collective-permute-done = bf16[32,128]{1,0:T(8,128)(2,1)S(1)} collective-permute-done((bf16[32,128]{1,0:T(8,128)(2,1)S(1)}, bf16[32,128]{1,0:T(8,128)(2,1)S(1)}, u32[]{:S(2)}, u32[]{:S(2)}) %collective-permute-start) | collective-permute-done | bytes 8224 | tf_op jit(solution)/shard_map/ppermute | solution.py:22
  18.3 6.9 %all-to-all-done = bf16[16,16,640]{2,1,0:T(8,128)(2,1)S(1)} async-done(((bf16[16,16,640]{2,1,0:T(8,128)(2,1)}), bf16[16,16,640]{2,1,0:T(8,128)(2,1)S(1)}, u32[]{:S(2)}, u32[]{:S(2)}) %all-to-all-start) | async-done | bytes 327712 | tf_op jit(solution)/shard_map/all_to_all | solution.py:17
  25.2 0.5 fusion.2
  25.8 3.0 %collective-permute-start.1 = (bf16[128,768]{1,0:T(8,128)(2,1)S(1)}, bf16[128,768]{1,0:T(8,128)(2,1)S(1)}, u32[]{:S(2)}, u32[]{:S(2)}) collective-permute-start(bf16[128,768]{1,0:T(8,128)(2,1)S(1)} %select_convert_fusion), channel_id=1, source_target_pairs={{0,1},{1,0},{2,3},{3,2},{4,5},{5,4},{6,7},{7,6},{8,9},{9,8},{10,11... | collective-permute-start | bytes 589832 | tf_op jit(solution)/shard_map/ppermute | solution.py:27
  28.8 0.6 convolution_convert_fusion.1
  29.3 0.5 collective-permute-done.1
  29.9 1.9 %collective-permute-start.2 = (bf16[128,768]{1,0:T(8,128)(2,1)S(1)}, bf16[128,768]{1,0:T(8,128)(2,1)S(1)}, u32[]{:S(2)}, u32[]{:S(2)}) collective-permute-start(bf16[128,768]{1,0:T(8,128)(2,1)S(1)} %convert_element_type.101), channel_id=1, source_target_pairs={{0,2},{1,3},{2,0},{3,1},{4,6},{5,7},{6,4},{7,5},{8,10},{9,11},{10,... | collective-permute-start | bytes 589832 | tf_op jit(solution)/shard_map/ppermute | solution.py:27
  31.8 3.4 %collective-permute-start.7 = (bf16[128,5120]{1,0:T(8,128)(2,1)}, bf16[128,5120]{1,0:T(8,128)(2,1)}, u32[]{:S(2)}, u32[]{:S(2)}) collective-permute-start(bf16[128,5120]{1,0:T(8,128)(2,1)} %bitcast.8), channel_id=1, source_target_pairs={{256,0},{512,256},{768,512},{257,1},{513,257},{769,513},{258,2},{5... | collective-permute-start | bytes 3932168 | tf_op jit(solution)/shard_map/ppermute | solution.py:22
  35.2 1.0 copy.12
  36.2 16.7 %all-to-all-start.1 = ((bf16[8,96,640]{2,1,0:T(8,128)(2,1)}), bf16[8,96,640]{2,1,0:T(8,128)(2,1)S(1)}, u32[]{:S(2)}, u32[]{:S(2)}) async-start(bf16[8,96,640]{2,1,0:T(8,128)(2,1)} %bitcast.22), calls=%async_computation.1 | async-start | bytes 1966080 | tf_op jit(solution)/shard_map/all_to_all | solution.py:17
  53.0 3.9 %collective-permute-start.3 = (bf16[128,768]{1,0:T(8,128)(2,1)S(1)}, bf16[128,768]{1,0:T(8,128)(2,1)S(1)}, u32[]{:S(2)}, u32[]{:S(2)}) collective-permute-start(bf16[128,768]{1,0:T(8,128)(2,1)S(1)} %fusion.16), channel_id=1, source_target_pairs={{0,4},{1,5},{2,6},{3,7},{4,0},{5,1},{6,2},{7,3},{8,12},{9,13},{10,... | collective-permute-start | bytes 589832 | tf_op jit(solution)/shard_map/ppermute | solution.py:27
  56.8 0.3 fusion.10
  57.1 9.4 %collective-permute-done.3 = bf16[128,768]{1,0:T(8,128)(2,1)S(1)} collective-permute-done((bf16[128,768]{1,0:T(8,128)(2,1)S(1)}, bf16[128,768]{1,0:T(8,128)(2,1)S(1)}, u32[]{:S(2)}, u32[]{:S(2)}) %collective-permute-start.3) | collective-permute-done | bytes 196640 | tf_op jit(solution)/shard_map/ppermute | solution.py:27
  66.6 0.1 fusion.13
  66.7 1.9 %collective-permute-start.4 = (bf16[128,768]{1,0:T(8,128)(2,1)S(1)}, bf16[128,768]{1,0:T(8,128)(2,1)S(1)}, u32[]{:S(2)}, u32[]{:S(2)}) collective-permute-start(bf16[128,768]{1,0:T(8,128)(2,1)S(1)} %fusion.13), channel_id=1, source_target_pairs={{0,1},{1,0},{2,3},{3,2},{4,5},{5,4},{6,7},{7,6},{8,9},{9,8},{10,11... | collective-permute-start | bytes 589832 | tf_op jit(solution)/shard_map/ppermute | solution.py:27
  68.6 1.4 %collective-permute-done.4 = bf16[128,768]{1,0:T(8,128)(2,1)S(1)} collective-permute-done((bf16[128,768]{1,0:T(8,128)(2,1)S(1)}, bf16[128,768]{1,0:T(8,128)(2,1)S(1)}, u32[]{:S(2)}, u32[]{:S(2)}) %collective-permute-start.4) | collective-permute-done | bytes 196640 | tf_op jit(solution)/shard_map/ppermute | solution.py:27
  70.0 1.9 %convolution_convert_fusion.3 = bf16[256,640]{1,0:T(8,128)(2,1)S(1)} fusion(bf16[1,640,768]{2,1,0:T(8,128)(2,1)} %param.12, bf16[128,768]{1,0:T(8,128)(2,1)S(1)} %get-tuple-element.32, bf16[128,768]{1,0:T(8,128)(2,1)S(1)} %get-tuple-element.31, s32[256]{0:T(256)S(1)} %get-tuple-element.47, s32[256]{0:T(256)S(1)} %get-tuple-element.48, s32[256]{0:T(256)S(1)} %add_xor_fusion), kind=kOutput, calls=%fused_computation.12 | convolution fusion | flops 353665024 | bytes 1707008 | tf_op jit(solution)/shard_map/dot_general | solution.py:196
  71.9 2.1 %collective-permute-start.5 = (bf16[1,8,16,640]{3,2,0,1:T(8,128)(2,1)S(1)}, bf16[1,8,16,640]{3,2,0,1:T(8,128)(2,1)S(1)}, u32[]{:S(2)}, u32[]{:S(2)}) collective-permute-start(bf16[1,8,16,640]{3,2,0,1:T(8,128)(2,1)S(1)} %get-tuple-element.40), channel_id=1, source_target_pairs={{0,1},{1,0},{2,3},{3,2},{4,5},{5,4},{6,7},{7,6},{8,9},{9,8},{10,11... | collective-permute-start | bytes 491528 | tf_op jit(solution)/shard_map/ppermute | solution.py:27
  74.0 1.5 %convolution_convert_fusion = bf16[768,640]{1,0:T(8,128)(2,1)S(1)} fusion(bf16[1,1,256,640]{3,2,1,0:T(8,128)(2,1)} %param.10, bf16[128,768]{1,0:T(8,128)(2,1)S(1)} %get-tuple-element.32, bf16[128,768]{1,0:T(8,128)(2,1)S(1)} %get-tuple-element.31), kind=kOutput, calls=%fused_computation.9 | convolution fusion | flops 252936192 | bytes 1703936 | tf_op jit(solution)/shard_map/dot_general | solution.py:181
  75.5 4.9 %all-to-all-done.1 = bf16[8,96,640]{2,1,0:T(8,128)(2,1)S(1)} async-done(((bf16[8,96,640]{2,1,0:T(8,128)(2,1)}), bf16[8,96,640]{2,1,0:T(8,128)(2,1)S(1)}, u32[]{:S(2)}, u32[]{:S(2)}) %all-to-all-start.1) | async-done | bytes 983072 | tf_op jit(solution)/shard_map/all_to_all | solution.py:17
  80.5 1.0 copy.14
  81.5 3.6 %all-to-all-start.2 = ((bf16[8,96,640]{2,1,0:T(8,128)(2,1)}), bf16[8,96,640]{2,1,0:T(8,128)(2,1)S(1)}, u32[]{:S(2)}, u32[]{:S(2)}) async-start(bf16[8,96,640]{2,1,0:T(8,128)(2,1)} %bitcast.84), calls=%async_computation.2 | async-start | bytes 1966080 | tf_op jit(solution)/shard_map/all_to_all | solution.py:17
  85.1 0.7 fusion.48
  85.8 3.6 %collective-permute-start.6 = (bf16[2,4,16,640]{3,2,0,1:T(8,128)(2,1)}, bf16[2,4,16,640]{3,2,0,1:T(8,128)(2,1)}, u32[]{:S(2)}, u32[]{:S(2)}) collective-permute-start(bf16[2,4,16,640]{3,2,0,1:T(8,128)(2,1)} %get-tuple-element.38), channel_id=1, source_target_pairs={{0,2},{1,3},{2,0},{3,1},{4,6},{5,7},{6,4},{7,5},{8,10},{9,11},{10,... | collective-permute-start | bytes 491528 | tf_op jit(solution)/shard_map/ppermute | solution.py:27
  89.4 0.1 convert_reduce_fusion
  89.6 4.5 %collective-permute-done.6 = bf16[2,4,16,640]{3,2,0,1:T(8,128)(2,1)} collective-permute-done((bf16[2,4,16,640]{3,2,0,1:T(8,128)(2,1)}, bf16[2,4,16,640]{3,2,0,1:T(8,128)(2,1)}, u32[]{:S(2)}, u32[]{:S(2)}) %collective-permute-start.6) | collective-permute-done | bytes 163872 | tf_op jit(solution)/shard_map/ppermute | solution.py:27
  94.1 1.0 pad_maximum_fusion.2
  95.1 3.4 %collective-permute-start.8 = (bf16[4,2,16,640]{3,2,0,1:T(8,128)(2,1)S(1)}, bf16[4,2,16,640]{3,2,0,1:T(8,128)(2,1)S(1)}, u32[]{:S(2)}, u32[]{:S(2)}) collective-permute-start(bf16[4,2,16,640]{3,2,0,1:T(8,128)(2,1)S(1)} %get-tuple-element.35), channel_id=1, source_target_pairs={{0,4},{1,5},{2,6},{3,7},{4,0},{5,1},{6,2},{7,3},{8,12},{9,13},{10,... | collective-permute-start | bytes 491528 | tf_op jit(solution)/shard_map/ppermute | solution.py:27
  98.5 8.2 %collective-permute-done.8 = bf16[4,2,16,640]{3,2,0,1:T(8,128)(2,1)S(1)} collective-permute-done((bf16[4,2,16,640]{3,2,0,1:T(8,128)(2,1)S(1)}, bf16[4,2,16,640]{3,2,0,1:T(8,128)(2,1)S(1)}, u32[]{:S(2)}, u32[]{:S(2)}) %collective-permute-start.8) | collective-permute-done | bytes 163872 | tf_op jit(solution)/shard_map/ppermute | solution.py:27
  106.7 5.2 %collective-permute-start.10 = (bf16[8,16,640]{2,1,0:T(8,128)(2,1)S(1)}, bf16[8,16,640]{2,1,0:T(8,128)(2,1)S(1)}, u32[]{:S(2)}, u32[]{:S(2)}) collective-permute-start(bf16[8,16,640]{2,1,0:T(8,128)(2,1)S(1)} %get-tuple-element.33), channel_id=1, source_target_pairs={{256,8},{257,9},{258,10},{259,11},{260,12},{261,13},{262,14},{263,... | collective-permute-start | bytes 491528 | tf_op jit(solution)/shard_map/ppermute | solution.py:78
  111.9 1.9 %collective-permute-start.9 = (bf16[8,16,640]{2,1,0:T(8,128)(2,1)S(1)}, bf16[8,16,640]{2,1,0:T(8,128)(2,1)S(1)}, u32[]{:S(2)}, u32[]{:S(2)}) collective-permute-start(bf16[8,16,640]{2,1,0:T(8,128)(2,1)S(1)} %get-tuple-element.34), channel_id=1, source_target_pairs={{256,0},{257,1},{258,2},{259,3},{260,4},{261,5},{262,6},{263,7},{2... | collective-permute-start | bytes 491528 | tf_op jit(solution)/shard_map/ppermute | solution.py:78
  113.9 0.1 convert_reduce_fusion.1
  114.1 7.7 %collective-permute-done.10.got = bf16[8,16,640]{2,1,0:T(8,128)(2,1)S(1)} collective-permute-done((bf16[8,16,640]{2,1,0:T(8,128)(2,1)S(1)}, bf16[8,16,640]{2,1,0:T(8,128)(2,1)S(1)}, u32[]{:S(2)}, u32[]{:S(2)}) %collective-permute-start.10) | collective-permute-done | bytes 163872 | tf_op jit(solution)/shard_map/ppermute | solution.py:78
  121.8 3.3 %collective-permute-start.11 = (bf16[2,48,640]{2,1,0:T(8,128)(2,1)S(1)}, bf16[2,48,640]{2,1,0:T(8,128)(2,1)S(1)}, u32[]{:S(2)}, u32[]{:S(2)}) collective-permute-start(bf16[2,48,640]{2,1,0:T(8,128)(2,1)S(1)} %pad_maximum_fusion.7), channel_id=1, source_target_pairs={{0,128},{16,144},{32,160},{48,176},{64,192},{80,208},{96,224},{112... | collective-permute-start | bytes 368648 | tf_op jit(solution)/shard_map/ppermute | solution.py:59
  125.1 0.7 copy.13
  125.8 3.9 %combine.1 = bf16[128,5120]{1,0:T(8,128)(2,1)} custom-call(s32[1]{0:T(128)} %bitcast.spot, bf16[128,5120]{1,0:T(8,128)(2,1)} %collective-permute-done.7.grads, bf16[128,32]{1,0:T(8,128)(2,1)} %bitcast.93, bf16[8,16,640]{2,1,0:T(8,128)(2,1)} %copy-done.3, bf16[8,16,640]{2,1,0:T(8,128)(2,1)} %copy-done.2), custom_call_target="tpu_custom_call" | custom-call | flops 41943040 | bytes 2949120 | tf_op jit(solution)/shard_map/combine/pallas_call | solution.py:96
  129.7 4.3 %collective-permute-done.11 = bf16[2,48,640]{2,1,0:T(8,128)(2,1)S(1)} collective-permute-done((bf16[2,48,640]{2,1,0:T(8,128)(2,1)S(1)}, bf16[2,48,640]{2,1,0:T(8,128)(2,1)S(1)}, u32[]{:S(2)}, u32[]{:S(2)}) %collective-permute-start.11) | collective-permute-done | bytes 122912 | tf_op jit(solution)/shard_map/ppermute | solution.py:59
  134.0 0.7 add_convert_fusion
  (34 shorter events, 0.6 us)
Async XLA Ops:
  0.6 24.6 %copy-start = (bf16[1,768,640]{2,1,0:T(8,128)(2,1)S(1)}, bf16[1,768,640]{2,1,0:T(8,128)(2,1)}, u32[]{:S(2)}) copy-start(bf16[1,768,640]{2,1,0:T(8,128)(2,1)} %param.13) | copy-start | bytes 2949124
  5.1 20.1 %all-to-all-start = ((bf16[16,16,640]{2,1,0:T(8,128)(2,1)}), bf16[16,16,640]{2,1,0:T(8,128)(2,1)S(1)}, u32[]{:S(2)}, u32[]{:S(2)}) async-start(bf16[16,16,640]{2,1,0:T(8,128)(2,1)} %bitcast.13), calls=%async_computation | async-start | bytes 655360 | tf_op jit(solution)/shard_map/all_to_all | solution.py:17
  12.8 5.5 %collective-permute-start = (bf16[32,128]{1,0:T(8,128)(2,1)S(1)}, bf16[32,128]{1,0:T(8,128)(2,1)S(1)}, u32[]{:S(2)}, u32[]{:S(2)}) collective-permute-start(bf16[32,128]{1,0:T(8,128)(2,1)S(1)} %fusion.38), channel_id=1, source_target_pairs={{256,0},{512,256},{768,512},{257,1},{513,257},{769,513},{258,2},{5... | collective-permute-start | bytes 24584 | tf_op jit(solution)/shard_map/ppermute | solution.py:22
  25.2 3.6 %copy-start.1 = (bf16[1,1,1,256,768]{4,3,2,1,0:T(8,128)(2,1)S(1)}, bf16[1,1,1,256,768]{4,3,2,1,0:T(8,128)(2,1)}, u32[]{:S(2)}) copy-start(bf16[1,1,1,256,768]{4,3,2,1,0:T(8,128)(2,1)} %param.11) | copy-start | bytes 1179652
  25.8 4.0 %collective-permute-start.1 = (bf16[128,768]{1,0:T(8,128)(2,1)S(1)}, bf16[128,768]{1,0:T(8,128)(2,1)S(1)}, u32[]{:S(2)}, u32[]{:S(2)}) collective-permute-start(bf16[128,768]{1,0:T(8,128)(2,1)S(1)} %select_convert_fusion), channel_id=1, source_target_pairs={{0,1},{1,0},{2,3},{3,2},{4,5},{5,4},{6,7},{7,6},{8,9},{9,8},{10,11... | collective-permute-start | bytes 589832 | tf_op jit(solution)/shard_map/ppermute | solution.py:27
  29.9 23.0 %collective-permute-start.2 = (bf16[128,768]{1,0:T(8,128)(2,1)S(1)}, bf16[128,768]{1,0:T(8,128)(2,1)S(1)}, u32[]{:S(2)}, u32[]{:S(2)}) collective-permute-start(bf16[128,768]{1,0:T(8,128)(2,1)S(1)} %convert_element_type.101), channel_id=1, source_target_pairs={{0,2},{1,3},{2,0},{3,1},{4,6},{5,7},{6,4},{7,5},{8,10},{9,11},{10,... | collective-permute-start | bytes 589832 | tf_op jit(solution)/shard_map/ppermute | solution.py:27
  31.8 63.2 %collective-permute-start.7 = (bf16[128,5120]{1,0:T(8,128)(2,1)}, bf16[128,5120]{1,0:T(8,128)(2,1)}, u32[]{:S(2)}, u32[]{:S(2)}) collective-permute-start(bf16[128,5120]{1,0:T(8,128)(2,1)} %bitcast.8), channel_id=1, source_target_pairs={{256,0},{512,256},{768,512},{257,1},{513,257},{769,513},{258,2},{5... | collective-permute-start | bytes 3932168 | tf_op jit(solution)/shard_map/ppermute | solution.py:22
  36.2 44.2 %all-to-all-start.1 = ((bf16[8,96,640]{2,1,0:T(8,128)(2,1)}), bf16[8,96,640]{2,1,0:T(8,128)(2,1)S(1)}, u32[]{:S(2)}, u32[]{:S(2)}) async-start(bf16[8,96,640]{2,1,0:T(8,128)(2,1)} %bitcast.22), calls=%async_computation.1 | async-start | bytes 1966080 | tf_op jit(solution)/shard_map/all_to_all | solution.py:17
  53.0 13.6 %collective-permute-start.3 = (bf16[128,768]{1,0:T(8,128)(2,1)S(1)}, bf16[128,768]{1,0:T(8,128)(2,1)S(1)}, u32[]{:S(2)}, u32[]{:S(2)}) collective-permute-start(bf16[128,768]{1,0:T(8,128)(2,1)S(1)} %fusion.16), channel_id=1, source_target_pairs={{0,4},{1,5},{2,6},{3,7},{4,0},{5,1},{6,2},{7,3},{8,12},{9,13},{10,... | collective-permute-start | bytes 589832 | tf_op jit(solution)/shard_map/ppermute | solution.py:27
  66.7 3.3 %collective-permute-start.4 = (bf16[128,768]{1,0:T(8,128)(2,1)S(1)}, bf16[128,768]{1,0:T(8,128)(2,1)S(1)}, u32[]{:S(2)}, u32[]{:S(2)}) collective-permute-start(bf16[128,768]{1,0:T(8,128)(2,1)S(1)} %fusion.13), channel_id=1, source_target_pairs={{0,1},{1,0},{2,3},{3,2},{4,5},{5,4},{6,7},{7,6},{8,9},{9,8},{10,11... | collective-permute-start | bytes 589832 | tf_op jit(solution)/shard_map/ppermute | solution.py:27
  71.9 3.5 %collective-permute-start.5 = (bf16[1,8,16,640]{3,2,0,1:T(8,128)(2,1)S(1)}, bf16[1,8,16,640]{3,2,0,1:T(8,128)(2,1)S(1)}, u32[]{:S(2)}, u32[]{:S(2)}) collective-permute-start(bf16[1,8,16,640]{3,2,0,1:T(8,128)(2,1)S(1)} %get-tuple-element.40), channel_id=1, source_target_pairs={{0,1},{1,0},{2,3},{3,2},{4,5},{5,4},{6,7},{7,6},{8,9},{9,8},{10,11... | collective-permute-start | bytes 491528 | tf_op jit(solution)/shard_map/ppermute | solution.py:27
  81.5 32.4 %all-to-all-start.2 = ((bf16[8,96,640]{2,1,0:T(8,128)(2,1)}), bf16[8,96,640]{2,1,0:T(8,128)(2,1)S(1)}, u32[]{:S(2)}, u32[]{:S(2)}) async-start(bf16[8,96,640]{2,1,0:T(8,128)(2,1)} %bitcast.84), calls=%async_computation.2 | async-start | bytes 1966080 | tf_op jit(solution)/shard_map/all_to_all | solution.py:17
  85.8 8.3 %collective-permute-start.6 = (bf16[2,4,16,640]{3,2,0,1:T(8,128)(2,1)}, bf16[2,4,16,640]{3,2,0,1:T(8,128)(2,1)}, u32[]{:S(2)}, u32[]{:S(2)}) collective-permute-start(bf16[2,4,16,640]{3,2,0,1:T(8,128)(2,1)} %get-tuple-element.38), channel_id=1, source_target_pairs={{0,2},{1,3},{2,0},{3,1},{4,6},{5,7},{6,4},{7,5},{8,10},{9,11},{10,... | collective-permute-start | bytes 491528 | tf_op jit(solution)/shard_map/ppermute | solution.py:27
  95.1 11.6 %collective-permute-start.8 = (bf16[4,2,16,640]{3,2,0,1:T(8,128)(2,1)S(1)}, bf16[4,2,16,640]{3,2,0,1:T(8,128)(2,1)S(1)}, u32[]{:S(2)}, u32[]{:S(2)}) collective-permute-start(bf16[4,2,16,640]{3,2,0,1:T(8,128)(2,1)S(1)} %get-tuple-element.35), channel_id=1, source_target_pairs={{0,4},{1,5},{2,6},{3,7},{4,0},{5,1},{6,2},{7,3},{8,12},{9,13},{10,... | collective-permute-start | bytes 491528 | tf_op jit(solution)/shard_map/ppermute | solution.py:27
  106.7 15.1 %collective-permute-start.10 = (bf16[8,16,640]{2,1,0:T(8,128)(2,1)S(1)}, bf16[8,16,640]{2,1,0:T(8,128)(2,1)S(1)}, u32[]{:S(2)}, u32[]{:S(2)}) collective-permute-start(bf16[8,16,640]{2,1,0:T(8,128)(2,1)S(1)} %get-tuple-element.33), channel_id=1, source_target_pairs={{256,8},{257,9},{258,10},{259,11},{260,12},{261,13},{262,14},{263,... | collective-permute-start | bytes 491528 | tf_op jit(solution)/shard_map/ppermute | solution.py:78
  111.9 9.9 %collective-permute-start.9 = (bf16[8,16,640]{2,1,0:T(8,128)(2,1)S(1)}, bf16[8,16,640]{2,1,0:T(8,128)(2,1)S(1)}, u32[]{:S(2)}, u32[]{:S(2)}) collective-permute-start(bf16[8,16,640]{2,1,0:T(8,128)(2,1)S(1)} %get-tuple-element.34), channel_id=1, source_target_pairs={{256,0},{257,1},{258,2},{259,3},{260,4},{261,5},{262,6},{263,7},{2... | collective-permute-start | bytes 491528 | tf_op jit(solution)/shard_map/ppermute | solution.py:78
  121.8 4.0 %copy-start.2 = (bf16[8,16,640]{2,1,0:T(8,128)(2,1)}, bf16[8,16,640]{2,1,0:T(8,128)(2,1)S(1)}, u32[]{:S(2)}) copy-start(bf16[8,16,640]{2,1,0:T(8,128)(2,1)S(1)} %collective-permute-done.10.got) | copy-start | bytes 491524
  121.8 4.0 %copy-start.3 = (bf16[8,16,640]{2,1,0:T(8,128)(2,1)}, bf16[8,16,640]{2,1,0:T(8,128)(2,1)S(1)}, u32[]{:S(2)}) copy-start(bf16[8,16,640]{2,1,0:T(8,128)(2,1)S(1)} %collective-permute-done.9.kept) | copy-start | bytes 491524
  121.8 12.2 %collective-permute-start.11 = (bf16[2,48,640]{2,1,0:T(8,128)(2,1)S(1)}, bf16[2,48,640]{2,1,0:T(8,128)(2,1)S(1)}, u32[]{:S(2)}, u32[]{:S(2)}) collective-permute-start(bf16[2,48,640]{2,1,0:T(8,128)(2,1)S(1)} %pad_maximum_fusion.7), channel_id=1, source_target_pairs={{0,128},{16,144},{32,160},{48,176},{64,192},{80,208},{96,224},{112... | collective-permute-start | bytes 368648 | tf_op jit(solution)/shard_map/ppermute | solution.py:59

commit v7 on v6

--- a/solution.py
+++ b/solution.py
@@ -52,11 +52,13 @@
     return jnp.stack([jnp.where(side == 1, s[0], s[1]).astype(jnp.bfloat16) for s in sums])
 
 
-def across_x(sums, away):
+def across_x(away):
     count = lax.axis_size("dp")
-    near = count // 2
-    side = lax.axis_index("dp") // near
-    got = lax.ppermute(away, "dp", [(i, (i + near) % count) for i in range(count)])
+    return lax.ppermute(away, "dp", [(i, (i + count // 2) % count) for i in range(count)])
+
+
+def staying_x(sums, got):
+    side = lax.axis_index("dp") // (lax.axis_size("dp") // 2)
     return [
         (jnp.where(side == 1, s[1], s[0]) + got[i].astype(jnp.float32)).astype(jnp.bfloat16)
         for i, s in enumerate(sums)
@@ -128,8 +130,8 @@
 
     expert_ids = jnp.arange(experts, dtype=jnp.int32)[:, None]
     slot_ids = jnp.arange(slots_per, dtype=jnp.int32)[None, :, None]
-    names = [chosen[:, k][None, :] == expert_ids for k in range(2)]
-    named = names[0] | names[1]
+    names = chosen.T[:, None, :] == expert_ids[None]
+    named = jnp.any(names, axis=0)
     token_ids = jnp.arange(tokens, dtype=jnp.int32)
     earlier = (token_ids[:, None] < token_ids[None, :]).astype(jnp.bfloat16)
     slot = jnp.dot(
@@ -137,7 +139,7 @@
     ).astype(jnp.int32)
     hit = named[:, None, :] & (slot[:, None, :] == slot_ids)
     place = hit.astype(jnp.bfloat16).reshape(all_slots, tokens)
-    pair_gate = jnp.where(names[0], weights[:, 0][None, :], weights[:, 1][None, :])
+    pair_gate = jnp.sum(jnp.where(names, weights.T[:, None, :], 0.0), axis=0)
     gate = jnp.sum(jnp.where(hit, pair_gate[:, None, :], 0.0), axis=2).reshape(all_slots, 1)
     picked = jnp.dot(place, grads, preferred_element_type=jnp.float32)
     packed = (gate * picked).astype(jnp.bfloat16)
@@ -146,8 +148,8 @@
         .transpose(0, 2, 1, 3)
         .reshape(count * slots_per, quarter)
     )
-    outgoing, place = hold(outgoing, place)
-    place_after = to_previous(place)
+    swapped = place.reshape(experts, slots_per, tokens)[::-1].reshape(all_slots, tokens)
+    place_after = to_previous(jnp.where(position >> levels == 1, swapped, place).T)
     rows = exchange(outgoing, "expert")
     rows, place_after = hold(rows, place_after)
 
@@ -165,7 +167,6 @@
     half = rows_all // 2
     keep, away = split_by(core, partial_value[:half], partial_value[half:])
     value = keep + partner(away.astype(jnp.bfloat16), "expert", 0).astype(jnp.float32)
-    value, term_down = hold(value, term_down)
     down_pieces = scatter_along_z(term_down)
     for level in range(1, levels):
         value = value + partner(value.astype(jnp.bfloat16), "expert", level).astype(jnp.float32)
@@ -178,9 +179,7 @@
     )
     grads_after = to_previous(grads)
 
-    term_up = lax.dot_general(
-        hidden_grad, saved_in[0, 0], (((0,), (0,)), ((), ())), preferred_element_type=jnp.float32
-    ).astype(jnp.bfloat16)
+    hidden_grad, down_pieces = hold(hidden_grad, down_pieces)
     out_block = jnp.arange(rows_all, dtype=jnp.int32)[:, None]
     in_block = jnp.arange(rows_all, dtype=jnp.int32)[None, :]
     bits = levels + 1
@@ -197,25 +196,25 @@
         ordered, w_up[0], (((1,), (1,)), ((), ())), preferred_element_type=jnp.float32
     ).astype(jnp.bfloat16)
 
+    back, hidden_grad = hold(back, hidden_grad)
+    term_up = lax.dot_general(
+        hidden_grad, saved_in[0, 0], (((0,), (0,)), ((), ())), preferred_element_type=jnp.float32
+    ).astype(jnp.bfloat16)
     buffer = back.reshape(1, count, slots_per, quarter)
     for level in range(levels):
         middle = buffer.shape[1] // 2
         got = partner(buffer[:, middle:], "expert", level)
         buffer = jnp.concatenate([buffer[:, :middle], got], axis=0)
         if level == 0:
-            buffer, down_pieces, term_up = hold(buffer, down_pieces, term_up)
+            buffer, term_up = hold(buffer, term_up)
             up_pieces = scatter_along_z(term_up)
-        if level == 1:
             buffer, grads_after = hold(buffer, grads_after)
     kept = behind(buffer[:, 0], 0)
     got = behind(buffer[:, 1], split)
     sums = [add_pieces(down_pieces), add_pieces(up_pieces)]
-    kept, got, away = hold(kept, got, leaving_x(sums))
-    mine = position >> levels
-    place_after = place_after.reshape(experts, slots_per, tokens)
-    place_after = jnp.where(mine == 1, place_after[::-1], place_after).reshape(all_slots, tokens)
-    total = combine(position & (split - 1), grads_after, place_after.T, kept, got)
-    down, up = across_x(sums, away)
+    crossed = across_x(leaving_x(sums))
+    total = combine(position & (split - 1), grads_after, place_after, kept, got)
+    down, up = staying_x(sums, crossed)
     return (total[None], up[None], down[None])
 
 

time: 136 us -> 128 us (0.941)
  the two profiles are of different devices: /device:TPU:12 before, /device:TPU:1 now
where the time goes in v7:
time: 128 us; the launch traced here: 125 us
  starting transfers between devices  58.1 us (45%)
  waiting for transfers between devices  48.4 us (38%)
  matrix products  5.26 us (4%)
  other arithmetic  4.56 us (4%)
  local copies, waits for them, and re-layouts  4.16 us (3%)
  Pallas kernels  3.93 us (3%)
    ppermute x7, waiting for transfers between devices, partner(): return lax.ppermute(block, axis, [(i, i ^ 1 << bit) for i in range(count)])  31.6 us
    all_to_all x3, starting transfers between devices, exchange(): return lax.all_to_all(x, axis, 0, 0, tiled=True, axis_index_groups=groups)  29.7 us
    ppermute x7, starting transfers between devices, partner(): return lax.ppermute(block, axis, [(i, i ^ 1 << bit) for i in range(count)])  16.1 us
    all_to_all x3, waiting for transfers between devices, exchange(): return lax.all_to_all(x, axis, 0, 0, tiled=True, axis_index_groups=groups)  13.2 us
    ppermute x1, starting transfers between devices, across_x(): lax.ppermute(away, 'dp', [(i, (i + count // 2) % count) for i in range(co...  7.11 us
    pallas_call x1, Pallas kernels, combine(): pl.pallas_call(combine_kernel, grid_spec=pltpu.PrefetchScalarGridSpec(num...  3.93 us
    ppermute x2, waiting for transfers between devices, to_previous(): return lax.ppermute(x, 'phase', [(i, i - 1) for i in range(1, peers)])  3.65 us
    ppermute x2, starting transfers between devices, to_previous(): return lax.ppermute(x, 'phase', [(i, i - 1) for i in range(1, peers)])  2.58 us
  transfers between devices with their start and end apart: 15, of which 10 were waited for; matrix products, arithmetic and copies ran while one was open for 6% of the time, Pallas kernels for 3%

profile of v7, /device:TPU:1, one launch (start us, length us, event | category | flops | bytes accessed | tf_op | source)
XLA Modules:
  0.0 125.4 jit_solution(17979057762712886056)
XLA Ops:
  0.6 0.8 fusion.40
  1.4 0.1 convolution_convert_fusion.4
  1.6 0.7 select_reduce_fusion.1
  2.3 0.1 select_reduce_fusion
  2.4 0.1 mul.46
  2.5 1.6 %fusion = bf16[32,5120]{1,0:T(8,128)(2,1)S(1)} fusion(pred[32,128]{1,0:T(8,128)(4,1)S(1)} %bitcast.86, f32[32]{0:T(128)S(1)} %mul.46, bf16[1,128,5120]{2,1,0:T(8,128)(2,1)} %param.7), kind=kOutput, calls=%fused_computation.1 | convolution fusion | flops 42270720 | bytes 1642624 | tf_op jit(solution)/shard_map/dot_general | solution.py:144
  4.1 0.8 copy.17
  4.9 17.5 %all-to-all-start = ((bf16[16,16,640]{2,1,0:T(8,128)(2,1)}), bf16[16,16,640]{2,1,0:T(8,128)(2,1)S(1)}, u32[]{:S(2)}, u32[]{:S(2)}) async-start(bf16[16,16,640]{2,1,0:T(8,128)(2,1)} %bitcast.8), calls=%async_computation | async-start | bytes 655360 | tf_op jit(solution)/shard_map/all_to_all | solution.py:17
  22.5 0.1 copy.19
  22.6 0.1 copy.20
  22.7 0.1 copy.18
  22.9 1.3 %collective-permute-start = (bf16[128,32]{1,0:T(8,128)(2,1)S(1)}, bf16[128,32]{1,0:T(8,128)(2,1)S(1)}, u32[]{:S(2)}, u32[]{:S(2)}) collective-permute-start(bf16[128,32]{1,0:T(8,128)(2,1)S(1)} %fusion.38), channel_id=1, source_target_pairs={{256,0},{512,256},{768,512},{257,1},{513,257},{769,513},{258,2},{5... | collective-permute-start | bytes 24584 | tf_op jit(solution)/shard_map/ppermute | solution.py:22
  24.2 3.6 %collective-permute-done.place = bf16[128,32]{1,0:T(8,128)(2,1)S(1)} collective-permute-done((bf16[128,32]{1,0:T(8,128)(2,1)S(1)}, bf16[128,32]{1,0:T(8,128)(2,1)S(1)}, u32[]{:S(2)}, u32[]{:S(2)}) %collective-permute-start) | collective-permute-done | bytes 8224 | tf_op jit(solution)/shard_map/ppermute | solution.py:22
  27.8 7.6 %all-to-all-done = bf16[16,16,640]{2,1,0:T(8,128)(2,1)S(1)} async-done(((bf16[16,16,640]{2,1,0:T(8,128)(2,1)}), bf16[16,16,640]{2,1,0:T(8,128)(2,1)S(1)}, u32[]{:S(2)}, u32[]{:S(2)}) %all-to-all-start) | async-done | bytes 327712 | tf_op jit(solution)/shard_map/all_to_all | solution.py:17
  35.4 0.5 fusion.2
  36.0 1.9 %collective-permute-start.1 = (bf16[128,768]{1,0:T(8,128)(2,1)S(1)}, bf16[128,768]{1,0:T(8,128)(2,1)S(1)}, u32[]{:S(2)}, u32[]{:S(2)}) collective-permute-start(bf16[128,768]{1,0:T(8,128)(2,1)S(1)} %select_convert_fusion), channel_id=1, source_target_pairs={{0,1},{1,0},{2,3},{3,2},{4,5},{5,4},{6,7},{7,6},{8,9},{9,8},{10,11... | collective-permute-start | bytes 589832 | tf_op jit(solution)/shard_map/ppermute | solution.py:27
  37.9 0.6 convolution_convert_fusion.1
  38.5 1.0 copy.21
  39.5 8.0 %all-to-all-start.1 = ((bf16[8,96,640]{2,1,0:T(8,128)(2,1)}), bf16[8,96,640]{2,1,0:T(8,128)(2,1)S(1)}, u32[]{:S(2)}, u32[]{:S(2)}) async-start(bf16[8,96,640]{2,1,0:T(8,128)(2,1)} %bitcast.75), calls=%async_computation.1 | async-start | bytes 1966080 | tf_op jit(solution)/shard_map/all_to_all | solution.py:17
  47.6 1.9 %collective-permute-start.2 = (bf16[128,768]{1,0:T(8,128)(2,1)S(1)}, bf16[128,768]{1,0:T(8,128)(2,1)S(1)}, u32[]{:S(2)}, u32[]{:S(2)}) collective-permute-start(bf16[128,768]{1,0:T(8,128)(2,1)S(1)} %get-tuple-element.23), channel_id=1, source_target_pairs={{0,2},{1,3},{2,0},{3,1},{4,6},{5,7},{6,4},{7,5},{8,10},{9,11},{10,... | collective-permute-start | bytes 589832 | tf_op jit(solution)/shard_map/ppermute | solution.py:27
  49.6 1.3 %collective-permute-start.6 = (bf16[128,5120]{1,0:T(8,128)(2,1)}, bf16[128,5120]{1,0:T(8,128)(2,1)}, u32[]{:S(2)}, u32[]{:S(2)}) collective-permute-start(bf16[128,5120]{1,0:T(8,128)(2,1)} %bitcast.6), channel_id=1, source_target_pairs={{256,0},{512,256},{768,512},{257,1},{513,257},{769,513},{258,2},{5... | collective-permute-start | bytes 3932168 | tf_op jit(solution)/shard_map/ppermute | solution.py:22
  50.9 4.3 %collective-permute-done.2 = bf16[128,768]{1,0:T(8,128)(2,1)S(1)} collective-permute-done((bf16[128,768]{1,0:T(8,128)(2,1)S(1)}, bf16[128,768]{1,0:T(8,128)(2,1)S(1)}, u32[]{:S(2)}, u32[]{:S(2)}) %collective-permute-start.2) | collective-permute-done | bytes 196640 | tf_op jit(solution)/shard_map/ppermute | solution.py:27
  55.2 2.9 %collective-permute-start.3 = (bf16[128,768]{1,0:T(8,128)(2,1)S(1)}, bf16[128,768]{1,0:T(8,128)(2,1)S(1)}, u32[]{:S(2)}, u32[]{:S(2)}) collective-permute-start(bf16[128,768]{1,0:T(8,128)(2,1)S(1)} %fusion.16), channel_id=1, source_target_pairs={{0,4},{1,5},{2,6},{3,7},{4,0},{5,1},{6,2},{7,3},{8,12},{9,13},{10,... | collective-permute-start | bytes 589832 | tf_op jit(solution)/shard_map/ppermute | solution.py:27
  58.1 0.3 fusion.9
  58.5 10.5 %collective-permute-done.3 = bf16[128,768]{1,0:T(8,128)(2,1)S(1)} collective-permute-done((bf16[128,768]{1,0:T(8,128)(2,1)S(1)}, bf16[128,768]{1,0:T(8,128)(2,1)S(1)}, u32[]{:S(2)}, u32[]{:S(2)}) %collective-permute-start.3) | collective-permute-done | bytes 196640 | tf_op jit(solution)/shard_map/ppermute | solution.py:27
  69.0 0.1 fusion.13
  69.1 2.5 %collective-permute-start.4 = (bf16[128,768]{1,0:T(8,128)(2,1)S(1)}, bf16[128,768]{1,0:T(8,128)(2,1)S(1)}, u32[]{:S(2)}, u32[]{:S(2)}) collective-permute-start(bf16[128,768]{1,0:T(8,128)(2,1)S(1)} %fusion.13), channel_id=1, source_target_pairs={{0,1},{1,0},{2,3},{3,2},{4,5},{5,4},{6,7},{7,6},{8,9},{9,8},{10,11... | collective-permute-start | bytes 589832 | tf_op jit(solution)/shard_map/ppermute | solution.py:27
  71.6 1.0 collective-permute-done.4
  72.7 2.7 %all-to-all-done.1 = bf16[8,96,640]{2,1,0:T(8,128)(2,1)S(1)} async-done(((bf16[8,96,640]{2,1,0:T(8,128)(2,1)}), bf16[8,96,640]{2,1,0:T(8,128)(2,1)S(1)}, u32[]{:S(2)}, u32[]{:S(2)}) %all-to-all-start.1) | async-done | bytes 983072 | tf_op jit(solution)/shard_map/all_to_all | solution.py:17
  75.3 1.9 %convolution_convert_fusion.3 = bf16[256,640]{1,0:T(8,128)(2,1)S(1)} fusion(bf16[256,768]{1,0:T(8,128)(2,1)S(1)} %pad_maximum_fusion, bf16[1,640,768]{2,1,0:T(8,128)(2,1)} %param.12, s32[256]{0:T(256)S(1)} %get-tuple-element.39, s32[256]{0:T(256)S(1)} %get-tuple-element.40, s32[256]{0:T(256)S(1)} %add_xor_fusion), kind=kOutput, calls=%fused_computation.12 | convolution fusion | flops 352878592 | bytes 1707008 | tf_op jit(solution)/shard_map/dot_general | solution.py:195
  77.3 2.4 %collective-permute-start.5 = (bf16[1,8,16,640]{3,2,0,1:T(8,128)(2,1)S(1)}, bf16[1,8,16,640]{3,2,0,1:T(8,128)(2,1)S(1)}, u32[]{:S(2)}, u32[]{:S(2)}) collective-permute-start(bf16[1,8,16,640]{3,2,0,1:T(8,128)(2,1)S(1)} %get-tuple-element.34), channel_id=1, source_target_pairs={{0,1},{1,0},{2,3},{3,2},{4,5},{5,4},{6,7},{7,6},{8,9},{9,8},{10,11... | collective-permute-start | bytes 491528 | tf_op jit(solution)/shard_map/ppermute | solution.py:27
  79.7 0.5 convolution_convert_fusion
  80.2 0.5 collective-permute-done.5
  80.8 1.0 copy.22
  81.8 4.2 %all-to-all-start.2 = ((bf16[8,96,640]{2,1,0:T(8,128)(2,1)}), bf16[8,96,640]{2,1,0:T(8,128)(2,1)}, u32[]{:S(2)}, u32[]{:S(2)}) async-start(bf16[8,96,640]{2,1,0:T(8,128)(2,1)} %bitcast.29), calls=%async_computation.2 | async-start | bytes 1966080 | tf_op jit(solution)/shard_map/all_to_all | solution.py:17
  86.1 1.9 %collective-permute-start.7 = (bf16[2,4,16,640]{3,2,0,1:T(8,128)(2,1)S(1)}, bf16[2,4,16,640]{3,2,0,1:T(8,128)(2,1)S(1)}, u32[]{:S(2)}, u32[]{:S(2)}) collective-permute-start(bf16[2,4,16,640]{3,2,0,1:T(8,128)(2,1)S(1)} %get-tuple-element.31), channel_id=1, source_target_pairs={{0,2},{1,3},{2,0},{3,1},{4,6},{5,7},{6,4},{7,5},{8,10},{9,11},{10,... | collective-permute-start | bytes 491528 | tf_op jit(solution)/shard_map/ppermute | solution.py:27
  88.0 0.1 convert_reduce_fusion
  88.2 5.3 %collective-permute-done.7 = bf16[2,4,16,640]{3,2,0,1:T(8,128)(2,1)S(1)} collective-permute-done((bf16[2,4,16,640]{3,2,0,1:T(8,128)(2,1)S(1)}, bf16[2,4,16,640]{3,2,0,1:T(8,128)(2,1)S(1)}, u32[]{:S(2)}, u32[]{:S(2)}) %collective-permute-start.7) | collective-permute-done | bytes 163872 | tf_op jit(solution)/shard_map/ppermute | solution.py:27
  93.5 2.5 %collective-permute-start.8 = (bf16[4,2,16,640]{3,2,0,1:T(8,128)(2,1)S(1)}, bf16[4,2,16,640]{3,2,0,1:T(8,128)(2,1)S(1)}, u32[]{:S(2)}, u32[]{:S(2)}) collective-permute-start(bf16[4,2,16,640]{3,2,0,1:T(8,128)(2,1)S(1)} %get-tuple-element.29), channel_id=1, source_target_pairs={{0,4},{1,5},{2,6},{3,7},{4,0},{5,1},{6,2},{7,3},{8,12},{9,13},{10,... | collective-permute-start | bytes 491528 | tf_op jit(solution)/shard_map/ppermute | solution.py:27
  96.1 9.9 %collective-permute-done.8 = bf16[4,2,16,640]{3,2,0,1:T(8,128)(2,1)S(1)} collective-permute-done((bf16[4,2,16,640]{3,2,0,1:T(8,128)(2,1)S(1)}, bf16[4,2,16,640]{3,2,0,1:T(8,128)(2,1)S(1)}, u32[]{:S(2)}, u32[]{:S(2)}) %collective-permute-start.8) | collective-permute-done | bytes 163872 | tf_op jit(solution)/shard_map/ppermute | solution.py:27
  106.0 1.3 %collective-permute-start.10 = (bf16[8,16,640]{2,1,0:T(8,128)(2,1)S(1)}, bf16[8,16,640]{2,1,0:T(8,128)(2,1)S(1)}, u32[]{:S(2)}, u32[]{:S(2)}) collective-permute-start(bf16[8,16,640]{2,1,0:T(8,128)(2,1)S(1)} %get-tuple-element.27), channel_id=1, source_target_pairs={{256,8},{257,9},{258,10},{259,11},{260,12},{261,13},{262,14},{263,... | collective-permute-start | bytes 491528 | tf_op jit(solution)/shard_map/ppermute | solution.py:80
  107.3 1.3 %collective-permute-start.9 = (bf16[8,16,640]{2,1,0:T(8,128)(2,1)S(1)}, bf16[8,16,640]{2,1,0:T(8,128)(2,1)S(1)}, u32[]{:S(2)}, u32[]{:S(2)}) collective-permute-start(bf16[8,16,640]{2,1,0:T(8,128)(2,1)S(1)} %get-tuple-element.28), channel_id=1, source_target_pairs={{256,0},{257,1},{258,2},{259,3},{260,4},{261,5},{262,6},{263,7},{2... | collective-permute-start | bytes 491528 | tf_op jit(solution)/shard_map/ppermute | solution.py:80
  108.6 2.9 %all-to-all-done.2 = bf16[8,96,640]{2,1,0:T(8,128)(2,1)} async-done(((bf16[8,96,640]{2,1,0:T(8,128)(2,1)}), bf16[8,96,640]{2,1,0:T(8,128)(2,1)}, u32[]{:S(2)}, u32[]{:S(2)}) %all-to-all-start.2) | async-done | bytes 983072 | tf_op jit(solution)/shard_map/all_to_all | solution.py:17
  111.5 1.4 %convert_reduce_fusion.1 = f32[96,640]{1,0:T(8,128)S(1)} fusion(bf16[8,96,640]{2,1,0:T(8,128)(2,1)} %all-to-all-done.2), kind=kLoop, calls=%fused_computation.3 | loop fusion | flops 921600 | bytes 1228800 | tf_op jit(solution)/shard_map/reduce_sum | solution.py:47
  113.0 7.1 %collective-permute-start.11 = (bf16[2,48,640]{2,1,0:T(8,128)(2,1)S(1)}, bf16[2,48,640]{2,1,0:T(8,128)(2,1)S(1)}, u32[]{:S(2)}, u32[]{:S(2)}) collective-permute-start(bf16[2,48,640]{2,1,0:T(8,128)(2,1)S(1)} %pad_maximum_fusion.4), channel_id=1, source_target_pairs={{0,128},{16,144},{32,160},{48,176},{64,192},{80,208},{96,224},{112... | collective-permute-start | bytes 368648 | tf_op jit(solution)/shard_map/ppermute | solution.py:57
  120.1 0.6 copy-done.3
  120.8 3.9 %combine.1 = bf16[128,5120]{1,0:T(8,128)(2,1)} custom-call(s32[1]{0:T(128)} %bitcast.spot, bf16[128,5120]{1,0:T(8,128)(2,1)} %collective-permute-done.6.grads, bf16[128,32]{1,0:T(8,128)(2,1)} %copy-done.5, bf16[8,16,640]{2,1,0:T(8,128)(2,1)} %copy-done.4, bf16[8,16,640]{2,1,0:T(8,128)(2,1)} %copy-done.3), custom_call_target="tpu_custom_call" | custom-call | flops 41943040 | bytes 2949120 | tf_op jit(solution)/shard_map/combine/pallas_call | solution.py:98
  124.7 0.7 add_convert_fusion
  (39 shorter events, 0.7 us)
Async XLA Ops:
  0.6 34.8 %copy-start = (bf16[1,768,640]{2,1,0:T(8,128)(2,1)S(1)}, bf16[1,768,640]{2,1,0:T(8,128)(2,1)}, u32[]{:S(2)}) copy-start(bf16[1,768,640]{2,1,0:T(8,128)(2,1)} %param.13) | copy-start | bytes 2949124
  4.9 30.5 %all-to-all-start = ((bf16[16,16,640]{2,1,0:T(8,128)(2,1)}), bf16[16,16,640]{2,1,0:T(8,128)(2,1)S(1)}, u32[]{:S(2)}, u32[]{:S(2)}) async-start(bf16[16,16,640]{2,1,0:T(8,128)(2,1)} %bitcast.8), calls=%async_computation | async-start | bytes 655360 | tf_op jit(solution)/shard_map/all_to_all | solution.py:17
  22.9 5.0 %collective-permute-start = (bf16[128,32]{1,0:T(8,128)(2,1)S(1)}, bf16[128,32]{1,0:T(8,128)(2,1)S(1)}, u32[]{:S(2)}, u32[]{:S(2)}) collective-permute-start(bf16[128,32]{1,0:T(8,128)(2,1)S(1)} %fusion.38), channel_id=1, source_target_pairs={{256,0},{512,256},{768,512},{257,1},{513,257},{769,513},{258,2},{5... | collective-permute-start | bytes 24584 | tf_op jit(solution)/shard_map/ppermute | solution.py:22
  27.8 8.2 %copy-start.5 = (bf16[128,32]{1,0:T(8,128)(2,1)}, bf16[128,32]{1,0:T(8,128)(2,1)S(1)}, u32[]{:S(2)}) copy-start(bf16[128,32]{1,0:T(8,128)(2,1)S(1)} %collective-permute-done.place) | copy-start | bytes 24580
  35.4 2.5 %copy-start.1 = (bf16[1,1,1,256,768]{4,3,2,1,0:T(8,128)(2,1)S(1)}, bf16[1,1,1,256,768]{4,3,2,1,0:T(8,128)(2,1)}, u32[]{:S(2)}) copy-start(bf16[1,1,1,256,768]{4,3,2,1,0:T(8,128)(2,1)} %param.11) | copy-start | bytes 1179652
  36.0 11.6 %collective-permute-start.1 = (bf16[128,768]{1,0:T(8,128)(2,1)S(1)}, bf16[128,768]{1,0:T(8,128)(2,1)S(1)}, u32[]{:S(2)}, u32[]{:S(2)}) collective-permute-start(bf16[128,768]{1,0:T(8,128)(2,1)S(1)} %select_convert_fusion), channel_id=1, source_target_pairs={{0,1},{1,0},{2,3},{3,2},{4,5},{5,4},{6,7},{7,6},{8,9},{9,8},{10,11... | collective-permute-start | bytes 589832 | tf_op jit(solution)/shard_map/ppermute | solution.py:27
  39.5 35.8 %all-to-all-start.1 = ((bf16[8,96,640]{2,1,0:T(8,128)(2,1)}), bf16[8,96,640]{2,1,0:T(8,128)(2,1)S(1)}, u32[]{:S(2)}, u32[]{:S(2)}) async-start(bf16[8,96,640]{2,1,0:T(8,128)(2,1)} %bitcast.75), calls=%async_computation.1 | async-start | bytes 1966080 | tf_op jit(solution)/shard_map/all_to_all | solution.py:17
  47.6 7.5 %collective-permute-start.2 = (bf16[128,768]{1,0:T(8,128)(2,1)S(1)}, bf16[128,768]{1,0:T(8,128)(2,1)S(1)}, u32[]{:S(2)}, u32[]{:S(2)}) collective-permute-start(bf16[128,768]{1,0:T(8,128)(2,1)S(1)} %get-tuple-element.23), channel_id=1, source_target_pairs={{0,2},{1,3},{2,0},{3,1},{4,6},{5,7},{6,4},{7,5},{8,10},{9,11},{10,... | collective-permute-start | bytes 589832 | tf_op jit(solution)/shard_map/ppermute | solution.py:27
  49.6 36.5 %collective-permute-start.6 = (bf16[128,5120]{1,0:T(8,128)(2,1)}, bf16[128,5120]{1,0:T(8,128)(2,1)}, u32[]{:S(2)}, u32[]{:S(2)}) collective-permute-start(bf16[128,5120]{1,0:T(8,128)(2,1)} %bitcast.6), channel_id=1, source_target_pairs={{256,0},{512,256},{768,512},{257,1},{513,257},{769,513},{258,2},{5... | collective-permute-start | bytes 3932168 | tf_op jit(solution)/shard_map/ppermute | solution.py:22
  55.2 13.8 %collective-permute-start.3 = (bf16[128,768]{1,0:T(8,128)(2,1)S(1)}, bf16[128,768]{1,0:T(8,128)(2,1)S(1)}, u32[]{:S(2)}, u32[]{:S(2)}) collective-permute-start(bf16[128,768]{1,0:T(8,128)(2,1)S(1)} %fusion.16), channel_id=1, source_target_pairs={{0,4},{1,5},{2,6},{3,7},{4,0},{5,1},{6,2},{7,3},{8,12},{9,13},{10,... | collective-permute-start | bytes 589832 | tf_op jit(solution)/shard_map/ppermute | solution.py:27
  69.1 3.5 %collective-permute-start.4 = (bf16[128,768]{1,0:T(8,128)(2,1)S(1)}, bf16[128,768]{1,0:T(8,128)(2,1)S(1)}, u32[]{:S(2)}, u32[]{:S(2)}) collective-permute-start(bf16[128,768]{1,0:T(8,128)(2,1)S(1)} %fusion.13), channel_id=1, source_target_pairs={{0,1},{1,0},{2,3},{3,2},{4,5},{5,4},{6,7},{7,6},{8,9},{9,8},{10,11... | collective-permute-start | bytes 589832 | tf_op jit(solution)/shard_map/ppermute | solution.py:27
  75.3 4.4 %copy-start.2 = (bf16[1,1,256,640]{3,2,1,0:T(8,128)(2,1)S(1)}, bf16[1,1,256,640]{3,2,1,0:T(8,128)(2,1)}, u32[]{:S(2)}) copy-start(bf16[1,1,256,640]{3,2,1,0:T(8,128)(2,1)} %param.10) | copy-start | bytes 983044
  77.3 3.4 %collective-permute-start.5 = (bf16[1,8,16,640]{3,2,0,1:T(8,128)(2,1)S(1)}, bf16[1,8,16,640]{3,2,0,1:T(8,128)(2,1)S(1)}, u32[]{:S(2)}, u32[]{:S(2)}) collective-permute-start(bf16[1,8,16,640]{3,2,0,1:T(8,128)(2,1)S(1)} %get-tuple-element.34), channel_id=1, source_target_pairs={{0,1},{1,0},{2,3},{3,2},{4,5},{5,4},{6,7},{7,6},{8,9},{9,8},{10,11... | collective-permute-start | bytes 491528 | tf_op jit(solution)/shard_map/ppermute | solution.py:27
  81.8 29.8 %all-to-all-start.2 = ((bf16[8,96,640]{2,1,0:T(8,128)(2,1)}), bf16[8,96,640]{2,1,0:T(8,128)(2,1)}, u32[]{:S(2)}, u32[]{:S(2)}) async-start(bf16[8,96,640]{2,1,0:T(8,128)(2,1)} %bitcast.29), calls=%async_computation.2 | async-start | bytes 1966080 | tf_op jit(solution)/shard_map/all_to_all | solution.py:17
  86.1 7.4 %collective-permute-start.7 = (bf16[2,4,16,640]{3,2,0,1:T(8,128)(2,1)S(1)}, bf16[2,4,16,640]{3,2,0,1:T(8,128)(2,1)S(1)}, u32[]{:S(2)}, u32[]{:S(2)}) collective-permute-start(bf16[2,4,16,640]{3,2,0,1:T(8,128)(2,1)S(1)} %get-tuple-element.31), channel_id=1, source_target_pairs={{0,2},{1,3},{2,0},{3,1},{4,6},{5,7},{6,4},{7,5},{8,10},{9,11},{10,... | collective-permute-start | bytes 491528 | tf_op jit(solution)/shard_map/ppermute | solution.py:27
  93.5 12.4 %collective-permute-start.8 = (bf16[4,2,16,640]{3,2,0,1:T(8,128)(2,1)S(1)}, bf16[4,2,16,640]{3,2,0,1:T(8,128)(2,1)S(1)}, u32[]{:S(2)}, u32[]{:S(2)}) collective-permute-start(bf16[4,2,16,640]{3,2,0,1:T(8,128)(2,1)S(1)} %get-tuple-element.29), channel_id=1, source_target_pairs={{0,4},{1,5},{2,6},{3,7},{4,0},{5,1},{6,2},{7,3},{8,12},{9,13},{10,... | collective-permute-start | bytes 491528 | tf_op jit(solution)/shard_map/ppermute | solution.py:27
  106.0 14.1 %collective-permute-start.10 = (bf16[8,16,640]{2,1,0:T(8,128)(2,1)S(1)}, bf16[8,16,640]{2,1,0:T(8,128)(2,1)S(1)}, u32[]{:S(2)}, u32[]{:S(2)}) collective-permute-start(bf16[8,16,640]{2,1,0:T(8,128)(2,1)S(1)} %get-tuple-element.27), channel_id=1, source_target_pairs={{256,8},{257,9},{258,10},{259,11},{260,12},{261,13},{262,14},{263,... | collective-permute-start | bytes 491528 | tf_op jit(solution)/shard_map/ppermute | solution.py:80
  107.3 12.8 %collective-permute-start.9 = (bf16[8,16,640]{2,1,0:T(8,128)(2,1)S(1)}, bf16[8,16,640]{2,1,0:T(8,128)(2,1)S(1)}, u32[]{:S(2)}, u32[]{:S(2)}) collective-permute-start(bf16[8,16,640]{2,1,0:T(8,128)(2,1)S(1)} %get-tuple-element.28), channel_id=1, source_target_pairs={{256,0},{257,1},{258,2},{259,3},{260,4},{261,5},{262,6},{263,7},{2... | collective-permute-start | bytes 491528 | tf_op jit(solution)/shard_map/ppermute | solution.py:80
  113.0 11.8 %collective-permute-start.11 = (bf16[2,48,640]{2,1,0:T(8,128)(2,1)S(1)}, bf16[2,48,640]{2,1,0:T(8,128)(2,1)S(1)}, u32[]{:S(2)}, u32[]{:S(2)}) collective-permute-start(bf16[2,48,640]{2,1,0:T(8,128)(2,1)S(1)} %pad_maximum_fusion.4), channel_id=1, source_target_pairs={{0,128},{16,144},{32,160},{48,176},{64,192},{80,208},{96,224},{112... | collective-permute-start | bytes 368648 | tf_op jit(solution)/shard_map/ppermute | solution.py:57
  120.1 0.7 copy-start.3
  120.1 0.7 copy-start.4

commit v8 on v7

--- a/solution.py
+++ b/solution.py
@@ -34,10 +34,16 @@
 def scatter_along_z(term):
     count = lax.axis_size("dp")
     near = count // 2
+    groups = [[h * near + z for z in range(near)] for h in range(2)]
+    return exchange(term, "dp", groups)
+
+
+def order_for_z(term):
+    count = lax.axis_size("dp")
+    near = count // 2
     hid, quarter = term.shape
-    groups = [[h * near + z for z in range(near)] for h in range(2)]
     ordered = term.reshape(2, near, hid // count, quarter).transpose(1, 0, 2, 3)
-    return exchange(ordered.reshape(hid, quarter), "dp", groups)
+    return ordered.reshape(hid, quarter)
 
 
 def add_pieces(pieces):
@@ -167,9 +173,11 @@
     half = rows_all // 2
     keep, away = split_by(core, partial_value[:half], partial_value[half:])
     value = keep + partner(away.astype(jnp.bfloat16), "expert", 0).astype(jnp.float32)
-    down_pieces = scatter_along_z(term_down)
     for level in range(1, levels):
         value = value + partner(value.astype(jnp.bfloat16), "expert", level).astype(jnp.float32)
+        if level == 1:
+            value, term_down = hold(value, term_down)
+            down_pieces = scatter_along_z(order_for_z(term_down))
     own_slope = jnp.where(core == 1, slope[half:], slope[:half])
     own_grad = (value * own_slope).astype(jnp.bfloat16)
     other_grad = partner(own_grad, "expert", 0)
@@ -179,7 +187,6 @@
     )
     grads_after = to_previous(grads)
 
-    hidden_grad, down_pieces = hold(hidden_grad, down_pieces)
     out_block = jnp.arange(rows_all, dtype=jnp.int32)[:, None]
     in_block = jnp.arange(rows_all, dtype=jnp.int32)[None, :]
     bits = levels + 1
@@ -200,15 +207,17 @@
     term_up = lax.dot_general(
         hidden_grad, saved_in[0, 0], (((0,), (0,)), ((), ())), preferred_element_type=jnp.float32
     ).astype(jnp.bfloat16)
+    term_up = order_for_z(term_up)
     buffer = back.reshape(1, count, slots_per, quarter)
     for level in range(levels):
         middle = buffer.shape[1] // 2
         got = partner(buffer[:, middle:], "expert", level)
         buffer = jnp.concatenate([buffer[:, :middle], got], axis=0)
-        if level == 0:
-            buffer, term_up = hold(buffer, term_up)
+        if level == 1:
+            buffer, grads_after, down_pieces, term_up = hold(
+                buffer, grads_after, down_pieces, term_up
+            )
             up_pieces = scatter_along_z(term_up)
-            buffer, grads_after = hold(buffer, grads_after)
     kept = behind(buffer[:, 0], 0)
     got = behind(buffer[:, 1], split)
     sums = [add_pieces(down_pieces), add_pieces(up_pieces)]

time: 128 us -> 134 us (1.047)
  the two profiles are of different devices: /device:TPU:1 before, /device:TPU:14 now
where the time goes in v8:
time: 134 us; the launch traced here: 133 us
  starting transfers between devices  65.4 us (49%)
  waiting for transfers between devices  49.9 us (37%)
  matrix products  5.26 us (4%)
  local copies, waits for them, and re-layouts  4.15 us (3%)
  Pallas kernels  3.92 us (3%)
  other arithmetic  3.37 us (3%)
    all_to_all x3, starting transfers between devices, exchange(): return lax.all_to_all(x, axis, 0, 0, tiled=True, axis_index_groups=groups)  27.9 us
    all_to_all x3, waiting for transfers between devices, exchange(): return lax.all_to_all(x, axis, 0, 0, tiled=True, axis_index_groups=groups)  24.3 us
    ppermute x7, waiting for transfers between devices, partner(): return lax.ppermute(block, axis, [(i, i ^ 1 << bit) for i in range(count)])  20.9 us
    ppermute x7, starting transfers between devices, partner(): return lax.ppermute(block, axis, [(i, i ^ 1 << bit) for i in range(count)])  18.3 us
    ppermute x2, starting transfers between devices, to_previous(): return lax.ppermute(x, 'phase', [(i, i - 1) for i in range(1, peers)])  7.76 us
    ppermute x2, starting transfers between devices, behind(): return lax.ppermute(block, ('phase', 'expert'), pairs)  7.32 us
    ppermute x1, starting transfers between devices, across_x(): lax.ppermute(away, 'dp', [(i, (i + count // 2) % count) for i in range(co...  4.04 us
    pallas_call x1, Pallas kernels, combine(): pl.pallas_call(combine_kernel, grid_spec=pltpu.PrefetchScalarGridSpec(num...  3.92 us
  transfers between devices with their start and end apart: 15, of which 10 were waited for; matrix products, arithmetic and copies ran while one was open for 5% of the time, Pallas kernels for 3%

profile of v8, /device:TPU:14, one launch (start us, length us, event | category | flops | bytes accessed | tf_op | source)
XLA Modules:
  0.0 133.0 jit_solution(10199023163820497754)
XLA Ops:
  0.6 0.8 fusion.40
  1.4 0.1 convolution_convert_fusion.4
  1.6 0.7 select_reduce_fusion.1
  2.3 0.1 select_reduce_fusion
  2.4 0.1 mul.46
  2.5 1.6 %fusion = bf16[32,5120]{1,0:T(8,128)(2,1)S(1)} fusion(pred[32,128]{1,0:T(8,128)(4,1)S(1)} %bitcast.85, f32[32]{0:T(128)S(1)} %mul.46, bf16[1,128,5120]{2,1,0:T(8,128)(2,1)} %param.7), kind=kOutput, calls=%fused_computation.1 | convolution fusion | flops 42270720 | bytes 1642624 | tf_op jit(solution)/shard_map/dot_general | solution.py:150
  4.1 0.8 copy.17
  4.9 7.7 %all-to-all-start = ((bf16[16,16,640]{2,1,0:T(8,128)(2,1)}), bf16[16,16,640]{2,1,0:T(8,128)(2,1)S(1)}, u32[]{:S(2)}, u32[]{:S(2)}) async-start(bf16[16,16,640]{2,1,0:T(8,128)(2,1)} %bitcast.8), calls=%async_computation | async-start | bytes 655360 | tf_op jit(solution)/shard_map/all_to_all | solution.py:17
  12.6 0.1 eq.107
  12.7 0.1 copy.19
  12.8 0.1 copy.20
  12.9 0.1 copy.18
  13.1 3.3 %collective-permute-start = (bf16[128,32]{1,0:T(8,128)(2,1)S(1)}, bf16[128,32]{1,0:T(8,128)(2,1)S(1)}, u32[]{:S(2)}, u32[]{:S(2)}) collective-permute-start(bf16[128,32]{1,0:T(8,128)(2,1)S(1)} %fusion.37), channel_id=1, source_target_pairs={{256,0},{512,256},{768,512},{257,1},{513,257},{769,513},{258,2},{5... | collective-permute-start | bytes 24584 | tf_op jit(solution)/shard_map/ppermute | solution.py:22
  16.4 1.6 %collective-permute-done.place = bf16[128,32]{1,0:T(8,128)(2,1)S(1)} collective-permute-done((bf16[128,32]{1,0:T(8,128)(2,1)S(1)}, bf16[128,32]{1,0:T(8,128)(2,1)S(1)}, u32[]{:S(2)}, u32[]{:S(2)}) %collective-permute-start) | collective-permute-done | bytes 8224 | tf_op jit(solution)/shard_map/ppermute | solution.py:22
  18.0 7.0 %all-to-all-done = bf16[16,16,640]{2,1,0:T(8,128)(2,1)S(1)} async-done(((bf16[16,16,640]{2,1,0:T(8,128)(2,1)}), bf16[16,16,640]{2,1,0:T(8,128)(2,1)S(1)}, u32[]{:S(2)}, u32[]{:S(2)}) %all-to-all-start) | async-done | bytes 327712 | tf_op jit(solution)/shard_map/all_to_all | solution.py:17
  25.0 0.5 fusion.2
  25.5 3.1 %collective-permute-start.1 = (bf16[128,768]{1,0:T(8,128)(2,1)S(1)}, bf16[128,768]{1,0:T(8,128)(2,1)S(1)}, u32[]{:S(2)}, u32[]{:S(2)}) collective-permute-start(bf16[128,768]{1,0:T(8,128)(2,1)S(1)} %select_convert_fusion), channel_id=1, source_target_pairs={{0,1},{1,0},{2,3},{3,2},{4,5},{5,4},{6,7},{7,6},{8,9},{9,8},{10,11... | collective-permute-start | bytes 589832 | tf_op jit(solution)/shard_map/ppermute | solution.py:27
  28.7 4.4 %collective-permute-start.7 = (bf16[128,5120]{1,0:T(8,128)(2,1)}, bf16[128,5120]{1,0:T(8,128)(2,1)}, u32[]{:S(2)}, u32[]{:S(2)}) collective-permute-start(bf16[128,5120]{1,0:T(8,128)(2,1)} %bitcast.6), channel_id=1, source_target_pairs={{256,0},{512,256},{768,512},{257,1},{513,257},{769,513},{258,2},{5... | collective-permute-start | bytes 3932168 | tf_op jit(solution)/shard_map/ppermute | solution.py:22
  33.2 1.9 %collective-permute-start.2 = (bf16[128,768]{1,0:T(8,128)(2,1)S(1)}, bf16[128,768]{1,0:T(8,128)(2,1)S(1)}, u32[]{:S(2)}, u32[]{:S(2)}) collective-permute-start(bf16[128,768]{1,0:T(8,128)(2,1)S(1)} %fusion.39), channel_id=1, source_target_pairs={{0,2},{1,3},{2,0},{3,1},{4,6},{5,7},{6,4},{7,5},{8,10},{9,11},{10,... | collective-permute-start | bytes 589832 | tf_op jit(solution)/shard_map/ppermute | solution.py:27
  35.1 0.6 convolution_convert_fusion.1
  35.7 5.9 %collective-permute-done.2 = bf16[128,768]{1,0:T(8,128)(2,1)S(1)} collective-permute-done((bf16[128,768]{1,0:T(8,128)(2,1)S(1)}, bf16[128,768]{1,0:T(8,128)(2,1)S(1)}, u32[]{:S(2)}, u32[]{:S(2)}) %collective-permute-start.2) | collective-permute-done | bytes 196640 | tf_op jit(solution)/shard_map/ppermute | solution.py:27
  41.7 2.8 %collective-permute-start.3 = (bf16[128,768]{1,0:T(8,128)(2,1)S(1)}, bf16[128,768]{1,0:T(8,128)(2,1)S(1)}, u32[]{:S(2)}, u32[]{:S(2)}) collective-permute-start(bf16[128,768]{1,0:T(8,128)(2,1)S(1)} %convert_element_type.106), channel_id=1, source_target_pairs={{0,4},{1,5},{2,6},{3,7},{4,0},{5,1},{6,2},{7,3},{8,12},{9,13},{10,... | collective-permute-start | bytes 589832 | tf_op jit(solution)/shard_map/ppermute | solution.py:27
  44.5 0.3 fusion.10
  44.8 1.0 copy.21
  45.9 16.7 %all-to-all-start.1 = ((bf16[8,96,640]{2,1,0:T(8,128)(2,1)}), bf16[8,96,640]{2,1,0:T(8,128)(2,1)S(1)}, u32[]{:S(2)}, u32[]{:S(2)}) async-start(bf16[8,96,640]{2,1,0:T(8,128)(2,1)} %bitcast.21), calls=%async_computation.1 | async-start | bytes 1966080 | tf_op jit(solution)/shard_map/all_to_all | solution.py:17
  62.7 1.9 %collective-permute-start.4 = (bf16[128,768]{1,0:T(8,128)(2,1)S(1)}, bf16[128,768]{1,0:T(8,128)(2,1)S(1)}, u32[]{:S(2)}, u32[]{:S(2)}) collective-permute-start(bf16[128,768]{1,0:T(8,128)(2,1)S(1)} %fusion.13), channel_id=1, source_target_pairs={{0,1},{1,0},{2,3},{3,2},{4,5},{5,4},{6,7},{7,6},{8,9},{9,8},{10,11... | collective-permute-start | bytes 589832 | tf_op jit(solution)/shard_map/ppermute | solution.py:27
  64.6 1.4 %collective-permute-done.4 = bf16[128,768]{1,0:T(8,128)(2,1)S(1)} collective-permute-done((bf16[128,768]{1,0:T(8,128)(2,1)S(1)}, bf16[128,768]{1,0:T(8,128)(2,1)S(1)}, u32[]{:S(2)}, u32[]{:S(2)}) %collective-permute-start.4) | collective-permute-done | bytes 196640 | tf_op jit(solution)/shard_map/ppermute | solution.py:27
  66.1 1.9 %convolution_convert_fusion.3 = bf16[256,640]{1,0:T(8,128)(2,1)S(1)} fusion(bf16[1,640,768]{2,1,0:T(8,128)(2,1)} %param.12, s32[256]{0:T(256)S(1)} %get-tuple-element.37, s32[256]{0:T(256)S(1)} %get-tuple-element.38, s32[256]{0:T(256)S(1)} %add_xor_fusion, bf16[128,768]{1,0:T(8,128)(2,1)S(1)} %get-tuple-element.24, bf16[128,768]{1,0:T(8,128)(2,1)S(1)} %get-tuple-element.23), kind=kOutput, calls=%fused_computation.12 | convolution fusion | flops 353665024 | bytes 1707008 | tf_op jit(solution)/shard_map/dot_general | solution.py:202
  68.0 2.0 %collective-permute-start.5 = (bf16[1,8,16,640]{3,2,0,1:T(8,128)(2,1)S(1)}, bf16[1,8,16,640]{3,2,0,1:T(8,128)(2,1)S(1)}, u32[]{:S(2)}, u32[]{:S(2)}) collective-permute-start(bf16[1,8,16,640]{3,2,0,1:T(8,128)(2,1)S(1)} %get-tuple-element.32), channel_id=1, source_target_pairs={{0,1},{1,0},{2,3},{3,2},{4,5},{5,4},{6,7},{7,6},{8,9},{9,8},{10,11... | collective-permute-start | bytes 491528 | tf_op jit(solution)/shard_map/ppermute | solution.py:27
  70.1 1.2 collective-permute-done.5
  71.4 3.1 %collective-permute-start.6 = (bf16[2,4,16,640]{3,2,0,1:T(8,128)(2,1)S(1)}, bf16[2,4,16,640]{3,2,0,1:T(8,128)(2,1)S(1)}, u32[]{:S(2)}, u32[]{:S(2)}) collective-permute-start(bf16[2,4,16,640]{3,2,0,1:T(8,128)(2,1)S(1)} %get-tuple-element.30), channel_id=1, source_target_pairs={{0,2},{1,3},{2,0},{3,1},{4,6},{5,7},{6,4},{7,5},{8,10},{9,11},{10,... | collective-permute-start | bytes 491528 | tf_op jit(solution)/shard_map/ppermute | solution.py:27
  74.5 0.5 convolution_convert_fusion
  75.0 1.0 copy.22
  76.0 3.5 %collective-permute-done.6 = bf16[2,4,16,640]{3,2,0,1:T(8,128)(2,1)S(1)} collective-permute-done((bf16[2,4,16,640]{3,2,0,1:T(8,128)(2,1)S(1)}, bf16[2,4,16,640]{3,2,0,1:T(8,128)(2,1)S(1)}, u32[]{:S(2)}, u32[]{:S(2)}) %collective-permute-start.6) | collective-permute-done | bytes 163872 | tf_op jit(solution)/shard_map/ppermute | solution.py:27
  79.6 9.5 %all-to-all-done.1 = bf16[8,96,640]{2,1,0:T(8,128)(2,1)S(1)} async-done(((bf16[8,96,640]{2,1,0:T(8,128)(2,1)}), bf16[8,96,640]{2,1,0:T(8,128)(2,1)S(1)}, u32[]{:S(2)}, u32[]{:S(2)}) %all-to-all-start.1) | async-done | bytes 983072 | tf_op jit(solution)/shard_map/all_to_all | solution.py:17
  89.1 3.6 %all-to-all-start.2 = ((bf16[8,96,640]{2,1,0:T(8,128)(2,1)}), bf16[8,96,640]{2,1,0:T(8,128)(2,1)S(1)}, u32[]{:S(2)}, u32[]{:S(2)}) async-start(bf16[8,96,640]{2,1,0:T(8,128)(2,1)} %bitcast.30), calls=%async_computation.2 | async-start | bytes 1966080 | tf_op jit(solution)/shard_map/all_to_all | solution.py:17
  92.7 3.4 %collective-permute-start.8 = (bf16[4,2,16,640]{3,2,0,1:T(8,128)(2,1)S(1)}, bf16[4,2,16,640]{3,2,0,1:T(8,128)(2,1)S(1)}, u32[]{:S(2)}, u32[]{:S(2)}) collective-permute-start(bf16[4,2,16,640]{3,2,0,1:T(8,128)(2,1)S(1)} %get-tuple-element.27), channel_id=1, source_target_pairs={{0,4},{1,5},{2,6},{3,7},{4,0},{5,1},{6,2},{7,3},{8,12},{9,13},{10,... | collective-permute-start | bytes 491528 | tf_op jit(solution)/shard_map/ppermute | solution.py:27
  96.1 0.1 convert_reduce_fusion
  96.3 8.8 %collective-permute-done.8 = bf16[4,2,16,640]{3,2,0,1:T(8,128)(2,1)S(1)} collective-permute-done((bf16[4,2,16,640]{3,2,0,1:T(8,128)(2,1)S(1)}, bf16[4,2,16,640]{3,2,0,1:T(8,128)(2,1)S(1)}, u32[]{:S(2)}, u32[]{:S(2)}) %collective-permute-start.8) | collective-permute-done | bytes 163872 | tf_op jit(solution)/shard_map/ppermute | solution.py:27
  105.2 4.0 %collective-permute-start.10 = (bf16[8,16,640]{2,1,0:T(8,128)(2,1)S(1)}, bf16[8,16,640]{2,1,0:T(8,128)(2,1)S(1)}, u32[]{:S(2)}, u32[]{:S(2)}) collective-permute-start(bf16[8,16,640]{2,1,0:T(8,128)(2,1)S(1)} %get-tuple-element.25), channel_id=1, source_target_pairs={{256,8},{257,9},{258,10},{259,11},{260,12},{261,13},{262,14},{263,... | collective-permute-start | bytes 491528 | tf_op jit(solution)/shard_map/ppermute | solution.py:86
  109.2 3.4 %collective-permute-start.9 = (bf16[8,16,640]{2,1,0:T(8,128)(2,1)S(1)}, bf16[8,16,640]{2,1,0:T(8,128)(2,1)S(1)}, u32[]{:S(2)}, u32[]{:S(2)}) collective-permute-start(bf16[8,16,640]{2,1,0:T(8,128)(2,1)S(1)} %get-tuple-element.26), channel_id=1, source_target_pairs={{256,0},{257,1},{258,2},{259,3},{260,4},{261,5},{262,6},{263,7},{2... | collective-permute-start | bytes 491528 | tf_op jit(solution)/shard_map/ppermute | solution.py:86
  112.5 7.8 %all-to-all-done.2 = bf16[8,96,640]{2,1,0:T(8,128)(2,1)S(1)} async-done(((bf16[8,96,640]{2,1,0:T(8,128)(2,1)}), bf16[8,96,640]{2,1,0:T(8,128)(2,1)S(1)}, u32[]{:S(2)}, u32[]{:S(2)}) %all-to-all-start.2) | async-done | bytes 983072 | tf_op jit(solution)/shard_map/all_to_all | solution.py:17
  120.4 0.1 convert_reduce_fusion.1
  120.5 4.0 %collective-permute-start.11 = (bf16[2,48,640]{2,1,0:T(8,128)(2,1)S(1)}, bf16[2,48,640]{2,1,0:T(8,128)(2,1)S(1)}, u32[]{:S(2)}, u32[]{:S(2)}) collective-permute-start(bf16[2,48,640]{2,1,0:T(8,128)(2,1)S(1)} %pad_maximum_fusion.4), channel_id=1, source_target_pairs={{0,128},{16,144},{32,160},{48,176},{64,192},{80,208},{96,224},{112... | collective-permute-start | bytes 368648 | tf_op jit(solution)/shard_map/ppermute | solution.py:63
  124.6 0.6 copy-done.3
  125.3 3.9 %combine.1 = bf16[128,5120]{1,0:T(8,128)(2,1)} custom-call(s32[1]{0:T(128)} %bitcast.spot, bf16[128,5120]{1,0:T(8,128)(2,1)} %collective-permute-done.7.grads, bf16[128,32]{1,0:T(8,128)(2,1)} %copy-done.5, bf16[8,16,640]{2,1,0:T(8,128)(2,1)} %copy-done.4, bf16[8,16,640]{2,1,0:T(8,128)(2,1)} %copy-done.3), custom_call_target="tpu_custom_call" | custom-call | flops 41943040 | bytes 2949120 | tf_op jit(solution)/shard_map/combine/pallas_call | solution.py:104
  129.3 3.1 %collective-permute-done.11 = bf16[2,48,640]{2,1,0:T(8,128)(2,1)S(1)} collective-permute-done((bf16[2,48,640]{2,1,0:T(8,128)(2,1)S(1)}, bf16[2,48,640]{2,1,0:T(8,128)(2,1)S(1)}, u32[]{:S(2)}, u32[]{:S(2)}) %collective-permute-start.11) | collective-permute-done | bytes 122912 | tf_op jit(solution)/shard_map/ppermute | solution.py:63
  132.3 0.7 add_convert_fusion
  (40 shorter events, 0.7 us)
Async XLA Ops:
  0.6 24.3 %copy-start = (bf16[1,768,640]{2,1,0:T(8,128)(2,1)S(1)}, bf16[1,768,640]{2,1,0:T(8,128)(2,1)}, u32[]{:S(2)}) copy-start(bf16[1,768,640]{2,1,0:T(8,128)(2,1)} %param.13) | copy-start | bytes 2949124
  4.9 20.1 %all-to-all-start = ((bf16[16,16,640]{2,1,0:T(8,128)(2,1)}), bf16[16,16,640]{2,1,0:T(8,128)(2,1)S(1)}, u32[]{:S(2)}, u32[]{:S(2)}) async-start(bf16[16,16,640]{2,1,0:T(8,128)(2,1)} %bitcast.8), calls=%async_computation | async-start | bytes 655360 | tf_op jit(solution)/shard_map/all_to_all | solution.py:17
  13.1 4.9 %collective-permute-start = (bf16[128,32]{1,0:T(8,128)(2,1)S(1)}, bf16[128,32]{1,0:T(8,128)(2,1)S(1)}, u32[]{:S(2)}, u32[]{:S(2)}) collective-permute-start(bf16[128,32]{1,0:T(8,128)(2,1)S(1)} %fusion.37), channel_id=1, source_target_pairs={{256,0},{512,256},{768,512},{257,1},{513,257},{769,513},{258,2},{5... | collective-permute-start | bytes 24584 | tf_op jit(solution)/shard_map/ppermute | solution.py:22
  18.0 7.5 %copy-start.5 = (bf16[128,32]{1,0:T(8,128)(2,1)}, bf16[128,32]{1,0:T(8,128)(2,1)S(1)}, u32[]{:S(2)}) copy-start(bf16[128,32]{1,0:T(8,128)(2,1)S(1)} %collective-permute-done.place) | copy-start | bytes 24580
  25.5 9.6 %copy-start.1 = (bf16[1,1,1,256,768]{4,3,2,1,0:T(8,128)(2,1)S(1)}, bf16[1,1,1,256,768]{4,3,2,1,0:T(8,128)(2,1)}, u32[]{:S(2)}) copy-start(bf16[1,1,1,256,768]{4,3,2,1,0:T(8,128)(2,1)} %param.11) | copy-start | bytes 1179652
  25.5 7.6 %collective-permute-start.1 = (bf16[128,768]{1,0:T(8,128)(2,1)S(1)}, bf16[128,768]{1,0:T(8,128)(2,1)S(1)}, u32[]{:S(2)}, u32[]{:S(2)}) collective-permute-start(bf16[128,768]{1,0:T(8,128)(2,1)S(1)} %select_convert_fusion), channel_id=1, source_target_pairs={{0,1},{1,0},{2,3},{3,2},{4,5},{5,4},{6,7},{7,6},{8,9},{9,8},{10,11... | collective-permute-start | bytes 589832 | tf_op jit(solution)/shard_map/ppermute | solution.py:27
  28.7 50.9 %collective-permute-start.7 = (bf16[128,5120]{1,0:T(8,128)(2,1)}, bf16[128,5120]{1,0:T(8,128)(2,1)}, u32[]{:S(2)}, u32[]{:S(2)}) collective-permute-start(bf16[128,5120]{1,0:T(8,128)(2,1)} %bitcast.6), channel_id=1, source_target_pairs={{256,0},{512,256},{768,512},{257,1},{513,257},{769,513},{258,2},{5... | collective-permute-start | bytes 3932168 | tf_op jit(solution)/shard_map/ppermute | solution.py:22
  33.2 8.4 %collective-permute-start.2 = (bf16[128,768]{1,0:T(8,128)(2,1)S(1)}, bf16[128,768]{1,0:T(8,128)(2,1)S(1)}, u32[]{:S(2)}, u32[]{:S(2)}) collective-permute-start(bf16[128,768]{1,0:T(8,128)(2,1)S(1)} %fusion.39), channel_id=1, source_target_pairs={{0,2},{1,3},{2,0},{3,1},{4,6},{5,7},{6,4},{7,5},{8,10},{9,11},{10,... | collective-permute-start | bytes 589832 | tf_op jit(solution)/shard_map/ppermute | solution.py:27
  41.7 20.9 %collective-permute-start.3 = (bf16[128,768]{1,0:T(8,128)(2,1)S(1)}, bf16[128,768]{1,0:T(8,128)(2,1)S(1)}, u32[]{:S(2)}, u32[]{:S(2)}) collective-permute-start(bf16[128,768]{1,0:T(8,128)(2,1)S(1)} %convert_element_type.106), channel_id=1, source_target_pairs={{0,4},{1,5},{2,6},{3,7},{4,0},{5,1},{6,2},{7,3},{8,12},{9,13},{10,... | collective-permute-start | bytes 589832 | tf_op jit(solution)/shard_map/ppermute | solution.py:27
  45.9 43.3 %all-to-all-start.1 = ((bf16[8,96,640]{2,1,0:T(8,128)(2,1)}), bf16[8,96,640]{2,1,0:T(8,128)(2,1)S(1)}, u32[]{:S(2)}, u32[]{:S(2)}) async-start(bf16[8,96,640]{2,1,0:T(8,128)(2,1)} %bitcast.21), calls=%async_computation.1 | async-start | bytes 1966080 | tf_op jit(solution)/shard_map/all_to_all | solution.py:17
  62.7 3.3 %collective-permute-start.4 = (bf16[128,768]{1,0:T(8,128)(2,1)S(1)}, bf16[128,768]{1,0:T(8,128)(2,1)S(1)}, u32[]{:S(2)}, u32[]{:S(2)}) collective-permute-start(bf16[128,768]{1,0:T(8,128)(2,1)S(1)} %fusion.13), channel_id=1, source_target_pairs={{0,1},{1,0},{2,3},{3,2},{4,5},{5,4},{6,7},{7,6},{8,9},{9,8},{10,11... | collective-permute-start | bytes 589832 | tf_op jit(solution)/shard_map/ppermute | solution.py:27
  66.1 8.4 %copy-start.2 = (bf16[1,1,256,640]{3,2,1,0:T(8,128)(2,1)S(1)}, bf16[1,1,256,640]{3,2,1,0:T(8,128)(2,1)}, u32[]{:S(2)}) copy-start(bf16[1,1,256,640]{3,2,1,0:T(8,128)(2,1)} %param.10) | copy-start | bytes 983044
  68.0 3.3 %collective-permute-start.5 = (bf16[1,8,16,640]{3,2,0,1:T(8,128)(2,1)S(1)}, bf16[1,8,16,640]{3,2,0,1:T(8,128)(2,1)S(1)}, u32[]{:S(2)}, u32[]{:S(2)}) collective-permute-start(bf16[1,8,16,640]{3,2,0,1:T(8,128)(2,1)S(1)} %get-tuple-element.32), channel_id=1, source_target_pairs={{0,1},{1,0},{2,3},{3,2},{4,5},{5,4},{6,7},{7,6},{8,9},{9,8},{10,11... | collective-permute-start | bytes 491528 | tf_op jit(solution)/shard_map/ppermute | solution.py:27
  71.4 8.1 %collective-permute-start.6 = (bf16[2,4,16,640]{3,2,0,1:T(8,128)(2,1)S(1)}, bf16[2,4,16,640]{3,2,0,1:T(8,128)(2,1)S(1)}, u32[]{:S(2)}, u32[]{:S(2)}) collective-permute-start(bf16[2,4,16,640]{3,2,0,1:T(8,128)(2,1)S(1)} %get-tuple-element.30), channel_id=1, source_target_pairs={{0,2},{1,3},{2,0},{3,1},{4,6},{5,7},{6,4},{7,5},{8,10},{9,11},{10,... | collective-permute-start | bytes 491528 | tf_op jit(solution)/shard_map/ppermute | solution.py:27
  89.1 31.3 %all-to-all-start.2 = ((bf16[8,96,640]{2,1,0:T(8,128)(2,1)}), bf16[8,96,640]{2,1,0:T(8,128)(2,1)S(1)}, u32[]{:S(2)}, u32[]{:S(2)}) async-start(bf16[8,96,640]{2,1,0:T(8,128)(2,1)} %bitcast.30), calls=%async_computation.2 | async-start | bytes 1966080 | tf_op jit(solution)/shard_map/all_to_all | solution.py:17
  92.7 12.4 %collective-permute-start.8 = (bf16[4,2,16,640]{3,2,0,1:T(8,128)(2,1)S(1)}, bf16[4,2,16,640]{3,2,0,1:T(8,128)(2,1)S(1)}, u32[]{:S(2)}, u32[]{:S(2)}) collective-permute-start(bf16[4,2,16,640]{3,2,0,1:T(8,128)(2,1)S(1)} %get-tuple-element.27), channel_id=1, source_target_pairs={{0,4},{1,5},{2,6},{3,7},{4,0},{5,1},{6,2},{7,3},{8,12},{9,13},{10,... | collective-permute-start | bytes 491528 | tf_op jit(solution)/shard_map/ppermute | solution.py:27
  105.2 19.4 %collective-permute-start.10 = (bf16[8,16,640]{2,1,0:T(8,128)(2,1)S(1)}, bf16[8,16,640]{2,1,0:T(8,128)(2,1)S(1)}, u32[]{:S(2)}, u32[]{:S(2)}) collective-permute-start(bf16[8,16,640]{2,1,0:T(8,128)(2,1)S(1)} %get-tuple-element.25), channel_id=1, source_target_pairs={{256,8},{257,9},{258,10},{259,11},{260,12},{261,13},{262,14},{263,... | collective-permute-start | bytes 491528 | tf_op jit(solution)/shard_map/ppermute | solution.py:86
  109.2 15.5 %collective-permute-start.9 = (bf16[8,16,640]{2,1,0:T(8,128)(2,1)S(1)}, bf16[8,16,640]{2,1,0:T(8,128)(2,1)S(1)}, u32[]{:S(2)}, u32[]{:S(2)}) collective-permute-start(bf16[8,16,640]{2,1,0:T(8,128)(2,1)S(1)} %get-tuple-element.26), channel_id=1, source_target_pairs={{256,0},{257,1},{258,2},{259,3},{260,4},{261,5},{262,6},{263,7},{2... | collective-permute-start | bytes 491528 | tf_op jit(solution)/shard_map/ppermute | solution.py:86
  120.5 11.8 %collective-permute-start.11 = (bf16[2,48,640]{2,1,0:T(8,128)(2,1)S(1)}, bf16[2,48,640]{2,1,0:T(8,128)(2,1)S(1)}, u32[]{:S(2)}, u32[]{:S(2)}) collective-permute-start(bf16[2,48,640]{2,1,0:T(8,128)(2,1)S(1)} %pad_maximum_fusion.4), channel_id=1, source_target_pairs={{0,128},{16,144},{32,160},{48,176},{64,192},{80,208},{96,224},{112... | collective-permute-start | bytes 368648 | tf_op jit(solution)/shard_map/ppermute | solution.py:63
  124.6 0.7 copy-start.3
  124.6 0.7 copy-start.4
